TPU v7x, 512 devices: a whole 4x4x16 slice. The times are simulated.
512 devices in a mesh: dp: 32 (over z_lo, y), row: 2 (over z_hi), col: 8 (over x, core).
Axes of the slice: x: 4, y: 4, z: 16 (z_hi: 2, z_lo: 8; z = z_hi * 8 + z_lo), core: 2. Of those that a mesh axis runs over, the one named last changes fastest.
Arguments:
- cotangent: bfloat16 [32, 3072, 4096], P('dp', None, ('row', 'col')), may hold values from -1.5 to 1.5
- routed: int32 [32, 768], P('dp'), may hold values from 0 to 3071, as said below
- counts: int32 [32], replicated, may hold values from 0 to 768, as said below
- logits: float32 [32, 768], P('dp'), may hold values from -6 to 6
- query_rows: bfloat16 [32, 768, 4096], P('dp', None, ('row', 'col')), may hold values from -7 to 7
- key_rows: bfloat16 [32, 768, 512], P('dp', None, 'row'), may hold values from -7 to 7
- routed_value_rows: bfloat16 [32, 768, 512], P('dp', None, 'row'), may hold values from -6 to 6
- w_out: bfloat16 [4096, 4096], P(None, ('row', 'col')), may hold values from -0.09375 to 0.09375
Outputs:
- grad_queries: bfloat16 [32, 768, 4096], P('dp', None, ('row', 'col'))
- grad_keys: bfloat16 [32, 768, 512], P('dp', None, 'row')
- grad_values: bfloat16 [32, 768, 512], P('dp', None, 'row')
- grad_w_out: bfloat16 [4096, 4096], P('dp', ('row', 'col'))
- grad_logits: float32 [32, 768], P('dp')
Inputs may be any that keep to these rules, and one draw needn't show every extreme that they name: counts[s] of sequence s's 768 slots are routed; the counts of all sequences sum to 12288, and one of them is 768. Each row holds distinct positions; its first counts[s] entries are increasing and are the routed tokens, the later ones are not used.
All inputs are finite; a program needn't handle non-finite values.
Results may differ from a plain program's by a relative error of at most 0.015.
Values may be sent and summed in bfloat16 or wider, within the bound.
No kernel may reach another device: no remote copies, remote signals or barrier semaphores. Data moves between devices by JAX's collectives and lax.ppermute only.
A program may use at most 64 MiB of HBM per device.

v0:
```python
import jax
import jax.numpy as jnp
from jax import lax
from jax.sharding import PartitionSpec as P

QUERY_HEAD_COUNT = 32
KEY_VALUE_HEADS = 4
HEAD_SIZE = 128


def project(grad_rows, scaled_rows, w_out):
    grad_full = lax.all_gather(grad_rows, ("row", "col"), axis=1, tiled=True)
    grad_o = jnp.dot(grad_full, w_out, preferred_element_type=jnp.float32)
    w_grad = lax.psum_scatter(
        lax.dot_general(
            grad_full, scaled_rows, (((0,), (0,)), ((), ())), preferred_element_type=jnp.float32
        ),
        "dp",
        scatter_dimension=0,
        tiled=True,
    )
    return (grad_o, w_grad)


def per_device(cotangent, routed, counts, logits, query_rows, key_rows, routed_value_rows, w_out):
    slot_total = routed.shape[1]
    dp_index = lax.axis_index("dp")
    own_count = lax.dynamic_index_in_dim(counts, dp_index, 0, keepdims=False)
    slot_ids = jnp.arange(slot_total, dtype=jnp.int32)
    live_rows = slot_ids < own_count
    positions = routed[0]
    picked = jnp.take(cotangent[0], positions, axis=0) * live_rows[:, None].astype(cotangent.dtype)
    router_weight = jax.nn.sigmoid(logits[0])
    local_heads = query_rows.shape[2] // HEAD_SIZE
    row_groups = key_rows.shape[2] // HEAD_SIZE
    group_width = QUERY_HEAD_COUNT // KEY_VALUE_HEADS
    head_group = (
        lax.axis_index("col") * local_heads + jnp.arange(local_heads, dtype=jnp.int32)
    ) // group_width
    query_heads = query_rows[0].reshape(slot_total, local_heads, HEAD_SIZE)
    key_head_rows = jnp.take(
        key_rows[0].reshape(slot_total, row_groups, HEAD_SIZE), head_group, axis=1
    )
    value_head_rows = jnp.take(
        routed_value_rows[0].reshape(slot_total, row_groups, HEAD_SIZE), head_group, axis=1
    )
    allowed = live_rows[None, :] & (positions[None, :] <= positions[:, None]) | (
        slot_ids[:, None] == slot_ids[None, :]
    )
    score_scale = HEAD_SIZE ** (-0.5)
    scores = (
        jnp.einsum("ihd,jhd->hij", query_heads, key_head_rows, preferred_element_type=jnp.float32)
        * score_scale
    )
    scores = jnp.where(allowed[None], scores, -jnp.inf)
    scores = scores - jnp.max(scores, axis=2, keepdims=True)
    exponent = jnp.exp(scores)
    attn_probs = exponent / jnp.sum(exponent, axis=2, keepdims=True)
    probs_rounded = attn_probs.astype(jnp.bfloat16)
    attended = jnp.einsum(
        "hij,jhd->ihd", probs_rounded, value_head_rows, preferred_element_type=jnp.float32
    )
    attended = attended.astype(jnp.bfloat16).reshape(slot_total, -1)
    attended_wide = attended.astype(jnp.float32)
    scaled = (router_weight[:, None] * attended_wide).astype(jnp.bfloat16)
    grad_o, w_grad = project(picked, scaled, w_out)
    router_grad = lax.psum(jnp.sum(grad_o * attended_wide, axis=1), ("row", "col"))
    grad_logits = router_grad * router_weight * (1.0 - router_weight)
    grad_attn = (
        (router_weight[:, None] * grad_o)
        .astype(jnp.bfloat16)
        .reshape(slot_total, local_heads, HEAD_SIZE)
    )
    value_portion = jnp.einsum(
        "hij,ihd->jhd", probs_rounded, grad_attn, preferred_element_type=jnp.float32
    )
    grad_probs = jnp.einsum(
        "ihd,jhd->hij", grad_attn, value_head_rows, preferred_element_type=jnp.float32
    )
    row_delta = jnp.sum(attn_probs * grad_probs, axis=2, keepdims=True)
    grad_scores = (attn_probs * (grad_probs - row_delta)).astype(jnp.bfloat16)
    grad_q = (
        jnp.einsum("hij,jhd->ihd", grad_scores, key_head_rows, preferred_element_type=jnp.float32)
        * score_scale
    )
    grad_q = grad_q.astype(jnp.bfloat16).reshape(slot_total, -1)
    key_portion = (
        jnp.einsum("hij,ihd->jhd", grad_scores, query_heads, preferred_element_type=jnp.float32)
        * score_scale
    )
    group_onehot = (head_group[:, None] == jnp.arange(row_groups, dtype=jnp.int32)[None, :]).astype(
        jnp.float32
    )
    key_sum = jnp.einsum("jhd,hg->jgd", key_portion, group_onehot).reshape(slot_total, -1)
    value_sum = jnp.einsum("jhd,hg->jgd", value_portion, group_onehot).reshape(slot_total, -1)
    key_total, value_total = lax.psum((key_sum, value_sum), "col")
    return (
        grad_q[None],
        key_total.astype(jnp.bfloat16)[None],
        value_total.astype(jnp.bfloat16)[None],
        w_grad.astype(jnp.bfloat16),
        grad_logits[None],
    )


def solution(mesh):
    placed = (
        P("dp", None, ("row", "col")),
        P("dp", None),
        P(),
        P("dp", None),
        P("dp", None, ("row", "col")),
        P("dp", None, "row"),
        P("dp", None, "row"),
        P(None, ("row", "col")),
    )
    return jax.shard_map(
        per_device,
        mesh=mesh,
        in_specs=placed,
        out_specs=(
            P("dp", None, ("row", "col")),
            P("dp", None, "row"),
            P("dp", None, "row"),
            P("dp", ("row", "col")),
            P("dp", None),
        ),
        check_vma=False,
    )
```

profile of v0, /device:TPU:6, one launch (start us, length us, event | category | flops | bytes accessed | tf_op | source)
XLA Modules:
  0.0 431.1 jit_solution(7841587764658297804)
XLA Ops:
  7.3 0.8 fusion.33
  8.1 0.7 reduce
  8.8 1.2 dynamic_slice.4
  10.7 3.7 gather_fusion
  14.5 1.0 select_multiply_fusion
  15.6 0.8 reshape_squeeze.10
  16.8 1.2 copy.30
  18.9 1.3 gather_fusion.2
  21.5 5.1 %fusion.44 = (f32[2,768]{1,0:T(2,128)S(1)}, f32[2,768,768]{1,2,0:T(8,128)}) fusion(pred[768,768]{0,1:T(8,128)(4,1)S(1)} %fusion.4, bf16[768,2,128]{2,1,0:T(2,128)(2,1)} %reshape_squeeze.10, bf16[2,768,128]{2,1,0:T(8,128)(2,1)S(1)} %gather_fusion.1, pred[2]{0:T(512)(128)(4,1)S(1)} %compare_and_fusion.1), kind=kOutput, calls=%fused_computation.75 | convolution fusion | flops 306905856 | bytes 6100994 | tf_op jit(solution)/shard_map/sub | solution.py:56
  26.6 2.9 fusion.8
  29.5 140.1 %all-gather.2.cloned.1.call-done = bf16[768,4096]{1,0:T(8,128)(2,1)} async-done(((bf16[768,256]{1,0:T(8,128)(2,1)}), bf16[768,4096]{1,0:T(8,128)(2,1)}) %all-gather.2.cloned.1.call-update) | async-done | bytes 6291472 | tf_op jit(solution)/shard_map/all_gather | solution.py:12
  169.6 5.6 %fusion.12 = (f32[768]{0:T(1024)S(1)}, bf16[768,256]{0,1:T(8,128)(2,1)S(1)}, bf16[768,256]{0,1:T(8,128)(2,1)}) fusion(f32[2,128,768]{2,1,0:T(8,128)S(1)} %fusion.8, f32[768]{0:T(1024)S(1)} %divide_reduce_fusion, bf16[768,4096]{1,0:T(8,128)(2,1)} %all-gather.2.cloned.1.call-done, bf16[4096,256]{1,0:T(8,128)(2,1)S(1)} %copy-done), kind=kOutput, calls=%fused_computation.29 | convolution fusion | flops 1611791616 | bytes 9967616 | tf_op jit(solution)/shard_map/dot_general | solution.py:13
  175.2 3.9 fusion.53
  179.0 51.4 %psum.23 = f32[768]{0:T(1024)S(1)} all-reduce(f32[768]{0:T(1024)S(1)} %get-tuple-element.23), channel_id=1, replica_groups=mesh['dp'=32,'row'=2,'col'=8] {'row','col'}, use_global_device_ids=true, to_apply=%region_7.9 | all-reduce | flops 768 | bytes 6144 | tf_op jit(solution)/shard_map/psum | solution.py:67
  231.0 3.4 convolution_bitcast_fusion
  235.5 3.5 multiply_reduce_fusion
  239.3 0.8 multiply_convert_fusion
  240.0 1.4 copy-done.2
  242.1 0.9 copy.41
  243.0 2.5 fusion.6
  246.0 0.9 copy.67
  246.9 63.1 %all-reduce.2 = (bf16[768,256]{1,0:T(8,128)(2,1)}, bf16[768,256]{1,0:T(8,128)(2,1)}) all-reduce(f32[768,256]{1,0:T(8,128)} %bitcast.90, f32[768,256]{1,0:T(8,128)S(1)} %bitcast.89), channel_id=1, replica_groups=mesh['dp'=32,'row'=2,'col'=8] {'col'}, use_global_device_ids=true, to_apply=%region_3.5 | all-reduce | flops 393216 | bytes 2359296 | tf_op jit(solution)/shard_map/psum | solution.py:96
  310.1 112.6 %reduce-scatter.2.cloned.1.call-done = f32[128,256]{1,0:T(8,128)} async-done(((f32[4096,256]{1,0:T(8,128)}), f32[128,256]{1,0:T(8,128)}) %reduce-scatter.2.cloned.1.call-update) | async-done | bytes 131088 | tf_op jit(solution)/shard_map/reduce_scatter | solution.py:14
  422.7 1.5 convert_element_type.62
  (45 shorter events, 6.3 us)
Async XLA Ops:
  7.2 162.4 %copy-start = (bf16[4096,256]{1,0:T(8,128)(2,1)S(1)}, bf16[4096,256]{1,0:T(8,128)(2,1)}, u32[]{:S(2)}) copy-start(bf16[4096,256]{1,0:T(8,128)(2,1)} %param.17) | copy-start | bytes 6291460
  7.2 8.4 %copy-start.5 = (bf16[1,768,256]{2,1,0:T(8,128)(2,1)S(1)}, bf16[1,768,256]{2,1,0:T(8,128)(2,1)}, u32[]{:S(2)}) copy-start(bf16[1,768,256]{2,1,0:T(8,128)(2,1)} %param.14) | copy-start | bytes 1179652
  7.2 9.2 %copy-start.6 = (bf16[1,768,256]{2,1,0:T(8,128)(2,1)S(1)}, bf16[1,768,256]{2,1,0:T(8,128)(2,1)}, u32[]{:S(2)}) copy-start(bf16[1,768,256]{2,1,0:T(8,128)(2,1)} %param.15) | copy-start | bytes 1179652
  7.2 162.4 %all-gather.2.cloned.1.call-start = ((), (), s32[]{:S(2)}) async-start(), calls=%async_computation.1 | async-start | bytes 6684672 | tf_op jit(solution)/shard_map/all_gather | solution.py:12
  10.7 10.2 %copy-start.8 = (f32[1,768]{1,0:T(1,128)S(1)}, f32[1,768]{1,0:T(1,128)}, u32[]{:S(2)}) copy-start(f32[1,768]{1,0:T(1,128)} %param.13) | copy-start | bytes 9220
  15.5 407.2 %reduce-scatter.2.cloned.1.call-start = ((), (), s32[]{:S(2)}) async-start(), calls=%async_computation.2 | async-start | bytes 4325376 | tf_op jit(solution)/shard_map/reduce_scatter | solution.py:14
  18.9 7.7 %copy-start.3 = (bf16[2,768,128]{2,1,0:T(8,128)(2,1)}, bf16[2,768,128]{2,1,0:T(8,128)(2,1)S(1)}, u32[]{:S(2)}) copy-start(bf16[2,768,128]{2,1,0:T(8,128)(2,1)S(1)} %gather_fusion.1) | copy-start | bytes 1179652
  21.4 5.1 %copy-start.7 = (bf16[2,768,128]{2,1,0:T(8,128)(2,1)S(1)}, bf16[2,768,128]{2,1,0:T(8,128)(2,1)}, u32[]{:S(2)}) copy-start(bf16[2,768,128]{2,1,0:T(8,128)(2,1)} %gather_fusion.2) | copy-start | bytes 1179652
  169.6 5.6 %copy-start.1 = (bf16[768,4096]{1,0:T(8,128)(2,1)S(1)}, bf16[768,4096]{1,0:T(8,128)(2,1)}, u32[]{:S(2)}) copy-start(bf16[768,4096]{1,0:T(8,128)(2,1)} %all-gather.2.cloned.1.call-done) | copy-start | bytes 18874372
  235.4 3.7 slice-start
  235.5 3.8 slice-start.1
  239.3 2.2 copy-start.4
  240.0 1.4 copy-start.2
Sparse Core Ops, SparseCore 0:
  15.6 153.9 all-gather.1
  179.2 243.4 reduce-scatter.1
where the time goes:
time: 431 us
  waiting for transfers between devices  253 us (59%)
  blocking collectives  114 us (26%)
  matrix products  28.5 us (7%)
  between operations  14.3 us (3%)
  local copies, waits for them, and re-layouts  14.2 us (3%)
  other arithmetic  6.75 us (2%)
    all_gather x1, waiting for transfers between devices, project(): grad_full = lax.all_gather(grad_rows, ('row', 'col'), axis=1, tiled=True)  140 us
    reduce_scatter x1, waiting for transfers between devices, project(): lax.psum_scatter(lax.dot_general(grad_full, scaled_rows, (((0,), (0,)), (...  113 us
    psum x1, blocking collectives, per_device(): key_total, value_total = lax.psum((key_sum, value_sum), 'col')  63.1 us
    psum x1, blocking collectives, per_device(): lax.psum(jnp.sum(grad_o * attended_wide, axis=1), ('row', 'col'))  51.4 us
  transfers between devices with their start and end apart: 2, of which 2 were waited for; matrix products, arithmetic and copies ran while one was open for 7% of the time, Pallas kernels for 0%

commit v1 on v0

v1 whole, which is shorter than its diff:
```python
import jax
import jax.numpy as jnp
from jax import lax
from jax.sharding import Mesh
from jax.sharding import PartitionSpec as P

QUERY_HEAD_COUNT = 32
KEY_VALUE_HEADS = 4
HEAD_SIZE = 128
ZL, Y, ZH, X, CORE = 8, 4, 2, 4, 2


def ring(n, k):
    return [(i, (i + k) % n) for i in range(n)]


def swap(value, axis):
    return lax.ppermute(value, axis, ring(2, 1))


def gather_x(block):
    copies = jnp.broadcast_to(block[None], (X,) + block.shape)
    return lax.all_to_all(copies, "x", 0, 0, tiled=True)


def attention_parts(positions, live_rows, query_heads, key_head, value_head):
    slot_ids = jnp.arange(positions.shape[0], dtype=jnp.int32)
    allowed = live_rows[None, :] & (positions[None, :] <= positions[:, None]) | (
        slot_ids[:, None] == slot_ids[None, :]
    )
    scores = jnp.einsum("ihd,jd->hij", query_heads, key_head, preferred_element_type=jnp.float32)
    scores = jnp.where(allowed[None], scores * HEAD_SIZE ** (-0.5), -jnp.inf)
    exponent = jnp.exp(scores - jnp.max(scores, axis=2, keepdims=True))
    return exponent / jnp.sum(exponent, axis=2, keepdims=True)


def half_products(near, far, w_half, scaled, core):
    both = jnp.where(core == 0, jnp.stack([near, far], 1), jnp.stack([far, near], 1))
    grad_o = jnp.einsum("xqif,xqfc->ic", both, w_half, preferred_element_type=jnp.float32)
    w_grad = jnp.einsum("xqif,ic->qfxc", both, scaled, preferred_element_type=jnp.float32)
    w_grad = w_grad.astype(jnp.bfloat16).reshape(CORE, 2, 128, X, 256).transpose(0, 1, 3, 2, 4)
    return grad_o, w_grad.reshape(Y, X, 128, 256)


def sum_over_y(blocks):
    moved = lax.all_to_all(blocks, "y", 0, 0, tiled=True)
    return jnp.sum(moved.astype(jnp.float32), axis=0).astype(jnp.bfloat16)


def per_device(cotangent, routed, counts, logits, query_rows, key_rows, routed_value_rows, w_out):
    slot_total = routed.shape[1]
    zh, x, core = lax.axis_index("zh"), lax.axis_index("x"), lax.axis_index("core")
    dp_index = lax.axis_index("zl") * Y + lax.axis_index("y")
    own_count = lax.dynamic_index_in_dim(counts, dp_index, 0, keepdims=False)
    live_rows = jnp.arange(slot_total, dtype=jnp.int32) < own_count
    positions = routed[0]
    picked = jnp.take(cotangent[0], positions, axis=0) * live_rows[:, None].astype(cotangent.dtype)
    other_picked = swap(picked, "zh")
    own_near = gather_x(picked)
    own_far = swap(own_near, "core")

    router_weight = jax.nn.sigmoid(logits[0])
    heads = query_rows.shape[2] // HEAD_SIZE
    group = x // 2
    query_heads = query_rows[0].reshape(slot_total, heads, HEAD_SIZE)
    key_head = lax.dynamic_slice_in_dim(key_rows[0], group * HEAD_SIZE, HEAD_SIZE, 1)
    value_head = lax.dynamic_slice_in_dim(routed_value_rows[0], group * HEAD_SIZE, HEAD_SIZE, 1)
    attn_probs = attention_parts(positions, live_rows, query_heads, key_head, value_head)
    probs_rounded = attn_probs.astype(jnp.bfloat16)
    attended = jnp.einsum(
        "hij,jd->ihd", probs_rounded, value_head, preferred_element_type=jnp.float32
    )
    attended_wide = attended.astype(jnp.bfloat16).reshape(slot_total, -1).astype(jnp.float32)
    scaled = (router_weight[:, None] * attended_wide).astype(jnp.bfloat16)

    w_parts = w_out.reshape(ZH, X, CORE, 256, 256)
    w_own = lax.dynamic_index_in_dim(w_parts, zh, 0, keepdims=False)
    w_other = lax.dynamic_index_in_dim(w_parts, 1 - zh, 0, keepdims=False)
    grad_o_own, w_grad_own = half_products(own_near, own_far, w_own, scaled, core)
    y_own = sum_over_y(w_grad_own)

    other_near = gather_x(other_picked)
    other_far = swap(other_near, "core")
    grad_o_other, w_grad_other = half_products(other_near, other_far, w_other, scaled, core)
    grad_o = grad_o_own + grad_o_other
    y_other = sum_over_y(w_grad_other)

    router = jnp.sum(grad_o * attended_wide, axis=1)
    grad_attn = (
        (router_weight[:, None] * grad_o)
        .astype(jnp.bfloat16)
        .reshape(slot_total, heads, HEAD_SIZE)
    )
    value_part = jnp.einsum(
        "hij,ihd->jd", probs_rounded, grad_attn, preferred_element_type=jnp.float32
    )
    grad_probs = jnp.einsum(
        "ihd,jd->hij", grad_attn, value_head, preferred_element_type=jnp.float32
    )
    row_delta = jnp.sum(attn_probs * grad_probs, axis=2, keepdims=True)
    grad_scores = (attn_probs * (grad_probs - row_delta)).astype(jnp.bfloat16)
    score_scale = HEAD_SIZE ** (-0.5)
    grad_q = (
        jnp.einsum("hij,jd->ihd", grad_scores, key_head, preferred_element_type=jnp.float32)
        * score_scale
    )
    grad_q = grad_q.astype(jnp.bfloat16).reshape(slot_total, -1)
    key_part = (
        jnp.einsum("hij,ihd->jd", grad_scores, query_heads, preferred_element_type=jnp.float32)
        * score_scale
    )

    half = slot_total // 2
    kv = jnp.concatenate([key_part, value_part], axis=1)
    kept = lax.dynamic_slice_in_dim(kv, core * half, half, 0)
    sent = lax.dynamic_slice_in_dim(kv, (1 - core) * half, half, 0).astype(jnp.bfloat16)
    chip = (kept + swap(sent, "core").astype(jnp.float32)).astype(jnp.bfloat16)
    router = router + swap(router, "core")
    pieces = [(x, chip)] + [
        ((x - k) % X, lax.ppermute(chip, "x", ring(X, k))) for k in (1, 3, 2)
    ]
    router = router + lax.ppermute(router, "x", ring(X, 1))
    router = router + lax.ppermute(router, "x", ring(X, 2))
    router = router + swap(router, "zh")
    totals = []
    for g in range(2):
        totals.append(
            sum(jnp.where(src // 2 == g, piece.astype(jnp.float32), 0.0) for src, piece in pieces)
        )
    joined = jnp.stack(totals, axis=1).reshape(half, 2, 2, HEAD_SIZE)
    joined = joined.transpose(0, 2, 1, 3).reshape(half, 4 * HEAD_SIZE).astype(jnp.bfloat16)
    theirs = swap(joined, "core")
    rows = jnp.where(
        core == 0, jnp.concatenate([joined, theirs], 0), jnp.concatenate([theirs, joined], 0)
    )
    key_total, value_total = rows[:, : 2 * HEAD_SIZE], rows[:, 2 * HEAD_SIZE :]

    blocks = jnp.where(
        zh == 0, jnp.concatenate([y_own, y_other], 0), jnp.concatenate([y_other, y_own], 0)
    )
    moved = lax.all_to_all(blocks, "zl", 0, 0, tiled=True)
    w_grad = jnp.sum(moved.astype(jnp.float32), axis=0).astype(jnp.bfloat16)

    grad_logits = router * router_weight * (1.0 - router_weight)
    return (grad_q[None], key_total[None], value_total[None], w_grad, grad_logits[None])


def solution(mesh):
    fine = Mesh(mesh.devices.reshape(ZL, Y, ZH, X, CORE), ("zl", "y", "zh", "x", "core"))
    dp, col = ("zl", "y"), ("x", "core")
    row_col = ("zh",) + col
    placed = (
        P(dp, None, row_col),
        P(dp, None),
        P(),
        P(dp, None),
        P(dp, None, row_col),
        P(dp, None, "zh"),
        P(dp, None, "zh"),
        P(None, row_col),
    )
    return jax.shard_map(
        per_device,
        mesh=fine,
        in_specs=placed,
        out_specs=(
            P(dp, None, row_col),
            P(dp, None, "zh"),
            P(dp, None, "zh"),
            P(dp, row_col),
            P(dp, None),
        ),
        check_vma=False,
    )
```

time: 431 us -> 236 us (0.55)
  waiting for transfers between devices: 253 us -> 63.6 us
  blocking collectives: 114 us -> 0 us
  starting transfers between devices: 0.08 us -> 98.2 us
  between operations: 14.3 us -> 1.22 us
  local copies, waits for them, and re-layouts: 14.2 us -> 24.8 us
  other arithmetic: 6.75 us -> 14.9 us
    all_gather x1 -> x0, waiting for transfers between devices: 140 us -> none  [project(): grad_full = lax.all_gather(grad_rows, ('row', 'col'), axis=1, tiled=True)]
    psum x2 -> x0, blocking collectives: 114 us -> none  [the longest x1 63.1 us: per_device(): key_total, value_total = lax.psum((key_sum, value_sum), 'col')]
    reduce_scatter x1 -> x0, waiting for transfers between devices: 113 us -> none  [project(): lax.psum_scatter(lax.dot_general(grad_full, scaled_rows, (((0,), (0,)), (...]
    all_to_all x0 -> x5, starting transfers between devices: none -> 49.5 us  [the longest x1 29.4 us: per_device(): moved = lax.all_to_all(blocks, 'zl', 0, 0, tiled=True)]
    ppermute x0 -> x12, starting transfers between devices: none -> 48.8 us  [the longest x7 33.7 us: swap(): return lax.ppermute(value, axis, ring(2, 1))]
    all_to_all x0 -> x5, waiting for transfers between devices: none -> 40.5 us  [the longest x2 23.7 us: gather_x(): return lax.all_to_all(copies, 'x', 0, 0, tiled=True)]
    ppermute x0 -> x12, waiting for transfers between devices: none -> 23.1 us  [the longest x7 14.8 us: swap(): return lax.ppermute(value, axis, ring(2, 1))]
    select_n x1 -> x3, other arithmetic: 0.01 us -> 4.66 us  [the longest x1 2.44 us: half_products(): jnp.where(core == 0, jnp.stack([near, far], 1), jnp.stack([far, near], 1))]
  transfers between devices with their start and end apart: 2 -> 17, of which waited for: 2 -> 8; matrix products, arithmetic and copies ran while one was open for 7% -> 19% of each run, Pallas kernels for 0% -> 0%
where the time goes in v1:
time: 236 us; the launch traced here: 232 us
  starting transfers between devices  98.2 us (42%)
  waiting for transfers between devices  63.6 us (27%)
  matrix products  29.4 us (12%)
  local copies, waits for them, and re-layouts  24.8 us (11%)
  other arithmetic  14.9 us (6%)
    ppermute x7, starting transfers between devices, swap(): return lax.ppermute(value, axis, ring(2, 1))  33.7 us
    all_to_all x1, starting transfers between devices, per_device(): moved = lax.all_to_all(blocks, 'zl', 0, 0, tiled=True)  29.4 us
    all_to_all x2, waiting for transfers between devices, gather_x(): return lax.all_to_all(copies, 'x', 0, 0, tiled=True)  23.7 us
    all_to_all x2, waiting for transfers between devices, sum_over_y(): moved = lax.all_to_all(blocks, 'y', 0, 0, tiled=True)  16.8 us
    ppermute x7, waiting for transfers between devices, swap(): return lax.ppermute(value, axis, ring(2, 1))  14.8 us
    all_to_all x2, starting transfers between devices, gather_x(): return lax.all_to_all(copies, 'x', 0, 0, tiled=True)  11.2 us
    ppermute x3, starting transfers between devices, per_device(): lax.ppermute(chip, 'x', ring(X, k))  11.1 us
    all_to_all x2, starting transfers between devices, sum_over_y(): moved = lax.all_to_all(blocks, 'y', 0, 0, tiled=True)  8.92 us
  transfers between devices with their start and end apart: 17, of which 8 were waited for; matrix products, arithmetic and copies ran while one was open for 19% of the time, Pallas kernels for 0%

profile of v1, /device:TPU:6, one launch (start us, length us, event | category | flops | bytes accessed | tf_op | source)
XLA Modules:
  0.0 232.1 jit_solution(11081826242362346457)
XLA Ops:
  7.0 15.7 %collective-permute-start.1 = (bf16[768,256]{1,0:T(8,128)(2,1)S(1)}, bf16[768,256]{1,0:T(8,128)(2,1)S(1)}, u32[]{:S(2)}, u32[]{:S(2)}) collective-permute-start(bf16[768,256]{1,0:T(8,128)(2,1)S(1)} %select_multiply_fusion), channel_id=1, source_target_pairs={{0,8},{8,0},{1,9},{9,1},{2,10},{10,2},{3,11},{11,3},{4,12},{12,4},... | collective-permute-start | bytes 1179656 | tf_op jit(solution)/shard_map/ppermute | solution.py:18
  22.8 13.6 %collective-permute-done.1 = bf16[768,256]{1,0:T(8,128)(2,1)S(1)} collective-permute-done((bf16[768,256]{1,0:T(8,128)(2,1)S(1)}, bf16[768,256]{1,0:T(8,128)(2,1)S(1)}, u32[]{:S(2)}, u32[]{:S(2)}) %collective-permute-start.1) | collective-permute-done | bytes 393248 | tf_op jit(solution)/shard_map/ppermute | solution.py:18
  37.8 4.8 %all-to-all-start.1 = ((bf16[4,768,256]{1,2,0:T(8,128)(2,1)}), bf16[4,768,256]{1,2,0:T(8,128)(2,1)S(1)}, u32[]{:S(2)}, u32[]{:S(2)}) async-start(bf16[4,768,256]{1,2,0:T(8,128)(2,1)} %broadcast_in_dim.69), calls=%async_computation.1 | async-start | bytes 3145728 | tf_op jit(solution)/shard_map/all_to_all | solution.py:23
  43.5 16.9 %all-to-all-done.1 = bf16[4,768,256]{1,2,0:T(8,128)(2,1)S(1)} async-done(((bf16[4,768,256]{1,2,0:T(8,128)(2,1)}), bf16[4,768,256]{1,2,0:T(8,128)(2,1)S(1)}, u32[]{:S(2)}, u32[]{:S(2)}) %all-to-all-start.1) | async-done | bytes 1572896 | tf_op jit(solution)/shard_map/all_to_all | solution.py:23
  62.7 6.4 %all-to-all-start = ((bf16[4,768,256]{1,2,0:T(8,128)(2,1)}), bf16[4,768,256]{1,2,0:T(8,128)(2,1)}, u32[]{:S(2)}, u32[]{:S(2)}) async-start(bf16[4,768,256]{1,2,0:T(8,128)(2,1)} %broadcast_in_dim.68), calls=%async_computation | async-start | bytes 3145728 | tf_op jit(solution)/shard_map/all_to_all | solution.py:23
  74.2 5.1 %fusion.77 = (f32[2,768]{1,0:T(2,128)S(1)}, f32[2,768,768]{1,2,0:T(8,128)}) fusion(pred[768,768]{0,1:T(8,128)(4,1)} %fusion.11, bf16[768,2,128]{0,2,1:T(8,128)(2,1)S(1)} %bitcast.136, bf16[1,768,256]{2,1,0:T(8,128)(2,1)} %param.13, s32[]{:T(128)S(6)} %select_n.161), kind=kOutput, calls=%fused_computation.107 | convolution fusion | flops 306709248 | bytes 5904388 | tf_op jit(solution)/shard_map/sub | solution.py:33
  79.3 6.8 %all-to-all-done = bf16[4,768,256]{1,2,0:T(8,128)(2,1)} async-done(((bf16[4,768,256]{1,2,0:T(8,128)(2,1)}), bf16[4,768,256]{1,2,0:T(8,128)(2,1)}, u32[]{:S(2)}, u32[]{:S(2)}) %all-to-all-start) | async-done | bytes 1572896 | tf_op jit(solution)/shard_map/all_to_all | solution.py:23
  88.0 3.0 %constant_dynamic-slice_fusion.1 = (bf16[1,4,2,256,256]{4,3,2,1,0:T(8,128)(2,1)}, bf16[1,4,2,256,256]{4,3,2,1,0:T(8,128)(2,1)}) fusion(bf16[2,4,2,256,256]{4,3,2,1,0:T(8,128)(2,1)} %bitcast.135, s32[]{:T(128)S(6)} %select_n.169, s32[]{:T(128)S(6)} %select_n.171), kind=kLoop, calls=%fused_computation.101 | loop fusion | bytes 4194312 | tf_op jit(solution)/shard_map/jit(dynamic_index_in_dim)/dynamic_slice | solution.py:77
  95.6 3.0 %fusion.23 = f32[128,2,768]{2,0,1:T(8,128)S(1)} fusion(bf16[1,768,256]{2,1,0:T(8,128)(2,1)} %param.14, s32[]{:T(128)S(6)} %select_n.161, f32[2,768,768]{1,2,0:T(8,128)} %get-tuple-element.35, f32[2,768]{1,0:T(2,128)S(1)} %get-tuple-element.34), kind=kOutput, calls=%fused_computation.30 | convolution fusion | flops 304742400 | bytes 5707780 | tf_op jit(solution)/shard_map/hij,jd->ihd/dot_general | solution.py:70
  102.3 5.2 %fusion.30 = (f32[768]{0:T(1024)S(1)}, bf16[768,256]{0,1:T(8,128)(2,1)S(1)}, bf16[768,256]{0,1:T(8,128)(2,1)}) fusion(f32[128,2,768]{2,0,1:T(8,128)S(1)} %fusion.23, f32[768]{0:T(1024)S(1)} %divide_reduce_fusion, f32[768,256]{0,1:T(8,128)S(1)} %fusion.16, bf16[1,4,2,256,256]{3,4,1,2,0:T(8,128)(2,1)S(1)} %copy-done.2, bf16[4,1,768,256]{2,3,1,0:T(8,128)(2,1)} %bitcast.10, ...), kind=kOutput, calls=%fused_computation.46 | convolution fusion | flops 811400448 | bytes 6559745 | tf_op jit(solution)/shard_map/xqif,xqfc->ic/dot_general | solution.py:39
  108.5 4.3 %convolution_convert_fusion.1 = bf16[256,4,2,256]{0,3,2,1:T(8,128)(2,1)S(1)} fusion(bf16[768,256]{0,1:T(8,128)(2,1)S(1)} %get-tuple-element.28, bf16[4,1,768,256]{2,3,1,0:T(8,128)(2,1)} %bitcast.10, bf16[4,1,768,256]{2,3,1,0:T(8,128)(2,1)} %bitcast.9, pred[]{:T(512)S(6)} %eq.56), kind=kOutput, calls=%fused_computation.23 | convolution fusion | flops 819986432 | bytes 4587521 | tf_op jit(solution)/shard_map/xqif,ic->qfxc/dot_general | solution.py:40
  115.0 4.5 %all-to-all-start.3 = ((bf16[4,4,128,256]{3,2,1,0:T(8,128)(2,1)}), bf16[4,4,128,256]{3,2,1,0:T(8,128)(2,1)S(1)}, u32[]{:S(2)}, u32[]{:S(2)}) async-start(bf16[4,4,128,256]{3,2,1,0:T(8,128)(2,1)} %bitcast.134), calls=%async_computation.3 | async-start | bytes 2097152 | tf_op jit(solution)/shard_map/all_to_all | solution.py:46
  119.4 3.4 %fusion.1 = (f32[2,768]{1,0:T(2,128)S(1)}, f32[768,768,2]{1,0,2:T(8,128)S(1)}) fusion(f32[2,768,768]{1,2,0:T(8,128)} %get-tuple-element.35, f32[2,768]{1,0:T(2,128)S(1)} %get-tuple-element.34, bf16[768,2,128]{0,2,1:T(8,128)(2,1)} %bitcast.143, bf16[1,768,256]{2,1,0:T(8,128)(2,1)S(1)} %copy-done.5, s32[]{:T(128)S(6)} %select_n.161), kind=kOutput, calls=%fused_computation.4 | convolution fusion | flops 305527296 | bytes 10039300 | tf_op jit(solution)/shard_map/ihd,jd->hij/dot_general | solution.py:97
  126.4 8.8 %all-to-all-done.3 = bf16[4,4,128,256]{3,2,1,0:T(8,128)(2,1)S(1)} async-done(((bf16[4,4,128,256]{3,2,1,0:T(8,128)(2,1)}), bf16[4,4,128,256]{3,2,1,0:T(8,128)(2,1)S(1)}, u32[]{:S(2)}, u32[]{:S(2)}) %all-to-all-start.3) | async-done | bytes 1048608 | tf_op jit(solution)/shard_map/all_to_all | solution.py:46
  135.2 4.5 %all-to-all-start.2 = ((bf16[4,4,128,256]{3,2,1,0:T(8,128)(2,1)}), bf16[4,4,128,256]{3,2,1,0:T(8,128)(2,1)}, u32[]{:S(2)}, u32[]{:S(2)}) async-start(bf16[4,4,128,256]{3,2,1,0:T(8,128)(2,1)} %bitcast.38), calls=%async_computation.2 | async-start | bytes 2097152 | tf_op jit(solution)/shard_map/all_to_all | solution.py:46
  139.7 3.3 %convolution_bitcast_fusion = f32[768,128]{0,1:T(8,128)S(1)} fusion(bf16[768,2,128]{0,2,1:T(8,128)(2,1)} %bitcast.144, f32[2,768,768]{1,2,0:T(8,128)} %get-tuple-element.35, f32[2,768]{1,0:T(2,128)S(1)} %get-tuple-element.34), kind=kOutput, calls=%fused_computation.31 | convolution fusion | flops 304349184 | bytes 5511168 | tf_op jit(solution)/shard_map/hij,ihd->jd/dot_general | solution.py:94
  146.5 8.0 %all-to-all-done.2 = bf16[4,4,128,256]{3,2,1,0:T(8,128)(2,1)} async-done(((bf16[4,4,128,256]{3,2,1,0:T(8,128)(2,1)}), bf16[4,4,128,256]{3,2,1,0:T(8,128)(2,1)}, u32[]{:S(2)}, u32[]{:S(2)}) %all-to-all-start.2) | async-done | bytes 1048608 | tf_op jit(solution)/shard_map/all_to_all | solution.py:46
  157.8 29.4 %all-to-all-start.4 = ((bf16[8,128,256]{2,1,0:T(8,128)(2,1)}), bf16[8,128,256]{2,1,0:T(8,128)(2,1)S(1)}, u32[]{:S(2)}, u32[]{:S(2)}) async-start(bf16[8,128,256]{2,1,0:T(8,128)(2,1)} %maximum_select_fusion.3), calls=%async_computation.4 | async-start | bytes 1048576 | tf_op jit(solution)/shard_map/all_to_all | solution.py:141
  188.2 4.0 %collective-permute-start.6 = (bf16[384,256]{0,1:T(8,128)(2,1)S(1)}, bf16[384,256]{0,1:T(8,128)(2,1)S(1)}, u32[]{:S(2)}, u32[]{:S(2)}) collective-permute-start(bf16[384,256]{0,1:T(8,128)(2,1)S(1)} %fusion.45), channel_id=1, source_target_pairs={{0,4},{2,6},{4,0},{6,2},{1,5},{3,7},{5,1},{7,3},{8,12},{10,14},{12... | collective-permute-start | bytes 589832 | tf_op jit(solution)/shard_map/ppermute | solution.py:120
  192.3 2.7 %collective-permute-start.5 = (bf16[384,256]{0,1:T(8,128)(2,1)S(1)}, bf16[384,256]{0,1:T(8,128)(2,1)S(1)}, u32[]{:S(2)}, u32[]{:S(2)}) collective-permute-start(bf16[384,256]{0,1:T(8,128)(2,1)S(1)} %fusion.45), channel_id=1, source_target_pairs={{0,6},{2,0},{4,2},{6,4},{1,7},{3,1},{5,3},{7,5},{8,14},{10,8},{12,... | collective-permute-start | bytes 589832 | tf_op jit(solution)/shard_map/ppermute | solution.py:120
  195.0 4.4 %collective-permute-start.4 = (bf16[384,256]{0,1:T(8,128)(2,1)S(1)}, bf16[384,256]{0,1:T(8,128)(2,1)S(1)}, u32[]{:S(2)}, u32[]{:S(2)}) collective-permute-start(bf16[384,256]{0,1:T(8,128)(2,1)S(1)} %fusion.45), channel_id=1, source_target_pairs={{0,2},{2,4},{4,6},{6,0},{1,3},{3,5},{5,7},{7,1},{8,10},{10,12},{12... | collective-permute-start | bytes 589832 | tf_op jit(solution)/shard_map/ppermute | solution.py:120
  204.4 3.5 %collective-permute-done.9 = f32[768]{0:T(1024)S(1)} collective-permute-done((f32[768]{0:T(1024)S(1)}, f32[768]{0:T(1024)S(1)}, u32[]{:S(2)}, u32[]{:S(2)}) %collective-permute-start.9) | collective-permute-done | bytes 3104 | tf_op jit(solution)/shard_map/ppermute | solution.py:122
  210.1 4.8 %collective-permute-done.10 = f32[768]{0:T(1024)S(1)} collective-permute-done((f32[768]{0:T(1024)S(1)}, f32[768]{0:T(1024)S(1)}, u32[]{:S(2)}, u32[]{:S(2)}) %collective-permute-start.10) | collective-permute-done | bytes 3104 | tf_op jit(solution)/shard_map/ppermute | solution.py:123
  214.9 8.4 %collective-permute-start.11 = (f32[768]{0:T(1024)S(1)}, f32[768]{0:T(1024)S(1)}, u32[]{:S(2)}, u32[]{:S(2)}) collective-permute-start(f32[768]{0:T(1024)S(1)} %add.132), channel_id=1, source_target_pairs={{0,8},{8,0},{1,9},{9,1},{2,10},{10,2},{3,11},{11,3},{4,12},{12,4},... | collective-permute-start | bytes 9224 | tf_op jit(solution)/shard_map/ppermute | solution.py:18
  (77 shorter events, 56.6 us)
Async XLA Ops:
  0.6 3.5 %copy-start = (bf16[1,3072,256]{2,1,0:T(8,128)(2,1)S(1)}, bf16[1,3072,256]{2,1,0:T(8,128)(2,1)}, u32[]{:S(2)}) copy-start(bf16[1,3072,256]{2,1,0:T(8,128)(2,1)} %param.8) | copy-start | bytes 4718596
  7.0 29.4 %collective-permute-start.1 = (bf16[768,256]{1,0:T(8,128)(2,1)S(1)}, bf16[768,256]{1,0:T(8,128)(2,1)S(1)}, u32[]{:S(2)}, u32[]{:S(2)}) collective-permute-start(bf16[768,256]{1,0:T(8,128)(2,1)S(1)} %select_multiply_fusion), channel_id=1, source_target_pairs={{0,8},{8,0},{1,9},{9,1},{2,10},{10,2},{3,11},{11,3},{4,12},{12,4},... | collective-permute-start | bytes 1179656 | tf_op jit(solution)/shard_map/ppermute | solution.py:18
  37.8 22.6 %all-to-all-start.1 = ((bf16[4,768,256]{1,2,0:T(8,128)(2,1)}), bf16[4,768,256]{1,2,0:T(8,128)(2,1)S(1)}, u32[]{:S(2)}, u32[]{:S(2)}) async-start(bf16[4,768,256]{1,2,0:T(8,128)(2,1)} %broadcast_in_dim.69), calls=%async_computation.1 | async-start | bytes 3145728 | tf_op jit(solution)/shard_map/all_to_all | solution.py:23
  62.7 23.4 %all-to-all-start = ((bf16[4,768,256]{1,2,0:T(8,128)(2,1)}), bf16[4,768,256]{1,2,0:T(8,128)(2,1)}, u32[]{:S(2)}, u32[]{:S(2)}) async-start(bf16[4,768,256]{1,2,0:T(8,128)(2,1)} %broadcast_in_dim.68), calls=%async_computation | async-start | bytes 3145728 | tf_op jit(solution)/shard_map/all_to_all | solution.py:23
  69.1 29.5 %collective-permute-start.2 = (bf16[4,768,256]{1,2,0:T(8,128)(2,1)S(1)}, bf16[4,768,256]{1,2,0:T(8,128)(2,1)}, u32[]{:S(2)}, u32[]{:S(2)}) collective-permute-start(bf16[4,768,256]{1,2,0:T(8,128)(2,1)S(1)} %all-to-all-done.1), channel_id=1, source_target_pairs={{0,1},{1,0},{2,3},{3,2},{4,5},{5,4},{6,7},{7,6},{8,9},{9,8},{10,11... | collective-permute-start | bytes 4718600 | tf_op jit(solution)/shard_map/ppermute | solution.py:18
  86.1 16.0 %collective-permute-start = (bf16[4,768,256]{1,2,0:T(8,128)(2,1)}, bf16[4,768,256]{1,2,0:T(8,128)(2,1)}, u32[]{:S(2)}, u32[]{:S(2)}) collective-permute-start(bf16[4,768,256]{1,2,0:T(8,128)(2,1)} %all-to-all-done), channel_id=1, source_target_pairs={{0,1},{1,0},{2,3},{3,2},{4,5},{5,4},{6,7},{7,6},{8,9},{9,8},{10,11... | collective-permute-start | bytes 4718600 | tf_op jit(solution)/shard_map/ppermute | solution.py:18
  91.1 4.5 %copy-start.4 = (f32[1,768]{1,0:T(1,128)S(1)}, f32[1,768]{1,0:T(1,128)}, u32[]{:S(2)}) copy-start(f32[1,768]{1,0:T(1,128)} %param.11) | copy-start | bytes 9220
  98.6 2.5 %copy-start.3 = (bf16[1,4,2,256,256]{3,4,1,2,0:T(8,128)(2,1)S(1)}, bf16[1,4,2,256,256]{3,4,1,2,0:T(8,128)(2,1)}, u32[]{:S(2)}) copy-start(bf16[1,4,2,256,256]{3,4,1,2,0:T(8,128)(2,1)} %copy.113) | copy-start | bytes 3145732
  112.8 6.6 %copy-start.5 = (bf16[1,768,256]{2,1,0:T(8,128)(2,1)S(1)}, bf16[1,768,256]{2,1,0:T(8,128)(2,1)}, u32[]{:S(2)}) copy-start(bf16[1,768,256]{2,1,0:T(8,128)(2,1)} %param.14) | copy-start | bytes 1179652
  115.0 20.2 %all-to-all-start.3 = ((bf16[4,4,128,256]{3,2,1,0:T(8,128)(2,1)}), bf16[4,4,128,256]{3,2,1,0:T(8,128)(2,1)S(1)}, u32[]{:S(2)}, u32[]{:S(2)}) async-start(bf16[4,4,128,256]{3,2,1,0:T(8,128)(2,1)} %bitcast.134), calls=%async_computation.3 | async-start | bytes 2097152 | tf_op jit(solution)/shard_map/all_to_all | solution.py:46
  119.4 3.7 %slice-start = ((s8[4718592]{0:T(1024)(128)(4,1)}), s8[4194304]{0:T(1024)(128)(4,1)S(1)}, s32[]{:S(2)}) async-start(s8[4718592]{0:T(1024)(128)(4,1)} %bitcast.132), calls=%async_computation.5 | async-start | bytes 8388608
  119.4 3.8 %slice-start.1 = ((s8[4718592]{0:T(1024)(128)(4,1)}), s8[524288]{0:T(1024)(128)(4,1)S(1)}, s32[]{:S(2)}) async-start(s8[4718592]{0:T(1024)(128)(4,1)} %bitcast.132), calls=%async_computation.6 | async-start | bytes 1048576
  124.0 1.4 copy-start.1
  135.2 19.3 %all-to-all-start.2 = ((bf16[4,4,128,256]{3,2,1,0:T(8,128)(2,1)}), bf16[4,4,128,256]{3,2,1,0:T(8,128)(2,1)}, u32[]{:S(2)}, u32[]{:S(2)}) async-start(bf16[4,4,128,256]{3,2,1,0:T(8,128)(2,1)} %bitcast.38), calls=%async_computation.2 | async-start | bytes 2097152 | tf_op jit(solution)/shard_map/all_to_all | solution.py:46
  143.7 43.5 %collective-permute-start.3 = (bf16[384,256]{0,1:T(8,128)(2,1)}, bf16[384,256]{0,1:T(8,128)(2,1)}, u32[]{:S(2)}, u32[]{:S(2)}) collective-permute-start(bf16[384,256]{0,1:T(8,128)(2,1)} %fusion.42), channel_id=1, source_target_pairs={{0,1},{1,0},{2,3},{3,2},{4,5},{5,4},{6,7},{7,6},{8,9},{9,8},{10,11... | collective-permute-start | bytes 589832 | tf_op jit(solution)/shard_map/ppermute | solution.py:18
  157.8 73.5 %all-to-all-start.4 = ((bf16[8,128,256]{2,1,0:T(8,128)(2,1)}), bf16[8,128,256]{2,1,0:T(8,128)(2,1)S(1)}, u32[]{:S(2)}, u32[]{:S(2)}) async-start(bf16[8,128,256]{2,1,0:T(8,128)(2,1)} %maximum_select_fusion.3), calls=%async_computation.4 | async-start | bytes 1048576 | tf_op jit(solution)/shard_map/all_to_all | solution.py:141
  188.2 35.0 %collective-permute-start.6 = (bf16[384,256]{0,1:T(8,128)(2,1)S(1)}, bf16[384,256]{0,1:T(8,128)(2,1)S(1)}, u32[]{:S(2)}, u32[]{:S(2)}) collective-permute-start(bf16[384,256]{0,1:T(8,128)(2,1)S(1)} %fusion.45), channel_id=1, source_target_pairs={{0,4},{2,6},{4,0},{6,2},{1,5},{3,7},{5,1},{7,3},{8,12},{10,14},{12... | collective-permute-start | bytes 589832 | tf_op jit(solution)/shard_map/ppermute | solution.py:120
  192.3 31.0 %collective-permute-start.5 = (bf16[384,256]{0,1:T(8,128)(2,1)S(1)}, bf16[384,256]{0,1:T(8,128)(2,1)S(1)}, u32[]{:S(2)}, u32[]{:S(2)}) collective-permute-start(bf16[384,256]{0,1:T(8,128)(2,1)S(1)} %fusion.45), channel_id=1, source_target_pairs={{0,6},{2,0},{4,2},{6,4},{1,7},{3,1},{5,3},{7,5},{8,14},{10,8},{12,... | collective-permute-start | bytes 589832 | tf_op jit(solution)/shard_map/ppermute | solution.py:120
  195.0 28.3 %collective-permute-start.4 = (bf16[384,256]{0,1:T(8,128)(2,1)S(1)}, bf16[384,256]{0,1:T(8,128)(2,1)S(1)}, u32[]{:S(2)}, u32[]{:S(2)}) collective-permute-start(bf16[384,256]{0,1:T(8,128)(2,1)S(1)} %fusion.45), channel_id=1, source_target_pairs={{0,2},{2,4},{4,6},{6,0},{1,3},{3,5},{5,7},{7,1},{8,10},{10,12},{12... | collective-permute-start | bytes 589832 | tf_op jit(solution)/shard_map/ppermute | solution.py:120
  199.3 3.1 %collective-permute-start.8 = (f32[768]{0:T(1024)S(1)}, f32[768]{0:T(1024)S(1)}, u32[]{:S(2)}, u32[]{:S(2)}) collective-permute-start(f32[768]{0:T(1024)S(1)} %get-tuple-element.27), channel_id=1, source_target_pairs={{0,1},{1,0},{2,3},{3,2},{4,5},{5,4},{6,7},{7,6},{8,9},{9,8},{10,11... | collective-permute-start | bytes 9224 | tf_op jit(solution)/shard_map/ppermute | solution.py:18
  202.4 5.5 %collective-permute-start.9 = (f32[768]{0:T(1024)S(1)}, f32[768]{0:T(1024)S(1)}, u32[]{:S(2)}, u32[]{:S(2)}) collective-permute-start(f32[768]{0:T(1024)S(1)} %add.130), channel_id=1, source_target_pairs={{0,2},{2,4},{4,6},{6,0},{1,3},{3,5},{5,7},{7,1},{8,10},{10,12},{12... | collective-permute-start | bytes 9224 | tf_op jit(solution)/shard_map/ppermute | solution.py:122
  207.9 7.0 %collective-permute-start.10 = (f32[768]{0:T(1024)S(1)}, f32[768]{0:T(1024)S(1)}, u32[]{:S(2)}, u32[]{:S(2)}) collective-permute-start(f32[768]{0:T(1024)S(1)} %add.131), channel_id=1, source_target_pairs={{0,4},{2,6},{4,0},{6,2},{1,5},{3,7},{5,1},{7,3},{8,12},{10,14},{12... | collective-permute-start | bytes 9224 | tf_op jit(solution)/shard_map/ppermute | solution.py:123
  214.9 14.7 %collective-permute-start.11 = (f32[768]{0:T(1024)S(1)}, f32[768]{0:T(1024)S(1)}, u32[]{:S(2)}, u32[]{:S(2)}) collective-permute-start(f32[768]{0:T(1024)S(1)} %add.132), channel_id=1, source_target_pairs={{0,8},{8,0},{1,9},{9,1},{2,10},{10,2},{3,11},{11,3},{4,12},{12,4},... | collective-permute-start | bytes 9224 | tf_op jit(solution)/shard_map/ppermute | solution.py:18
  224.4 5.7 %collective-permute-start.7 = (bf16[384,512]{1,0:T(8,128)(2,1)S(1)}, bf16[384,512]{1,0:T(8,128)(2,1)S(1)}, u32[]{:S(2)}, u32[]{:S(2)}) collective-permute-start(bf16[384,512]{1,0:T(8,128)(2,1)S(1)} %convert_element_type.103), channel_id=1, source_target_pairs={{0,1},{1,0},{2,3},{3,2},{4,5},{5,4},{6,7},{7,6},{8,9},{9,8},{10,11... | collective-permute-start | bytes 1179656 | tf_op jit(solution)/shard_map/ppermute | solution.py:18
  (1 other events, 1.2 us)

commit v2 on v1

v2 whole, which is shorter than its diff:
```python
import functools

import jax
import jax.numpy as jnp
from jax import lax
from jax.experimental import pallas as pl
from jax.experimental.pallas import tpu as pltpu
from jax.sharding import Mesh
from jax.sharding import PartitionSpec as P

HEAD_SIZE = 128
ZL, Y, ZH, X, CORE = 8, 4, 2, 4, 2
SLOTS, WIDE, HEADS = 768, 256, 2
SCALE = HEAD_SIZE ** (-0.5)
BF, F32 = jnp.bfloat16, jnp.float32
ROWS = 256
STEP = 192
EXTRA = 16
LIMIT = pltpu.CompilerParams(vmem_limit_bytes=40 * 1024 * 1024)


def ring(n, k):
    return [(i, (i + k) % n) for i in range(n)]


def swap(value, axis):
    return lax.ppermute(value, axis, ring(2, 1))


def spread_x(copies):
    return lax.all_to_all(copies, "x", 0, 0, tiled=True)


def repeated(block):
    return jnp.broadcast_to(block[None], (X,) + block.shape)


def exchange(rows, picked):
    other = swap(picked[:rows], "zh")
    near = spread_x(repeated(picked))
    far = swap(near, "core")
    other = jnp.pad(other, ((0, SLOTS - rows), (0, 0)))
    return repeated(other), near, far


def transposed_dot(a, b):
    return lax.dot_general(a, b, (((0,), (0,)), ((), ())), preferred_element_type=F32)


def rows_dot(a, b):
    return lax.dot_general(a, b, (((1,), (1,)), ((), ())), preferred_element_type=F32)


def allowed_block(info_ref, pos_col, pos_row):
    first = pl.program_id(0) * ROWS
    shape = (ROWS, SLOTS)
    i = lax.broadcasted_iota(jnp.int32, shape, 0) + first
    j = lax.broadcasted_iota(jnp.int32, shape, 1)
    return ((j < info_ref[1]) & (pos_row <= pos_col)) | (i == j)


def forward_kernel(info_ref, q_ref, k_ref, v_ref, col_ref, row_ref, logit_ref, att_ref, scaled_ref, lse_ref):
    allowed = allowed_block(info_ref, col_ref[...], row_ref[...])
    weight = 1.0 / (1.0 + jnp.exp(-logit_ref[...]))
    for h in range(HEADS):
        lanes = slice(h * HEAD_SIZE, (h + 1) * HEAD_SIZE)
        s = rows_dot(q_ref[:, lanes], k_ref[...]) * SCALE
        s = jnp.where(allowed, s, -1e30)
        top = jnp.max(s, axis=1, keepdims=True)
        e = jnp.exp(s - top)
        total = jnp.sum(e, axis=1, keepdims=True)
        p = (e * (1.0 / total)).astype(BF)
        att = jnp.dot(p, v_ref[...], preferred_element_type=F32).astype(BF)
        att_ref[:, lanes] = att
        scaled_ref[:, lanes] = (weight * att.astype(F32)).astype(BF)
        lse_ref[:, h : h + 1] = top + jnp.log(total)


def backward_kernel(
    info_ref, q_ref, k_ref, v_ref, col_ref, row_ref, logit_ref, lse_ref, att_ref, go_ref,
    gq_ref, kv_ref, router_ref, sum_ref,
):
    step = pl.program_id(0)
    allowed = allowed_block(info_ref, col_ref[...], row_ref[...])
    weight = 1.0 / (1.0 + jnp.exp(-logit_ref[...]))
    grad_o = go_ref[...]
    router_ref[...] = jnp.sum(grad_o * att_ref[...].astype(F32), axis=1, keepdims=True)
    grad_attn = (weight * grad_o).astype(BF)

    @pl.when(step == 0)
    def _():
        sum_ref[...] = jnp.zeros_like(sum_ref)

    for h in range(HEADS):
        lanes = slice(h * HEAD_SIZE, (h + 1) * HEAD_SIZE)
        q = q_ref[:, lanes]
        s = rows_dot(q, k_ref[...]) * SCALE
        p = jnp.exp(jnp.where(allowed, s - lse_ref[:, h : h + 1], -1e30))
        ga = grad_attn[:, lanes]
        gp = rows_dot(ga, v_ref[...])
        delta = jnp.sum(p * gp, axis=1, keepdims=True)
        gs = (p * (gp - delta)).astype(BF)
        gq = jnp.dot(gs, k_ref[...], preferred_element_type=F32) * SCALE
        gq_ref[:, lanes] = gq.astype(BF)
        sum_ref[:, :HEAD_SIZE] += transposed_dot(gs, q)
        sum_ref[:, HEAD_SIZE:] += transposed_dot(p.astype(BF), ga)

    @pl.when(step == pl.num_programs(0) - 1)
    def _():
        kv_ref[:, :HEAD_SIZE] = (sum_ref[:, :HEAD_SIZE] * SCALE).astype(BF)
        kv_ref[:, HEAD_SIZE:] = sum_ref[:, HEAD_SIZE:].astype(BF)


def by_rows(width):
    return pl.BlockSpec((ROWS, width), lambda i, info: (i, 0))


def by_group():
    return pl.BlockSpec((SLOTS, HEAD_SIZE), lambda i, info: (0, info[0]))


def whole(shape):
    return pl.BlockSpec(shape, lambda i, info: (0,) * len(shape))


def shape_of(shape, dtype):
    return jax.ShapeDtypeStruct(shape, dtype)


def forward(info, q, k, v, pos_col, pos_row, logit_col):
    return pl.pallas_call(
        forward_kernel,
        grid_spec=pltpu.PrefetchScalarGridSpec(
            num_scalar_prefetch=1,
            grid=(SLOTS // ROWS,),
            in_specs=[by_rows(WIDE), by_group(), by_group(), by_rows(1), whole((1, SLOTS)), by_rows(1)],
            out_specs=[by_rows(WIDE), by_rows(WIDE), by_rows(HEADS)],
        ),
        out_shape=[shape_of((SLOTS, WIDE), BF), shape_of((SLOTS, WIDE), BF), shape_of((SLOTS, HEADS), F32)],
        compiler_params=LIMIT,
        cost_estimate=pl.CostEstimate(flops=604 * 10**6, bytes_accessed=2 * 10**6, transcendentals=1200000),
    )(info, q, k, v, pos_col, pos_row, logit_col)


def backward(info, q, k, v, pos_col, pos_row, logit_col, lse, att, grad_o):
    return pl.pallas_call(
        backward_kernel,
        grid_spec=pltpu.PrefetchScalarGridSpec(
            num_scalar_prefetch=1,
            grid=(SLOTS // ROWS,),
            in_specs=[
                by_rows(WIDE), by_group(), by_group(), by_rows(1), whole((1, SLOTS)), by_rows(1),
                by_rows(HEADS), by_rows(WIDE), by_rows(WIDE),
            ],
            out_specs=[by_rows(WIDE), whole((SLOTS, WIDE)), by_rows(1)],
            scratch_shapes=[pltpu.VMEM((SLOTS, WIDE), F32)],
        ),
        out_shape=[shape_of((SLOTS, WIDE), BF), shape_of((SLOTS, WIDE), BF), shape_of((SLOTS, 1), F32)],
        compiler_params=LIMIT,
        cost_estimate=pl.CostEstimate(flops=1510 * 10**6, bytes_accessed=4 * 10**6, transcendentals=1200000),
    )(info, q, k, v, pos_col, pos_row, logit_col, lse, att, grad_o)


def products_kernel(info_ref, near_ref, far_ref, wn_ref, wf_ref, scaled_ref, *refs):
    go_ref, wg_ref = refs[-2:]
    core = info_ref[0]
    near, far, scaled = near_ref[0], far_ref[0], scaled_ref[...]
    part = jnp.dot(near, wn_ref[0], preferred_element_type=F32)
    part = part + jnp.dot(far, wf_ref[0], preferred_element_type=F32)
    first = pl.program_id(0) == 0

    @pl.when(first)
    def _():
        go_ref[...] = part + refs[0][...] if len(refs) == 3 else part

    @pl.when(jnp.logical_not(first))
    def _():
        go_ref[...] += part

    wg_ref[pl.ds(2 * core, 2), 0] = transposed_dot(near, scaled).astype(BF).reshape(2, 128, WIDE)
    wg_ref[pl.ds(2 - 2 * core, 2), 0] = transposed_dot(far, scaled).astype(BF).reshape(2, 128, WIDE)


def products(core, half, near, far, w_out, scaled, begin=None):
    info = jnp.stack([core, half]).astype(jnp.int32)
    shard = pl.BlockSpec((1, SLOTS, WIDE), lambda i, info: (i, 0, 0))
    w_near = pl.BlockSpec((1, WIDE, WIDE), lambda i, info: (info[1] * 8 + i * 2 + info[0], 0, 0))
    w_far = pl.BlockSpec((1, WIDE, WIDE), lambda i, info: (info[1] * 8 + i * 2 + 1 - info[0], 0, 0))
    w_parts = w_out.reshape(ZH * X * CORE, WIDE, WIDE)
    more = [] if begin is None else [begin]
    return pl.pallas_call(
        products_kernel,
        grid_spec=pltpu.PrefetchScalarGridSpec(
            num_scalar_prefetch=1,
            grid=(X,),
            in_specs=[shard, shard, w_near, w_far, whole((SLOTS, WIDE))] + [whole((SLOTS, WIDE)) for _ in more],
            out_specs=[
                whole((SLOTS, WIDE)),
                pl.BlockSpec((Y, 1, 128, WIDE), lambda i, info: (0, i, 0, 0)),
            ],
        ),
        out_shape=[shape_of((SLOTS, WIDE), F32), shape_of((Y, X, 128, WIDE), BF)],
        compiler_params=LIMIT,
        cost_estimate=pl.CostEstimate(flops=1610 * 10**6, bytes_accessed=7 * 10**6, transcendentals=0),
    )(info, near, far, w_parts, w_parts, scaled, *more)


def fold_kernel(info_ref, moved_ref, *refs):
    refs[-1][0] = jnp.sum(moved_ref[...].astype(F32), axis=0)[0].astype(BF)


def fold(half, moved, begin=None):
    more = [] if begin is None else [begin]
    return pl.pallas_call(
        fold_kernel,
        grid_spec=pltpu.PrefetchScalarGridSpec(
            num_scalar_prefetch=1,
            grid=(X,),
            in_specs=[pl.BlockSpec((Y, 1, 128, WIDE), lambda i, info: (0, i, 0, 0))]
            + [pl.BlockSpec(memory_space=pl.ANY) for _ in more],
            out_specs=pl.BlockSpec((1, 128, WIDE), lambda i, info: (info[0] * 4 + i, 0, 0)),
        ),
        out_shape=shape_of((ZL, 128, WIDE), BF),
        input_output_aliases={2: 0} if more else {},
        compiler_params=LIMIT,
        cost_estimate=pl.CostEstimate(flops=4 * 10**6, bytes_accessed=3 * 10**6, transcendentals=0),
    )(half.astype(jnp.int32).reshape(1), moved, *more)


def over_y(blocks):
    return lax.all_to_all(blocks, "y", 0, 0, tiled=True)


def packed(router):
    lead = lax.reduce_precision(router, 8, 7)
    terms = jnp.concatenate([lead, router - lead]).astype(BF).reshape(-1, WIDE)
    return jnp.pad(terms, ((0, EXTRA - terms.shape[0]), (0, 0)))


def unpacked(rows):
    terms = rows[: 2 * SLOTS // WIDE].astype(F32).reshape(2, SLOTS)
    return terms[0] + terms[1]


def per_device(cotangent, routed, counts, logits, query_rows, key_rows, routed_value_rows, w_out):
    zh, x, core = lax.axis_index("zh"), lax.axis_index("x"), lax.axis_index("core")
    dp_index = lax.axis_index("zl") * Y + lax.axis_index("y")
    own = jnp.arange(counts.shape[0], dtype=jnp.int32) == dp_index
    own_count = jnp.sum(jnp.where(own, counts, 0))
    live_rows = jnp.arange(SLOTS, dtype=jnp.int32) < own_count
    positions = routed[0]
    picked = cotangent[0].at[positions].get(mode="promise_in_bounds")
    picked = jnp.where(live_rows[:, None], picked, jnp.zeros((), BF))

    sizes = range(STEP, SLOTS + 1, STEP)
    branch = jnp.maximum(own_count - 1, 0) // STEP
    other_copies, own_near, own_far = lax.switch(
        branch, [functools.partial(exchange, rows) for rows in sizes], picked
    )
    other_near = spread_x(other_copies)

    info = jnp.stack([x // 2, own_count]).astype(jnp.int32)
    attention = (
        info, query_rows[0], key_rows[0], routed_value_rows[0],
        positions[:, None], positions[None, :], logits[0][:, None],
    )
    attended, scaled, lse = forward(*attention)
    grad_o_own, w_grad_own = products(core, zh, own_near, own_far, w_out, scaled)
    blocks = fold(zh, over_y(w_grad_own))

    other_far = swap(other_near, "core")
    grad_o, w_grad_other = products(core, 1 - zh, other_near, other_far, w_out, scaled, grad_o_own)
    moved_other = over_y(w_grad_other)

    grad_q, kv, router = backward(*attention, lse, attended, grad_o)
    router = router[:, 0]
    half = SLOTS // 2
    kept = lax.dynamic_slice_in_dim(kv, core * half, half, 0)
    sent = lax.dynamic_slice_in_dim(kv, (1 - core) * half, half, 0)
    came = swap(jnp.concatenate([sent, packed(router)], 0), "core")
    chip = (kept.astype(F32) + came[:half].astype(F32)).astype(BF)
    router = router + unpacked(came[half:])
    pieces = spread_x(repeated(jnp.concatenate([chip, packed(router)], 0)))

    blocks = fold(1 - zh, moved_other, blocks)
    final = lax.all_to_all(blocks, "zl", 0, 0, tiled=True)
    w_grad = jnp.sum(final.astype(F32), axis=0).astype(BF)

    wide = pieces[:, :half].astype(F32)
    first, second = wide[0] + wide[1], wide[2] + wide[3]
    joined = jnp.concatenate(
        [first[:, :HEAD_SIZE], second[:, :HEAD_SIZE], first[:, HEAD_SIZE:], second[:, HEAD_SIZE:]], 1
    ).astype(BF)
    theirs = swap(joined, "core")
    router = sum(unpacked(pieces[s, half:]) for s in range(X))
    router = router + swap(router, "zh")
    rows = jnp.where(
        core == 0, jnp.concatenate([joined, theirs], 0), jnp.concatenate([theirs, joined], 0)
    )
    key_total, value_total = rows[:, : 2 * HEAD_SIZE], rows[:, 2 * HEAD_SIZE :]
    router_weight = jax.nn.sigmoid(logits[0])
    grad_logits = router * router_weight * (1.0 - router_weight)
    return (grad_q[None], key_total[None], value_total[None], w_grad, grad_logits[None])


def solution(mesh):
    fine = Mesh(mesh.devices.reshape(ZL, Y, ZH, X, CORE), ("zl", "y", "zh", "x", "core"))
    dp, col = ("zl", "y"), ("x", "core")
    row_col = ("zh",) + col
    placed = (
        P(dp, None, row_col),
        P(dp, None),
        P(),
        P(dp, None),
        P(dp, None, row_col),
        P(dp, None, "zh"),
        P(dp, None, "zh"),
        P(None, row_col),
    )
    return jax.shard_map(
        per_device,
        mesh=fine,
        in_specs=placed,
        out_specs=(
            P(dp, None, row_col),
            P(dp, None, "zh"),
            P(dp, None, "zh"),
            P(dp, row_col),
            P(dp, None),
        ),
        check_vma=False,
    )
```

time: 236 us -> 225 us (0.953)
  the two profiles are of different devices: /device:TPU:6 before, /device:TPU:64 now
where the time goes in v2:
time: 225 us; the launch traced here: 224 us
  starting transfers between devices  66 us (29%)
  waiting for transfers between devices  51.6 us (23%)
  blocking collectives  48.2 us (21%)
  Pallas kernels  31.2 us (14%)
  local copies, waits for them, and re-layouts  18 us (8%)
  other arithmetic  7.37 us (3%)
    all_to_all x2, blocking collectives, spread_x(): return lax.all_to_all(copies, 'x', 0, 0, tiled=True)  48.2 us
    ppermute x6, starting transfers between devices, swap(): return lax.ppermute(value, axis, ring(2, 1))  31.4 us
    ppermute x6, waiting for transfers between devices, swap(): return lax.ppermute(value, axis, ring(2, 1))  28.3 us
    all_to_all x1, starting transfers between devices, per_device(): final = lax.all_to_all(blocks, 'zl', 0, 0, tiled=True)  17.7 us
    all_to_all x2, waiting for transfers between devices, over_y(): return lax.all_to_all(blocks, 'y', 0, 0, tiled=True)  15.6 us
    pallas_call x2, Pallas kernels, products(): pl.pallas_call(products_kernel, grid_spec=pltpu.PrefetchScalarGridSpec(nu...  13.5 us
    all_to_all x2, starting transfers between devices, over_y(): return lax.all_to_all(blocks, 'y', 0, 0, tiled=True)  13.4 us
    unnamed x46, local copies, waits for them, and re-layouts  10.6 us
  transfers between devices with their start and end apart: 10, of which 4 were waited for; matrix products, arithmetic and copies ran while one was open for 3% of the time, Pallas kernels for 14%

profile of v2, /device:TPU:64, one launch (start us, length us, event | category | flops | bytes accessed | tf_op | source)
XLA Modules:
  0.0 224.2 jit_solution(1572603218892059969)
XLA Ops:
  4.1 2.7 %gather_fusion = bf16[768,256]{1,0:T(8,128)(2,1)S(1)} fusion(bf16[3072,256]{1,0:T(8,128)(2,1)S(1)} %bitcast.22, s32[1024]{0:T(1024)S(1)} %pad_clamp_fusion), kind=kCustom, calls=%fused_computation | custom fusion | bytes 789504 | tf_op jit(solution)/shard_map/gather | solution.py:252
  7.0 54.2 %conditional.1 = (bf16[4,768,256]{2,1,0:T(8,128)(2,1)S(1)}, bf16[4,768,256]{2,1,0:T(8,128)(2,1)}, bf16[4,768,256]{2,1,0:T(8,128)(2,1)}) conditional(s32[]{:T(128)} %clamp.3, bf16[768,256]{1,0:T(8,128)(2,1)S(1)} %broadcast_select_fusion, bf16[768,256]{1,0:T(8,128)(2,1)S(1)} %broadcast_select_fusion, ...), branch_computations={%region_1.2_spmd, %region_2.3_spmd, %region_3.4_spmd, %region_4.5_... | conditional | bytes 15827050 | solution.py:257
  7.1 24.9 %all_to_all.43 = bf16[4,768,256]{2,1,0:T(8,128)(2,1)} all-to-all(bf16[4,768,256]{2,1,0:T(8,128)(2,1)S(1)} %broadcast_in_dim.47), channel_id=1, replica_groups=mesh['zl'=8,'y'=4,'zh'=2,'x'=4,'core'=2] {'x'}, dimensions={0} | all-to-all | bytes 3145728 | tf_op jit(solution)/shard_map/cond/branch_2_fun/all_to_all | solution.py:31
  32.0 1.9 collective-permute-start.5
  34.0 13.9 %collective-permute-start.4 = (bf16[576,256]{1,0:T(8,128)(2,1)S(1)}, bf16[576,256]{1,0:T(8,128)(2,1)S(1)}, u32[]{:S(2)}, u32[]{:S(2)}) collective-permute-start(bf16[576,256]{1,0:T(8,128)(2,1)S(1)} %slice.98), channel_id=1, source_target_pairs={{0,8},{8,0},{1,9},{9,1},{2,10},{10,2},{3,11},{11,3},{4,12},{12,4},... | collective-permute-start | bytes 884744 | tf_op jit(solution)/shard_map/cond/branch_2_fun/ppermute | solution.py:27
  47.9 13.1 %collective-permute-done.4 = bf16[576,256]{1,0:T(8,128)(2,1)S(1)} collective-permute-done((bf16[576,256]{1,0:T(8,128)(2,1)S(1)}, bf16[576,256]{1,0:T(8,128)(2,1)S(1)}, u32[]{:S(2)}, u32[]{:S(2)}) %collective-permute-start.4) | collective-permute-done | bytes 294944 | tf_op jit(solution)/shard_map/cond/branch_2_fun/ppermute | solution.py:27
  61.2 23.3 %all_to_all.45.near_ref = bf16[4,768,256]{2,1,0:T(8,128)(2,1)S(1)} all-to-all(bf16[4,768,256]{2,1,0:T(8,128)(2,1)S(1)} %get-tuple-element.24), channel_id=1, replica_groups=mesh['zl'=8,'y'=4,'zh'=2,'x'=4,'core'=2] {'x'}, dimensions={0} | all-to-all | bytes 3145728 | tf_op jit(solution)/shard_map/all_to_all | solution.py:31
  84.5 1.9 collective-permute-start.8
  94.2 5.2 %shard_map.119 = (bf16[768,256]{1,0:T(8,128)(2,1)S(1)}, bf16[768,256]{1,0:T(8,128)(2,1)S(1)}, f32[768,2]{1,0:T(8,128)S(1)}) custom-call(s32[2]{0:T(128)S(1)} %pad_add_fusion.info_ref, bf16[768,256]{1,0:T(8,128)(2,1)S(1)} %bitcast.28, bf16[768,256]{1,0:T(8,128)(2,1)S(1)} %bitcast.30, bf16[768,256]{1,0:T(8,128)(2,1)S(1)} %bitcast.32, s32[768,1]{1,0:T(8,128)S(1)} %copy-done.7, ...), custom_call_target="tpu_custom_call" | custom-call | flops 604000000 | bytes 2000000 | tf_op jit(solution)/shard_map/pallas_call | solution.py:131
  99.5 6.7 %shard_map.120 = (f32[768,256]{1,0:T(8,128)S(1)}, bf16[4,4,128,256]{3,2,1,0:T(8,128)(2,1)S(1)}) custom-call(s32[2]{0:T(128)S(1)} %pad_add_fusion.2.info_ref, bf16[4,768,256]{2,1,0:T(8,128)(2,1)} %get-tuple-element.26.near_ref, bf16[4,768,256]{2,1,0:T(8,128)(2,1)} %get-tuple-element.27.far_ref, bf16[16,256,256]{2,1,0:T(8,128)(2,1)S(1)} %bitcast.23, ...), custom_call_target="tpu_custom_call" | custom-call | flops 1610000000 | bytes 7000000 | tf_op jit(solution)/shard_map/pallas_call | solution.py:191
  108.1 8.8 %all-to-all-start.7 = ((bf16[4,4,128,256]{3,2,1,0:T(8,128)(2,1)}), bf16[4,4,128,256]{3,2,1,0:T(8,128)(2,1)}, u32[]{:S(2)}, u32[]{:S(2)}) async-start(bf16[4,4,128,256]{3,2,1,0:T(8,128)(2,1)} %copy-done.4), calls=%async_computation.7 | async-start | bytes 2097152 | tf_op jit(solution)/shard_map/all_to_all | solution.py:231
  117.0 1.6 copy-done.2
  119.7 6.8 %shard_map.121 = (f32[768,256]{1,0:T(8,128)S(1)}, bf16[4,4,128,256]{3,2,1,0:T(8,128)(2,1)S(1)}) custom-call(s32[2]{0:T(128)S(1)} %pad_add_fusion.1.info_ref, bf16[4,768,256]{2,1,0:T(8,128)(2,1)S(1)} %all_to_all.45.near_ref, bf16[4,768,256]{2,1,0:T(8,128)(2,1)} %collective-permute-done.8.far_ref, bf16[16,256,256]{2,1,0:T(8,128)(2,1)S(1)} %bitcast.25, ...), custom_call_target="tpu_custom_call" | custom-call | flops 1610000000 | bytes 7000000 | tf_op jit(solution)/shard_map/pallas_call | solution.py:191
  127.6 7.8 %shard_map.122 = (bf16[768,256]{1,0:T(8,128)(2,1)}, bf16[768,256]{1,0:T(8,128)(2,1)S(1)}, f32[768,1]{1,0:T(8,128)S(1)}) custom-call(s32[2]{0:T(128)S(1)} %pad_add_fusion.info_ref, bf16[768,256]{1,0:T(8,128)(2,1)S(1)} %bitcast.29, bf16[768,256]{1,0:T(8,128)(2,1)S(1)} %bitcast.31, bf16[768,256]{1,0:T(8,128)(2,1)S(1)} %bitcast.33, s32[768,1]{1,0:T(8,128)S(1)} %copy-done.8, ...), custom_call_target="tpu_custom_call" | custom-call | flops 1510000000 | bytes 4000000 | tf_op jit(solution)/shard_map/pallas_call | solution.py:146
  135.7 2.1 collective-permute-start.9
  137.8 4.6 %all-to-all-start.6 = ((bf16[4,4,128,256]{3,2,1,0:T(8,128)(2,1)}), bf16[4,4,128,256]{3,2,1,0:T(8,128)(2,1)S(1)}, u32[]{:S(2)}, u32[]{:S(2)}) async-start(bf16[4,4,128,256]{3,2,1,0:T(8,128)(2,1)} %copy-done.3), calls=%async_computation.6 | async-start | bytes 2097152 | tf_op jit(solution)/shard_map/all_to_all | solution.py:231
  142.6 15.6 %all-to-all-done.6.moved_ref = bf16[4,4,128,256]{3,2,1,0:T(8,128)(2,1)S(1)} async-done(((bf16[4,4,128,256]{3,2,1,0:T(8,128)(2,1)}), bf16[4,4,128,256]{3,2,1,0:T(8,128)(2,1)S(1)}, u32[]{:S(2)}, u32[]{:S(2)}) %all-to-all-start.6) | async-done | bytes 1048608 | tf_op jit(solution)/shard_map/all_to_all | solution.py:231
  159.1 3.5 %all-to-all-start.5 = ((bf16[4,400,256]{2,1,0:T(8,128)(2,1)}), bf16[4,400,256]{2,1,0:T(8,128)(2,1)S(1)}, u32[]{:S(2)}, u32[]{:S(2)}) async-start(bf16[4,400,256]{2,1,0:T(8,128)(2,1)} %broadcast_in_dim.78), calls=%async_computation.5 | async-start | bytes 1638400 | tf_op jit(solution)/shard_map/all_to_all | solution.py:31
  162.6 3.2 %shard_map.123.refs_0_ = bf16[8,128,256]{2,1,0:T(8,128)(2,1)} custom-call(s32[1]{0:T(128)} %bitcast.11.info_ref, bf16[4,4,128,256]{3,2,1,0:T(8,128)(2,1)} %all-to-all-done.7.moved_ref), custom_call_target="tpu_custom_call" | custom-call | flops 4000000 | bytes 3000000 | tf_op jit(solution)/shard_map/pallas_call | solution.py:214
  167.3 7.8 %all-to-all-done.5 = bf16[4,400,256]{2,1,0:T(8,128)(2,1)S(1)} async-done(((bf16[4,400,256]{2,1,0:T(8,128)(2,1)}), bf16[4,400,256]{2,1,0:T(8,128)(2,1)S(1)}, u32[]{:S(2)}, u32[]{:S(2)}) %all-to-all-start.5) | async-done | bytes 819232 | tf_op jit(solution)/shard_map/all_to_all | solution.py:31
  175.1 17.7 %all-to-all-start.8 = ((bf16[8,128,256]{2,1,0:T(8,128)(2,1)}), bf16[8,128,256]{2,1,0:T(8,128)(2,1)S(1)}, u32[]{:S(2)}, u32[]{:S(2)}) async-start(bf16[8,128,256]{2,1,0:T(8,128)(2,1)} %shard_map.124), calls=%async_computation.8 | async-start | bytes 1048576 | tf_op jit(solution)/shard_map/all_to_all | solution.py:286
  193.9 1.9 collective-permute-start.10
  195.8 9.6 %collective-permute-start.11 = (f32[768]{0:T(1024)S(1)}, f32[768]{0:T(1024)S(1)}, u32[]{:S(2)}, u32[]{:S(2)}) collective-permute-start(f32[768]{0:T(1024)S(1)} %reshape.133), channel_id=1, source_target_pairs={{0,8},{8,0},{1,9},{9,1},{2,10},{10,2},{3,11},{11,3},{4,12},{12,4},... | collective-permute-start | bytes 9224 | tf_op jit(solution)/shard_map/ppermute | solution.py:27
  205.5 15.1 %collective-permute-done.11 = f32[768]{0:T(1024)S(1)} collective-permute-done((f32[768]{0:T(1024)S(1)}, f32[768]{0:T(1024)S(1)}, u32[]{:S(2)}, u32[]{:S(2)}) %collective-permute-start.11) | collective-permute-done | bytes 3104 | tf_op jit(solution)/shard_map/ppermute | solution.py:27
  (91 shorter events, 22.6 us)
Async XLA Ops:
  0.6 3.5 %copy-start = (bf16[1,3072,256]{2,1,0:T(8,128)(2,1)S(1)}, bf16[1,3072,256]{2,1,0:T(8,128)(2,1)}, u32[]{:S(2)}) copy-start(bf16[1,3072,256]{2,1,0:T(8,128)(2,1)} %param.12) | copy-start | bytes 4718596
  32.0 29.0 %collective-permute-start.5 = (bf16[4,768,256]{2,1,0:T(8,128)(2,1)}, bf16[4,768,256]{2,1,0:T(8,128)(2,1)}, u32[]{:S(2)}, u32[]{:S(2)}) collective-permute-start(bf16[4,768,256]{2,1,0:T(8,128)(2,1)} %all_to_all.43), channel_id=1, source_target_pairs={{0,1},{1,0},{2,3},{3,2},{4,5},{5,4},{6,7},{7,6},{8,9},{9,8},{10,11... | collective-permute-start | bytes 4718600 | tf_op jit(solution)/shard_map/cond/branch_2_fun/ppermute | solution.py:27
  34.0 27.0 %collective-permute-start.4 = (bf16[576,256]{1,0:T(8,128)(2,1)S(1)}, bf16[576,256]{1,0:T(8,128)(2,1)S(1)}, u32[]{:S(2)}, u32[]{:S(2)}) collective-permute-start(bf16[576,256]{1,0:T(8,128)(2,1)S(1)} %slice.98), channel_id=1, source_target_pairs={{0,8},{8,0},{1,9},{9,1},{2,10},{10,2},{3,11},{11,3},{4,12},{12,4},... | collective-permute-start | bytes 884744 | tf_op jit(solution)/shard_map/cond/branch_2_fun/ppermute | solution.py:27
  61.2 25.3 %copy-start.11 = (s32[1,768]{1,0:T(1,128)S(1)}, s32[1,768]{1,0:T(1,128)}, u32[]{:S(2)}) copy-start(s32[1,768]{1,0:T(1,128)} %row_ref.3) | copy-start | bytes 9220
  61.2 26.2 %copy-start.22 = (f32[1,768]{1,0:T(1,128)S(1)}, f32[1,768]{1,0:T(1,128)}, u32[]{:S(2)}) copy-start(f32[1,768]{1,0:T(1,128)} %param.15) | copy-start | bytes 9220
  84.5 32.5 %collective-permute-start.8 = (bf16[4,768,256]{2,1,0:T(8,128)(2,1)S(1)}, bf16[4,768,256]{2,1,0:T(8,128)(2,1)}, u32[]{:S(2)}, u32[]{:S(2)}) collective-permute-start(bf16[4,768,256]{2,1,0:T(8,128)(2,1)S(1)} %all_to_all.45.near_ref), channel_id=1, source_target_pairs={{0,1},{1,0},{2,3},{3,2},{4,5},{5,4},{6,7},{7,6},{8,9},{9,8},{10,11... | collective-permute-start | bytes 4718600 | tf_op jit(solution)/shard_map/ppermute | solution.py:27
  88.3 11.2 %copy-start.1 = (bf16[4096,256]{1,0:T(8,128)(2,1)S(1)}, bf16[4096,256]{1,0:T(8,128)(2,1)}, u32[]{:S(2)}) copy-start(bf16[4096,256]{1,0:T(8,128)(2,1)} %param.19) | copy-start | bytes 6291460
  99.4 6.8 %copy-start.18 = (bf16[768,256]{1,0:T(8,128)(2,1)}, bf16[768,256]{1,0:T(8,128)(2,1)S(1)}, u32[]{:S(2)}) copy-start(bf16[768,256]{1,0:T(8,128)(2,1)S(1)} %get-tuple-element.23.att_ref) | copy-start | bytes 1179652
  99.4 6.8 %copy-start.20 = (f32[768,2]{1,0:T(8,128)}, f32[768,2]{1,0:T(8,128)S(1)}, u32[]{:S(2)}) copy-start(f32[768,2]{1,0:T(8,128)S(1)} %get-tuple-element.22.lse_ref) | copy-start | bytes 18436
  108.1 29.7 %all-to-all-start.7 = ((bf16[4,4,128,256]{3,2,1,0:T(8,128)(2,1)}), bf16[4,4,128,256]{3,2,1,0:T(8,128)(2,1)}, u32[]{:S(2)}, u32[]{:S(2)}) async-start(bf16[4,4,128,256]{3,2,1,0:T(8,128)(2,1)} %copy-done.4), calls=%async_computation.7 | async-start | bytes 2097152 | tf_op jit(solution)/shard_map/all_to_all | solution.py:231
  117.0 1.6 copy-start.2
  119.7 7.8 %copy-start.8 = (s32[768,1]{1,0:T(8,128)S(1)}, s32[768,1]{1,0:T(8,128)}, u32[]{:S(2)}) copy-start(s32[768,1]{1,0:T(8,128)} %copy.16.col_ref) | copy-start | bytes 9220
  119.7 7.8 %copy-start.10 = (f32[768,1]{1,0:T(8,128)S(1)}, f32[768,1]{1,0:T(8,128)}, u32[]{:S(2)}) copy-start(f32[768,1]{1,0:T(8,128)} %copy.17.logit_ref) | copy-start | bytes 9220
  119.7 7.8 %copy-start.13 = (bf16[1,768,256]{2,1,0:T(8,128)(2,1)S(1)}, bf16[1,768,256]{2,1,0:T(8,128)(2,1)}, u32[]{:S(2)}) copy-start(bf16[1,768,256]{2,1,0:T(8,128)(2,1)} %param.16) | copy-start | bytes 1179652
  119.7 7.8 %copy-start.15 = (bf16[1,768,256]{2,1,0:T(8,128)(2,1)S(1)}, bf16[1,768,256]{2,1,0:T(8,128)(2,1)}, u32[]{:S(2)}) copy-start(bf16[1,768,256]{2,1,0:T(8,128)(2,1)} %param.17) | copy-start | bytes 1179652
  119.7 7.9 %copy-start.17 = (bf16[1,768,256]{2,1,0:T(8,128)(2,1)S(1)}, bf16[1,768,256]{2,1,0:T(8,128)(2,1)}, u32[]{:S(2)}) copy-start(bf16[1,768,256]{2,1,0:T(8,128)(2,1)} %param.18) | copy-start | bytes 1179652
  119.7 7.8 %copy-start.19 = (bf16[768,256]{1,0:T(8,128)(2,1)S(1)}, bf16[768,256]{1,0:T(8,128)(2,1)}, u32[]{:S(2)}) copy-start(bf16[768,256]{1,0:T(8,128)(2,1)} %copy-done.18) | copy-start | bytes 1179652
  119.7 7.8 %copy-start.21 = (f32[768,2]{1,0:T(8,128)S(1)}, f32[768,2]{1,0:T(8,128)}, u32[]{:S(2)}) copy-start(f32[768,2]{1,0:T(8,128)} %copy-done.20) | copy-start | bytes 18436
  135.7 6.7 %collective-permute-start.9 = (bf16[400,256]{1,0:T(8,128)(2,1)S(1)}, bf16[400,256]{1,0:T(8,128)(2,1)S(1)}, u32[]{:S(2)}, u32[]{:S(2)}) collective-permute-start(bf16[400,256]{1,0:T(8,128)(2,1)S(1)} %pad_maximum_fusion.1), channel_id=1, source_target_pairs={{0,1},{1,0},{2,3},{3,2},{4,5},{5,4},{6,7},{7,6},{8,9},{9,8},{10,11... | collective-permute-start | bytes 614408 | tf_op jit(solution)/shard_map/ppermute | solution.py:27
  137.8 20.4 %all-to-all-start.6 = ((bf16[4,4,128,256]{3,2,1,0:T(8,128)(2,1)}), bf16[4,4,128,256]{3,2,1,0:T(8,128)(2,1)S(1)}, u32[]{:S(2)}, u32[]{:S(2)}) async-start(bf16[4,4,128,256]{3,2,1,0:T(8,128)(2,1)} %copy-done.3), calls=%async_computation.6 | async-start | bytes 2097152 | tf_op jit(solution)/shard_map/all_to_all | solution.py:231
  159.1 15.9 %all-to-all-start.5 = ((bf16[4,400,256]{2,1,0:T(8,128)(2,1)}), bf16[4,400,256]{2,1,0:T(8,128)(2,1)S(1)}, u32[]{:S(2)}, u32[]{:S(2)}) async-start(bf16[4,400,256]{2,1,0:T(8,128)(2,1)} %broadcast_in_dim.78), calls=%async_computation.5 | async-start | bytes 1638400 | tf_op jit(solution)/shard_map/all_to_all | solution.py:31
  175.1 48.5 %all-to-all-start.8 = ((bf16[8,128,256]{2,1,0:T(8,128)(2,1)}), bf16[8,128,256]{2,1,0:T(8,128)(2,1)S(1)}, u32[]{:S(2)}, u32[]{:S(2)}) async-start(bf16[8,128,256]{2,1,0:T(8,128)(2,1)} %shard_map.124), calls=%async_computation.8 | async-start | bytes 1048576 | tf_op jit(solution)/shard_map/all_to_all | solution.py:286
  193.9 27.4 %collective-permute-start.10 = (bf16[384,512]{1,0:T(8,128)(2,1)}, bf16[384,512]{1,0:T(8,128)(2,1)}, u32[]{:S(2)}, u32[]{:S(2)}) collective-permute-start(bf16[384,512]{1,0:T(8,128)(2,1)} %pad_maximum_fusion), channel_id=1, source_target_pairs={{0,1},{1,0},{2,3},{3,2},{4,5},{5,4},{6,7},{7,6},{8,9},{9,8},{10,11... | collective-permute-start | bytes 1179656 | tf_op jit(solution)/shard_map/ppermute | solution.py:27
  195.8 24.8 %collective-permute-start.11 = (f32[768]{0:T(1024)S(1)}, f32[768]{0:T(1024)S(1)}, u32[]{:S(2)}, u32[]{:S(2)}) collective-permute-start(f32[768]{0:T(1024)S(1)} %reshape.133), channel_id=1, source_target_pairs={{0,8},{8,0},{1,9},{9,1},{2,10},{10,2},{3,11},{11,3},{4,12},{12,4},... | collective-permute-start | bytes 9224 | tf_op jit(solution)/shard_map/ppermute | solution.py:27
  (9 other events, 9.0 us)

commit v3 on v2

--- a/solution.py
+++ b/solution.py
@@ -9,14 +9,14 @@
 from jax.sharding import PartitionSpec as P
 
 HEAD_SIZE = 128
-ZL, Y, ZH, X, CORE = 8, 4, 2, 4, 2
+ZQ, ZP, Y, ZH, X, CORE = 4, 2, 4, 2, 4, 2
 SLOTS, WIDE, HEADS = 768, 256, 2
 SCALE = HEAD_SIZE ** (-0.5)
 BF, F32 = jnp.bfloat16, jnp.float32
 ROWS = 256
-STEP = 192
+STEP = 64
 EXTRA = 16
-LIMIT = pltpu.CompilerParams(vmem_limit_bytes=40 * 1024 * 1024)
+LIMIT = pltpu.CompilerParams(vmem_limit_bytes=60 * 1024 * 1024)
 
 
 def ring(n, k):
@@ -35,12 +35,11 @@
     return jnp.broadcast_to(block[None], (X,) + block.shape)
 
 
-def exchange(rows, picked):
-    other = swap(picked[:rows], "zh")
-    near = spread_x(repeated(picked))
-    far = swap(near, "core")
+def exchange(rows, copies):
+    other = swap(copies[0, :rows], "zh")
+    near = spread_x(copies)
     other = jnp.pad(other, ((0, SLOTS - rows), (0, 0)))
-    return repeated(other), near, far
+    return repeated(other), near
 
 
 def transposed_dot(a, b):
@@ -72,7 +71,7 @@
         p = (e * (1.0 / total)).astype(BF)
         att = jnp.dot(p, v_ref[...], preferred_element_type=F32).astype(BF)
         att_ref[:, lanes] = att
-        scaled_ref[:, lanes] = (weight * att.astype(F32)).astype(BF)
+        scaled_ref[lanes, :] = (weight * att.astype(F32)).astype(BF).T
         lse_ref[:, h : h + 1] = top + jnp.log(total)
 
 
@@ -134,9 +133,9 @@
             num_scalar_prefetch=1,
             grid=(SLOTS // ROWS,),
             in_specs=[by_rows(WIDE), by_group(), by_group(), by_rows(1), whole((1, SLOTS)), by_rows(1)],
-            out_specs=[by_rows(WIDE), by_rows(WIDE), by_rows(HEADS)],
-        ),
-        out_shape=[shape_of((SLOTS, WIDE), BF), shape_of((SLOTS, WIDE), BF), shape_of((SLOTS, HEADS), F32)],
+            out_specs=[by_rows(WIDE), pl.BlockSpec((WIDE, ROWS), lambda i, info: (0, i)), by_rows(HEADS)],
+        ),
+        out_shape=[shape_of((SLOTS, WIDE), BF), shape_of((WIDE, SLOTS), BF), shape_of((SLOTS, HEADS), F32)],
         compiler_params=LIMIT,
         cost_estimate=pl.CostEstimate(flops=604 * 10**6, bytes_accessed=2 * 10**6, transcendentals=1200000),
     )(info, q, k, v, pos_col, pos_row, logit_col)
@@ -161,48 +160,54 @@
     )(info, q, k, v, pos_col, pos_row, logit_col, lse, att, grad_o)
 
 
-def products_kernel(info_ref, near_ref, far_ref, wn_ref, wf_ref, scaled_ref, *refs):
+def products_kernel(info_ref, shard_ref, w_ref, scaled_ref, *refs):
     go_ref, wg_ref = refs[-2:]
-    core = info_ref[0]
-    near, far, scaled = near_ref[0], far_ref[0], scaled_ref[...]
-    part = jnp.dot(near, wn_ref[0], preferred_element_type=F32)
-    part = part + jnp.dot(far, wf_ref[0], preferred_element_type=F32)
+    shard = shard_ref[0]
+    part = jnp.dot(shard, w_ref[0], preferred_element_type=F32)
     first = pl.program_id(0) == 0
 
     @pl.when(first)
     def _():
-        go_ref[...] = part + refs[0][...] if len(refs) == 3 else part
+        go_ref[...] = part + refs[0][...] if len(refs) > 2 else part
 
     @pl.when(jnp.logical_not(first))
     def _():
         go_ref[...] += part
 
-    wg_ref[pl.ds(2 * core, 2), 0] = transposed_dot(near, scaled).astype(BF).reshape(2, 128, WIDE)
-    wg_ref[pl.ds(2 - 2 * core, 2), 0] = transposed_dot(far, scaled).astype(BF).reshape(2, 128, WIDE)
-
-
-def products(core, half, near, far, w_out, scaled, begin=None):
+    grad = jnp.dot(scaled_ref[...], shard, preferred_element_type=F32).astype(BF)
+    wg_ref[0, 0, 0] = grad[:, :128]
+    wg_ref[0, 1, 0] = grad[:, 128:]
+
+
+def products(core, half, shards, w_out, scaled_t, grad_o=None, blocks=None):
     info = jnp.stack([core, half]).astype(jnp.int32)
-    shard = pl.BlockSpec((1, SLOTS, WIDE), lambda i, info: (i, 0, 0))
-    w_near = pl.BlockSpec((1, WIDE, WIDE), lambda i, info: (info[1] * 8 + i * 2 + info[0], 0, 0))
-    w_far = pl.BlockSpec((1, WIDE, WIDE), lambda i, info: (info[1] * 8 + i * 2 + 1 - info[0], 0, 0))
-    w_parts = w_out.reshape(ZH * X * CORE, WIDE, WIDE)
-    more = [] if begin is None else [begin]
+    more, more_specs, aliases = [], [], {}
+    if grad_o is not None:
+        more, more_specs = [grad_o], [whole((SLOTS, WIDE))]
+    if blocks is not None:
+        aliases = {4 + len(more): 1}
+        more, more_specs = more + [blocks], more_specs + [pl.BlockSpec(memory_space=pl.ANY)]
     return pl.pallas_call(
         products_kernel,
         grid_spec=pltpu.PrefetchScalarGridSpec(
             num_scalar_prefetch=1,
             grid=(X,),
-            in_specs=[shard, shard, w_near, w_far, whole((SLOTS, WIDE))] + [whole((SLOTS, WIDE)) for _ in more],
+            in_specs=[
+                pl.BlockSpec((1, SLOTS, WIDE), lambda i, info: (i, 0, 0)),
+                pl.BlockSpec((1, WIDE, WIDE), lambda i, info: (info[1] * 8 + i * 2 + info[0], 0, 0)),
+                whole((WIDE, SLOTS)),
+            ]
+            + more_specs,
             out_specs=[
                 whole((SLOTS, WIDE)),
-                pl.BlockSpec((Y, 1, 128, WIDE), lambda i, info: (0, i, 0, 0)),
+                pl.BlockSpec((1, 2, 1, WIDE, 128), lambda i, info: (i % 2, info[0], i // 2, 0, 0)),
             ],
         ),
-        out_shape=[shape_of((SLOTS, WIDE), F32), shape_of((Y, X, 128, WIDE), BF)],
-        compiler_params=LIMIT,
-        cost_estimate=pl.CostEstimate(flops=1610 * 10**6, bytes_accessed=7 * 10**6, transcendentals=0),
-    )(info, near, far, w_parts, w_parts, scaled, *more)
+        out_shape=[shape_of((SLOTS, WIDE), F32), shape_of((ZP, Y, 2, WIDE, 128), BF)],
+        input_output_aliases=aliases,
+        compiler_params=LIMIT,
+        cost_estimate=pl.CostEstimate(flops=805 * 10**6, bytes_accessed=4 * 10**6, transcendentals=0),
+    )(info, shards, w_out.reshape(ZH * X * CORE, WIDE, WIDE), scaled_t, *more)
 
 
 def fold_kernel(info_ref, moved_ref, *refs):
@@ -215,20 +220,66 @@
         fold_kernel,
         grid_spec=pltpu.PrefetchScalarGridSpec(
             num_scalar_prefetch=1,
-            grid=(X,),
-            in_specs=[pl.BlockSpec((Y, 1, 128, WIDE), lambda i, info: (0, i, 0, 0))]
+            grid=(2,),
+            in_specs=[pl.BlockSpec((ZP * Y, 1, WIDE, 128), lambda i, info: (0, i, 0, 0))]
             + [pl.BlockSpec(memory_space=pl.ANY) for _ in more],
-            out_specs=pl.BlockSpec((1, 128, WIDE), lambda i, info: (info[0] * 4 + i, 0, 0)),
-        ),
-        out_shape=shape_of((ZL, 128, WIDE), BF),
+            out_specs=pl.BlockSpec((1, WIDE, 128), lambda i, info: (info[0] * 2 + i, 0, 0)),
+        ),
+        out_shape=shape_of((ZQ, WIDE, 128), BF),
         input_output_aliases={2: 0} if more else {},
         compiler_params=LIMIT,
-        cost_estimate=pl.CostEstimate(flops=4 * 10**6, bytes_accessed=3 * 10**6, transcendentals=0),
+        cost_estimate=pl.CostEstimate(flops=1 * 10**6, bytes_accessed=2 * 10**6, transcendentals=0),
     )(half.astype(jnp.int32).reshape(1), moved, *more)
 
 
-def over_y(blocks):
-    return lax.all_to_all(blocks, "y", 0, 0, tiled=True)
+def over_zp_y(blocks):
+    blocks = blocks.reshape(ZP * Y, 2, WIDE, 128)
+    return lax.all_to_all(blocks, ("zp", "y"), 0, 0, tiled=True)
+
+
+PICK = 512
+
+
+def pick_kernel(row_ref, cot_ref, out_ref, col_ref, sum_ref):
+    step = pl.program_id(0)
+
+    @pl.when(step == 0)
+    def _():
+        sum_ref[...] = jnp.zeros_like(sum_ref)
+        for a in range(SLOTS // 128):
+            lanes = slice(a * 128, (a + 1) * 128)
+            col_ref[lanes, :] = jnp.broadcast_to(row_ref[:, lanes], (128, 128)).T
+
+    lane = lax.broadcasted_iota(jnp.int32, (SLOTS, 128), 1).astype(F32)
+    total = sum_ref[...]
+    for b in range(PICK // 128):
+        token = lane + (step * PICK + b * 128).astype(F32)
+        hot = jnp.where(col_ref[...] == token, 1.0, 0.0).astype(BF)
+        total = total + jnp.dot(hot, cot_ref[b * 128 : (b + 1) * 128, :], preferred_element_type=F32)
+    sum_ref[...] = total
+
+    @pl.when(step == pl.num_programs(0) - 1)
+    def _():
+        rows = total.astype(BF)
+        for a in range(X):
+            out_ref[a] = rows
+
+
+def pick(cotangent, live_positions):
+    tokens = cotangent.shape[0]
+    return pl.pallas_call(
+        pick_kernel,
+        grid=(tokens // PICK,),
+        in_specs=[
+            pl.BlockSpec((1, SLOTS), lambda i: (0, 0)),
+            pl.BlockSpec((PICK, WIDE), lambda i: (i, 0)),
+        ],
+        out_specs=pl.BlockSpec((X, SLOTS, WIDE), lambda i: (0, 0, 0)),
+        out_shape=shape_of((X, SLOTS, WIDE), BF),
+        scratch_shapes=[pltpu.VMEM((SLOTS, 128), F32), pltpu.VMEM((SLOTS, WIDE), F32)],
+        compiler_params=LIMIT,
+        cost_estimate=pl.CostEstimate(flops=1208 * 10**6, bytes_accessed=3 * 10**6, transcendentals=0),
+    )(live_positions.astype(F32), cotangent)
 
 
 def packed(router):
@@ -244,35 +295,44 @@
 
 def per_device(cotangent, routed, counts, logits, query_rows, key_rows, routed_value_rows, w_out):
     zh, x, core = lax.axis_index("zh"), lax.axis_index("x"), lax.axis_index("core")
-    dp_index = lax.axis_index("zl") * Y + lax.axis_index("y")
+    dp_index = (lax.axis_index("zq") * ZP + lax.axis_index("zp")) * Y + lax.axis_index("y")
     own = jnp.arange(counts.shape[0], dtype=jnp.int32) == dp_index
     own_count = jnp.sum(jnp.where(own, counts, 0))
-    live_rows = jnp.arange(SLOTS, dtype=jnp.int32) < own_count
     positions = routed[0]
-    picked = cotangent[0].at[positions].get(mode="promise_in_bounds")
-    picked = jnp.where(live_rows[:, None], picked, jnp.zeros((), BF))
+    live = jnp.arange(SLOTS, dtype=jnp.int32) < own_count
+    copies = pick(cotangent[0], jnp.where(live, positions, -1)[None, :])
 
     sizes = range(STEP, SLOTS + 1, STEP)
     branch = jnp.maximum(own_count - 1, 0) // STEP
-    other_copies, own_near, own_far = lax.switch(
-        branch, [functools.partial(exchange, rows) for rows in sizes], picked
+    other_copies, own_near = lax.switch(
+        branch, [functools.partial(exchange, rows) for rows in sizes], copies
     )
     other_near = spread_x(other_copies)
+    own_far = swap(own_near, "core")
 
     info = jnp.stack([x // 2, own_count]).astype(jnp.int32)
     attention = (
         info, query_rows[0], key_rows[0], routed_value_rows[0],
         positions[:, None], positions[None, :], logits[0][:, None],
     )
-    attended, scaled, lse = forward(*attention)
-    grad_o_own, w_grad_own = products(core, zh, own_near, own_far, w_out, scaled)
-    blocks = fold(zh, over_y(w_grad_own))
-
+    attended, scaled_t, lse = forward(*attention)
+    begun, w_grad_own = products(core, zh, own_near, w_out, scaled_t)
+    begun, w_grad_own = products(1 - core, zh, own_far, w_out, scaled_t, begun, w_grad_own)
+
+    other_near, begun, w_grad_own = lax.optimization_barrier((other_near, begun, w_grad_own))
     other_far = swap(other_near, "core")
-    grad_o, w_grad_other = products(core, 1 - zh, other_near, other_far, w_out, scaled, grad_o_own)
-    moved_other = over_y(w_grad_other)
+    moved_own = over_zp_y(w_grad_own)
+    begun, w_grad_other = products(core, 1 - zh, other_near, w_out, scaled_t, begun)
+    grad_o, w_grad_other = products(1 - core, 1 - zh, other_far, w_out, scaled_t, begun, w_grad_other)
+    moved_other = over_zp_y(w_grad_other)
 
     grad_q, kv, router = backward(*attention, lse, attended, grad_o)
+    moved_other, _ = lax.optimization_barrier((moved_other, kv))
+    blocks = fold(zh, moved_own)
+    blocks = fold(1 - zh, moved_other, blocks)
+    final = lax.all_to_all(blocks, "zq", 0, 0, tiled=True)
+    w_grad = jnp.sum(final.astype(F32), axis=0).T.astype(BF)
+
     router = router[:, 0]
     half = SLOTS // 2
     kept = lax.dynamic_slice_in_dim(kv, core * half, half, 0)
@@ -281,10 +341,6 @@
     chip = (kept.astype(F32) + came[:half].astype(F32)).astype(BF)
     router = router + unpacked(came[half:])
     pieces = spread_x(repeated(jnp.concatenate([chip, packed(router)], 0)))
-
-    blocks = fold(1 - zh, moved_other, blocks)
-    final = lax.all_to_all(blocks, "zl", 0, 0, tiled=True)
-    w_grad = jnp.sum(final.astype(F32), axis=0).astype(BF)
 
     wide = pieces[:, :half].astype(F32)
     first, second = wide[0] + wide[1], wide[2] + wide[3]
@@ -304,8 +360,8 @@
 
 
 def solution(mesh):
-    fine = Mesh(mesh.devices.reshape(ZL, Y, ZH, X, CORE), ("zl", "y", "zh", "x", "core"))
-    dp, col = ("zl", "y"), ("x", "core")
+    fine = Mesh(mesh.devices.reshape(ZQ, ZP, Y, ZH, X, CORE), ("zq", "zp", "y", "zh", "x", "core"))
+    dp, col = ("zq", "zp", "y"), ("x", "core")
     row_col = ("zh",) + col
     placed = (
         P(dp, None, row_col),

time: 225 us -> 206 us (0.916)
  the two profiles are of different devices: /device:TPU:64 before, /device:TPU:8 now
where the time goes in v3:
time: 206 us; the launch traced here: 204 us
  starting transfers between devices  56.6 us (27%)
  Pallas kernels  52.5 us (25%)
  blocking collectives  44.9 us (22%)
  waiting for transfers between devices  28.9 us (14%)
  local copies, waits for them, and re-layouts  10.8 us (5%)
  other arithmetic  9.09 us (4%)
    ppermute x6, starting transfers between devices, swap(): return lax.ppermute(value, axis, ring(2, 1))  36.2 us
    all_to_all x1, blocking collectives, over_zp_y(): return lax.all_to_all(blocks, ('zp', 'y'), 0, 0, tiled=True)  27 us
    pallas_call x4, Pallas kernels, products(): pl.pallas_call(products_kernel, grid_spec=pltpu.PrefetchScalarGridSpec(nu...  25 us
    all_to_all x1, blocking collectives, spread_x(): return lax.all_to_all(copies, 'x', 0, 0, tiled=True)  17.8 us
    all_to_all x1, waiting for transfers between devices, per_device(): final = lax.all_to_all(blocks, 'zq', 0, 0, tiled=True)  16 us
    ppermute x6, waiting for transfers between devices, swap(): return lax.ppermute(value, axis, ring(2, 1))  12.9 us
    pallas_call x1, Pallas kernels, backward(): pl.pallas_call(backward_kernel, grid_spec=pltpu.PrefetchScalarGridSpec(nu...  9.57 us
    all_to_all x2, starting transfers between devices, spread_x(): return lax.all_to_all(copies, 'x', 0, 0, tiled=True)  8.89 us
  transfers between devices with their start and end apart: 10, of which 3 were waited for; matrix products, arithmetic and copies ran while one was open for 4% of the time, Pallas kernels for 15%

profile of v3, /device:TPU:8, one launch (start us, length us, event | category | flops | bytes accessed | tf_op | source)
XLA Modules:
  0.0 204.2 jit_solution(15646698662846615740)
XLA Ops:
  2.6 1.9 fusion.16.row_ref
  4.5 6.6 %shard_map.120 = bf16[4,768,256]{2,1,0:T(8,128)(2,1)} custom-call(f32[1,768]{1,0:T(1,128)} %fusion.16.row_ref, bf16[3072,256]{1,0:T(8,128)(2,1)} %bitcast.57), custom_call_target="tpu_custom_call" | custom-call | flops 1208000000 | bytes 3000000 | tf_op jit(solution)/shard_map/pallas_call | solution.py:270
  11.1 34.1 %conditional.1 = (bf16[4,768,256]{2,1,0:T(8,128)(2,1)}, bf16[4,768,256]{2,1,0:T(8,128)(2,1)}) conditional(s32[]{:T(128)} %clamp.3, bf16[4,768,256]{2,1,0:T(8,128)(2,1)} %shard_map.120, bf16[4,768,256]{2,1,0:T(8,128)(2,1)} %shard_map.120, bf16[4,768,256]{2,1,0:T(8,128)(2,1)} %shard_map.120, ...), branch_computations={%region_1.2_spmd, %region_2.3_spmd, %region_3.4_spmd, %region_4.5_... | conditional | bytes 9601114 | solution.py:307
  11.1 4.3 %all-to-all-start.9 = ((bf16[4,768,256]{2,1,0:T(8,128)(2,1)}), bf16[4,768,256]{2,1,0:T(8,128)(2,1)}, u32[]{:S(2)}, u32[]{:S(2)}) async-start(bf16[4,768,256]{2,1,0:T(8,128)(2,1)} %param.9), calls=%async_computation.9 | async-start | bytes 3145728 | tf_op jit(solution)/shard_map/cond/branch_9_fun/all_to_all | solution.py:31
  16.4 15.7 %collective-permute-start.9 = (bf16[640,256]{1,0:T(8,128)(2,1)S(1)}, bf16[640,256]{1,0:T(8,128)(2,1)S(1)}, u32[]{:S(2)}, u32[]{:S(2)}) collective-permute-start(bf16[640,256]{1,0:T(8,128)(2,1)S(1)} %slice_bitcast_fusion.9), channel_id=1, source_target_pairs={{0,8},{8,0},{1,9},{9,1},{2,10},{10,2},{3,11},{11,3},{4,12},{12,4},... | collective-permute-start | bytes 983048 | tf_op jit(solution)/shard_map/cond/branch_9_fun/ppermute | solution.py:27
  32.2 11.7 %collective-permute-done.9 = bf16[640,256]{1,0:T(8,128)(2,1)S(1)} collective-permute-done((bf16[640,256]{1,0:T(8,128)(2,1)S(1)}, bf16[640,256]{1,0:T(8,128)(2,1)S(1)}, u32[]{:S(2)}, u32[]{:S(2)}) %collective-permute-start.9) | collective-permute-done | bytes 327712 | tf_op jit(solution)/shard_map/cond/branch_9_fun/ppermute | solution.py:27
  45.2 1.9 collective-permute-start.12
  47.2 4.5 %all-to-all-start.12 = ((bf16[4,768,256]{2,1,0:T(8,128)(2,1)}), bf16[4,768,256]{2,1,0:T(8,128)(2,1)S(1)}, u32[]{:S(2)}, u32[]{:S(2)}) async-start(bf16[4,768,256]{2,1,0:T(8,128)(2,1)} %get-tuple-element.39), calls=%async_computation.12 | async-start | bytes 3145728 | tf_op jit(solution)/shard_map/all_to_all | solution.py:31
  54.8 7.5 %shard_map.119 = (bf16[768,256]{1,0:T(8,128)(2,1)}, bf16[256,768]{1,0:T(8,128)(2,1)}, f32[768,2]{1,0:T(8,128)}) custom-call(s32[2]{0:T(128)} %pad_add_fusion.info_ref, bf16[768,256]{1,0:T(8,128)(2,1)} %bitcast.58, bf16[768,256]{1,0:T(8,128)(2,1)} %bitcast.60, bf16[768,256]{1,0:T(8,128)(2,1)} %bitcast.62, s32[768,1]{1,0:T(8,128)} %copy.22.col_ref, ...), custom_call_target="tpu_custom_call" | custom-call | flops 604000000 | bytes 2000000 | tf_op jit(solution)/shard_map/pallas_call | solution.py:130
  62.9 6.1 %shard_map.121 = (f32[768,256]{1,0:T(8,128)}, bf16[2,4,2,256,128]{4,3,2,1,0:T(8,128)(2,1)}) custom-call(s32[2]{0:T(128)} %get-tuple-element.79.info_ref, bf16[4,768,256]{2,1,0:T(8,128)(2,1)} %get-tuple-element.40.shard_ref, bf16[16,256,256]{2,1,0:T(8,128)(2,1)} %bitcast.49, bf16[256,768]{1,0:T(8,128)(2,1)} %get-tuple-element.41.scaled_ref), custom_call_target="tpu_custom_call" | custom-call | flops 805000000 | bytes 4000000 | tf_op jit(solution)/shard_map/pallas_call | solution.py:190
  70.7 6.3 %shard_map.122 = (f32[768,256]{1,0:T(8,128)}, bf16[2,4,2,256,128]{4,3,2,1,0:T(8,128)(2,1)}) custom-call(s32[2]{0:T(128)} %pad_add_fusion.3.info_ref, bf16[4,768,256]{2,1,0:T(8,128)(2,1)} %copy-done.3, bf16[16,256,256]{2,1,0:T(8,128)(2,1)} %bitcast.50, bf16[256,768]{1,0:T(8,128)(2,1)} %get-tuple-element.41.scaled_ref, ...), custom_call_target="tpu_custom_call", output_to_operand_aliasing={{1}: (5, {})} | custom-call | flops 805000000 | bytes 4000000 | tf_op jit(solution)/shard_map/pallas_call | solution.py:190
  77.0 2.3 %collective-permute-start.13 = (bf16[4,768,256]{2,1,0:T(8,128)(2,1)S(1)}, bf16[4,768,256]{2,1,0:T(8,128)(2,1)S(1)}, u32[]{:S(2)}, u32[]{:S(2)}) collective-permute-start(bf16[4,768,256]{2,1,0:T(8,128)(2,1)S(1)} %all-to-all-done.12.shard_ref), channel_id=1, source_target_pairs={{0,1},{1,0},{2,3},{3,2},{4,5},{5,4},{6,7},{7,6},{8,9},{9,8},{10,11... | collective-permute-start | bytes 4718600 | tf_op jit(solution)/shard_map/ppermute | solution.py:27
  79.9 6.3 %shard_map.123 = (f32[768,256]{1,0:T(8,128)}, bf16[2,4,2,256,128]{4,3,2,1,0:T(8,128)(2,1)}) custom-call(s32[2]{0:T(128)} %get-tuple-element.78.info_ref, bf16[4,768,256]{2,1,0:T(8,128)(2,1)} %copy-done, bf16[16,256,256]{2,1,0:T(8,128)(2,1)} %bitcast.51, bf16[256,768]{1,0:T(8,128)(2,1)} %get-tuple-element.41.scaled_ref, f32[768,256]{1,0:T(8,128)} %get-tuple-element.47.refs_0_), custom_call_target="tpu_custom_call" | custom-call | flops 805000000 | bytes 4000000 | tf_op jit(solution)/shard_map/pallas_call | solution.py:190
  87.4 6.3 %shard_map.124 = (f32[768,256]{1,0:T(8,128)}, bf16[2,4,2,256,128]{4,3,2,1,0:T(8,128)(2,1)}) custom-call(s32[2]{0:T(128)} %pad_add_fusion.2.info_ref, bf16[4,768,256]{2,1,0:T(8,128)(2,1)} %copy-done.4, bf16[16,256,256]{2,1,0:T(8,128)(2,1)} %bitcast.52, bf16[256,768]{1,0:T(8,128)(2,1)} %get-tuple-element.41.scaled_ref, ...), custom_call_target="tpu_custom_call", output_to_operand_aliasing={{1}: (5, {})} | custom-call | flops 805000000 | bytes 4000000 | tf_op jit(solution)/shard_map/pallas_call | solution.py:190
  93.7 9.6 %shard_map.125 = (bf16[768,256]{1,0:T(8,128)(2,1)}, bf16[768,256]{1,0:T(8,128)(2,1)}, f32[768,1]{1,0:T(8,128)}) custom-call(s32[2]{0:T(128)} %pad_add_fusion.info_ref, bf16[768,256]{1,0:T(8,128)(2,1)} %bitcast.59, bf16[768,256]{1,0:T(8,128)(2,1)} %bitcast.61, bf16[768,256]{1,0:T(8,128)(2,1)} %bitcast.63, s32[768,1]{1,0:T(8,128)} %copy.22.col_ref, ...), custom_call_target="tpu_custom_call" | custom-call | flops 1510000000 | bytes 4000000 | tf_op jit(solution)/shard_map/pallas_call | solution.py:145
  105.5 2.2 %collective-permute-start.14 = (bf16[400,256]{1,0:T(8,128)(2,1)S(1)}, bf16[400,256]{1,0:T(8,128)(2,1)S(1)}, u32[]{:S(2)}, u32[]{:S(2)}) collective-permute-start(bf16[400,256]{1,0:T(8,128)(2,1)S(1)} %pad_maximum_fusion.1), channel_id=1, source_target_pairs={{0,1},{1,0},{2,3},{3,2},{4,5},{5,4},{6,7},{7,6},{8,9},{9,8},{10,11... | collective-permute-start | bytes 614408 | tf_op jit(solution)/shard_map/ppermute | solution.py:27
  109.9 17.8 %all_to_all.73 = bf16[4,400,256]{2,1,0:T(8,128)(2,1)S(1)} all-to-all(bf16[4,400,256]{2,1,0:T(8,128)(2,1)S(1)} %broadcast_in_dim.85), channel_id=1, replica_groups=mesh['zq'=4,'zp'=2,'y'=4,'zh'=2,'x'=4,'core'=2] {'x'}, dimensions={0} | all-to-all | bytes 1638400 | tf_op jit(solution)/shard_map/all_to_all | solution.py:31
  127.8 27.0 %all_to_all.74.moved_ref = bf16[8,2,256,128]{3,2,1,0:T(8,128)(2,1)} all-to-all(bf16[8,2,256,128]{3,2,1,0:T(8,128)(2,1)S(1)} %bitcast.53), channel_id=1, replica_groups=mesh['zq'=4,'zp'=2,'y'=4,'zh'=2,'x'=4,'core'=2] {'zp','y'}, dimensions={0} | all-to-all | bytes 2097152 | tf_op jit(solution)/shard_map/all_to_all | solution.py:237
  154.8 5.3 %all-to-all-start.14 = ((bf16[8,2,256,128]{3,2,1,0:T(8,128)(2,1)}), bf16[8,2,256,128]{3,2,1,0:T(8,128)(2,1)S(1)}, u32[]{:S(2)}, u32[]{:S(2)}) async-start(bf16[8,2,256,128]{3,2,1,0:T(8,128)(2,1)} %bitcast.30), calls=%async_computation.14 | async-start | bytes 2097152 | tf_op jit(solution)/shard_map/all_to_all | solution.py:237
  160.4 1.9 collective-permute-start.15
  162.4 12.2 %collective-permute-start.16 = (f32[768]{0:T(1024)S(1)}, f32[768]{0:T(1024)S(1)}, u32[]{:S(2)}, u32[]{:S(2)}) collective-permute-start(f32[768]{0:T(1024)S(1)} %reshape.123), channel_id=1, source_target_pairs={{0,8},{8,0},{1,9},{9,1},{2,10},{10,2},{3,11},{11,3},{4,12},{12,4},... | collective-permute-start | bytes 9224 | tf_op jit(solution)/shard_map/ppermute | solution.py:27
  174.5 1.9 shard_map.126.refs_0_
  179.4 6.2 %all-to-all-start.16 = ((bf16[4,256,128]{2,1,0:T(8,128)(2,1)}), bf16[4,256,128]{2,1,0:T(8,128)(2,1)S(1)}, u32[]{:S(2)}, u32[]{:S(2)}) async-start(bf16[4,256,128]{2,1,0:T(8,128)(2,1)} %shard_map.127), calls=%async_computation.16 | async-start | bytes 524288 | tf_op jit(solution)/shard_map/all_to_all | solution.py:333
  187.4 16.0 %all-to-all-done.16 = bf16[4,256,128]{2,1,0:T(8,128)(2,1)S(1)} async-done(((bf16[4,256,128]{2,1,0:T(8,128)(2,1)}), bf16[4,256,128]{2,1,0:T(8,128)(2,1)S(1)}, u32[]{:S(2)}, u32[]{:S(2)}) %all-to-all-start.16) | async-done | bytes 262176 | tf_op jit(solution)/shard_map/all_to_all | solution.py:333
  (60 shorter events, 21.0 us)
Async XLA Ops:
  11.1 32.8 %all-to-all-start.9 = ((bf16[4,768,256]{2,1,0:T(8,128)(2,1)}), bf16[4,768,256]{2,1,0:T(8,128)(2,1)}, u32[]{:S(2)}, u32[]{:S(2)}) async-start(bf16[4,768,256]{2,1,0:T(8,128)(2,1)} %param.9), calls=%async_computation.9 | async-start | bytes 3145728 | tf_op jit(solution)/shard_map/cond/branch_9_fun/all_to_all | solution.py:31
  16.4 27.4 %collective-permute-start.9 = (bf16[640,256]{1,0:T(8,128)(2,1)S(1)}, bf16[640,256]{1,0:T(8,128)(2,1)S(1)}, u32[]{:S(2)}, u32[]{:S(2)}) collective-permute-start(bf16[640,256]{1,0:T(8,128)(2,1)S(1)} %slice_bitcast_fusion.9), channel_id=1, source_target_pairs={{0,8},{8,0},{1,9},{9,1},{2,10},{10,2},{3,11},{11,3},{4,12},{12,4},... | collective-permute-start | bytes 983048 | tf_op jit(solution)/shard_map/cond/branch_9_fun/ppermute | solution.py:27
  45.2 24.3 %collective-permute-start.12 = (bf16[4,768,256]{2,1,0:T(8,128)(2,1)}, bf16[4,768,256]{2,1,0:T(8,128)(2,1)S(1)}, u32[]{:S(2)}, u32[]{:S(2)}) collective-permute-start(bf16[4,768,256]{2,1,0:T(8,128)(2,1)} %get-tuple-element.40.shard_ref), channel_id=1, source_target_pairs={{0,1},{1,0},{2,3},{3,2},{4,5},{5,4},{6,7},{7,6},{8,9},{9,8},{10,11... | collective-permute-start | bytes 4718600 | tf_op jit(solution)/shard_map/ppermute | solution.py:27
  47.1 4.6 %copy-start.6 = (s32[1,768]{1,0:T(1,128)S(1)}, s32[1,768]{1,0:T(1,128)}, u32[]{:S(2)}) copy-start(s32[1,768]{1,0:T(1,128)} %row_ref.3) | copy-start | bytes 9220
  47.1 5.5 %copy-start.5 = (f32[1,768]{1,0:T(1,128)S(1)}, f32[1,768]{1,0:T(1,128)}, u32[]{:S(2)}) copy-start(f32[1,768]{1,0:T(1,128)} %param.23) | copy-start | bytes 9220
  47.2 29.9 %all-to-all-start.12 = ((bf16[4,768,256]{2,1,0:T(8,128)(2,1)}), bf16[4,768,256]{2,1,0:T(8,128)(2,1)S(1)}, u32[]{:S(2)}, u32[]{:S(2)}) async-start(bf16[4,768,256]{2,1,0:T(8,128)(2,1)} %get-tuple-element.39), calls=%async_computation.12 | async-start | bytes 3145728 | tf_op jit(solution)/shard_map/all_to_all | solution.py:31
  69.5 1.1 copy-start.3
  77.0 2.9 %copy-start = (bf16[4,768,256]{2,1,0:T(8,128)(2,1)}, bf16[4,768,256]{2,1,0:T(8,128)(2,1)S(1)}, u32[]{:S(2)}) copy-start(bf16[4,768,256]{2,1,0:T(8,128)(2,1)S(1)} %all-to-all-done.12.shard_ref) | copy-start | bytes 4718596
  77.0 9.2 %collective-permute-start.13 = (bf16[4,768,256]{2,1,0:T(8,128)(2,1)S(1)}, bf16[4,768,256]{2,1,0:T(8,128)(2,1)S(1)}, u32[]{:S(2)}, u32[]{:S(2)}) collective-permute-start(bf16[4,768,256]{2,1,0:T(8,128)(2,1)S(1)} %all-to-all-done.12.shard_ref), channel_id=1, source_target_pairs={{0,1},{1,0},{2,3},{3,2},{4,5},{5,4},{6,7},{7,6},{8,9},{9,8},{10,11... | collective-permute-start | bytes 4718600 | tf_op jit(solution)/shard_map/ppermute | solution.py:27
  86.2 1.2 copy-start.4
  105.5 3.3 %collective-permute-start.14 = (bf16[400,256]{1,0:T(8,128)(2,1)S(1)}, bf16[400,256]{1,0:T(8,128)(2,1)S(1)}, u32[]{:S(2)}, u32[]{:S(2)}) collective-permute-start(bf16[400,256]{1,0:T(8,128)(2,1)S(1)} %pad_maximum_fusion.1), channel_id=1, source_target_pairs={{0,1},{1,0},{2,3},{3,2},{4,5},{5,4},{6,7},{7,6},{8,9},{9,8},{10,11... | collective-permute-start | bytes 614408 | tf_op jit(solution)/shard_map/ppermute | solution.py:27
  109.8 17.9 %copy-start.2 = (bf16[2,4,2,256,128]{4,3,2,1,0:T(8,128)(2,1)S(1)}, bf16[2,4,2,256,128]{4,3,2,1,0:T(8,128)(2,1)}, u32[]{:S(2)}) copy-start(bf16[2,4,2,256,128]{4,3,2,1,0:T(8,128)(2,1)} %get-tuple-element.56) | copy-start | bytes 3145732
  154.8 21.7 %all-to-all-start.14 = ((bf16[8,2,256,128]{3,2,1,0:T(8,128)(2,1)}), bf16[8,2,256,128]{3,2,1,0:T(8,128)(2,1)S(1)}, u32[]{:S(2)}, u32[]{:S(2)}) async-start(bf16[8,2,256,128]{3,2,1,0:T(8,128)(2,1)} %bitcast.30), calls=%async_computation.14 | async-start | bytes 2097152 | tf_op jit(solution)/shard_map/all_to_all | solution.py:237
  160.4 25.8 %collective-permute-start.15 = (bf16[384,512]{1,0:T(8,128)(2,1)S(1)}, bf16[384,512]{1,0:T(8,128)(2,1)S(1)}, u32[]{:S(2)}, u32[]{:S(2)}) collective-permute-start(bf16[384,512]{1,0:T(8,128)(2,1)S(1)} %pad_maximum_fusion), channel_id=1, source_target_pairs={{0,1},{1,0},{2,3},{3,2},{4,5},{5,4},{6,7},{7,6},{8,9},{9,8},{10,11... | collective-permute-start | bytes 1179656 | tf_op jit(solution)/shard_map/ppermute | solution.py:27
  162.4 23.2 %collective-permute-start.16 = (f32[768]{0:T(1024)S(1)}, f32[768]{0:T(1024)S(1)}, u32[]{:S(2)}, u32[]{:S(2)}) collective-permute-start(f32[768]{0:T(1024)S(1)} %reshape.123), channel_id=1, source_target_pairs={{0,8},{8,0},{1,9},{9,1},{2,10},{10,2},{3,11},{11,3},{4,12},{12,4},... | collective-permute-start | bytes 9224 | tf_op jit(solution)/shard_map/ppermute | solution.py:27
  176.5 1.0 copy-start.1
  179.4 24.1 %all-to-all-start.16 = ((bf16[4,256,128]{2,1,0:T(8,128)(2,1)}), bf16[4,256,128]{2,1,0:T(8,128)(2,1)S(1)}, u32[]{:S(2)}, u32[]{:S(2)}) async-start(bf16[4,256,128]{2,1,0:T(8,128)(2,1)} %shard_map.127), calls=%async_computation.16 | async-start | bytes 524288 | tf_op jit(solution)/shard_map/all_to_all | solution.py:333

commit v4 on v2

v4 whole, which is shorter than its diff:
```python
import functools

import jax
import jax.numpy as jnp
from jax import lax
from jax.experimental import pallas as pl
from jax.experimental.pallas import tpu as pltpu
from jax.sharding import Mesh
from jax.sharding import PartitionSpec as P

HEAD_SIZE = 128
ZQ, ZP, Y, ZH, X, CORE = 4, 2, 4, 2, 4, 2
SLOTS, WIDE, HEADS = 768, 256, 2
SCALE = HEAD_SIZE ** (-0.5)
BF, F32 = jnp.bfloat16, jnp.float32
ROWS = 256
STEP = 64
HALF, EXTRA = SLOTS // 2, 16
LIMIT = pltpu.CompilerParams(vmem_limit_bytes=24 * 1024 * 1024)


def ring(n, k):
    return [(i, (i + k) % n) for i in range(n)]


def swap(value, axis):
    return lax.ppermute(value, axis, ring(2, 1))


def spread_x(copies):
    return lax.all_to_all(copies, "x", 0, 0, tiled=True)


def repeated(block):
    return jnp.broadcast_to(block[None], (X,) + block.shape)


def exchange(rows, picked, attention):
    other = swap(picked[:rows], "zh")
    near = spread_x(repeated(picked))
    other = jnp.pad(other, ((0, SLOTS - rows), (0, 0)))
    return repeated(other), near, forward(*attention)


def transposed_dot(a, b):
    return lax.dot_general(a, b, (((0,), (0,)), ((), ())), preferred_element_type=F32)


def rows_dot(a, b):
    return lax.dot_general(a, b, (((1,), (1,)), ((), ())), preferred_element_type=F32)


def column(row):
    parts = [
        jnp.broadcast_to(row[:, a : a + 128], (128, 128)).T for a in range(0, row.shape[1], 128)
    ]
    return jnp.concatenate(parts, axis=0)[:, :1]


def allowed_block(info_ref, pos_col, pos_row):
    first = pl.program_id(0) * ROWS
    shape = (ROWS, SLOTS)
    i = lax.broadcasted_iota(jnp.int32, shape, 0) + first
    j = lax.broadcasted_iota(jnp.int32, shape, 1)
    return ((j < info_ref[1]) & (pos_row <= pos_col)) | (i == j)


def forward_kernel(info_ref, q_ref, k_ref, v_ref, col_ref, row_ref, logit_ref, att_ref, scaled_ref, lse_ref):
    allowed = allowed_block(info_ref, column(col_ref[...]), row_ref[...])
    weight = 1.0 / (1.0 + jnp.exp(-column(logit_ref[...])))
    for h in range(HEADS):
        lanes = slice(h * HEAD_SIZE, (h + 1) * HEAD_SIZE)
        s = rows_dot(q_ref[:, lanes], k_ref[...]) * SCALE
        s = jnp.where(allowed, s, -1e30)
        top = jnp.max(s, axis=1, keepdims=True)
        e = jnp.exp(s - top)
        total = jnp.sum(e, axis=1, keepdims=True)
        p = (e * (1.0 / total)).astype(BF)
        att = jnp.dot(p, v_ref[...], preferred_element_type=F32).astype(BF)
        att_ref[:, lanes] = att
        scaled_ref[lanes, :] = (weight * att.astype(F32)).astype(BF).T
        lse_ref[:, h : h + 1] = top + jnp.log(total)


def backward_kernel(
    info_ref, q_ref, k_ref, v_ref, col_ref, row_ref, logit_ref, lse_ref, att_ref, go_ref,
    gq_ref, kept_ref, sent_ref, router_ref, sum_ref, terms_ref,
):
    step = pl.program_id(0)
    allowed = allowed_block(info_ref, column(col_ref[...]), row_ref[...])
    weight = 1.0 / (1.0 + jnp.exp(-column(logit_ref[...])))
    grad_o = go_ref[...]
    router = jnp.sum(grad_o * att_ref[...].astype(F32), axis=1, keepdims=True)
    router = jnp.broadcast_to(router, (ROWS, 128)).T[:1]
    router_ref[...] = router
    lead = router.astype(BF).astype(F32)
    grad_attn = (weight * grad_o).astype(BF)

    @pl.when(step == 0)
    def _():
        sum_ref[...] = jnp.zeros_like(sum_ref)
        terms_ref[...] = jnp.zeros_like(terms_ref)

    terms_ref[pl.ds(step, 1), :] = lead
    terms_ref[pl.ds(step + SLOTS // ROWS, 1), :] = router - lead
    for h in range(HEADS):
        lanes = slice(h * HEAD_SIZE, (h + 1) * HEAD_SIZE)
        q = q_ref[:, lanes]
        s = rows_dot(q, k_ref[...]) * SCALE
        p = jnp.exp(jnp.where(allowed, s - lse_ref[:, h : h + 1], -1e30))
        ga = grad_attn[:, lanes]
        gp = rows_dot(ga, v_ref[...])
        delta = jnp.sum(p * gp, axis=1, keepdims=True)
        gs = (p * (gp - delta)).astype(BF)
        gq = jnp.dot(gs, k_ref[...], preferred_element_type=F32) * SCALE
        gq_ref[:, lanes] = gq.astype(BF)
        sum_ref[:, :HEAD_SIZE] += transposed_dot(gs, q)
        sum_ref[:, HEAD_SIZE:] += transposed_dot(p.astype(BF), ga)

    @pl.when(step == pl.num_programs(0) - 1)
    def _():
        core = info_ref[2]
        for ref, side in ((kept_ref, core), (sent_ref, 1 - core)):
            rows = pl.ds(pl.multiple_of(side * HALF, HALF), HALF)
            ref[:HALF, :HEAD_SIZE] = (sum_ref[rows, :HEAD_SIZE] * SCALE).astype(BF)
            ref[:HALF, HEAD_SIZE:] = sum_ref[rows, HEAD_SIZE:].astype(BF)
        sent_ref[HALF:, :] = terms_ref[...].astype(BF)


def by_rows(width):
    return pl.BlockSpec((ROWS, width), lambda i, info: (i, 0))


def row_part():
    return pl.BlockSpec((1, ROWS), lambda i, info: (0, i))


def by_group():
    return pl.BlockSpec((SLOTS, HEAD_SIZE), lambda i, info: (0, info[0]))


def whole(shape):
    return pl.BlockSpec(shape, lambda i, info: (0,) * len(shape))


def shape_of(shape, dtype):
    return jax.ShapeDtypeStruct(shape, dtype)


def forward(info, q, k, v, pos_col, pos_row, logit_col):
    return pl.pallas_call(
        forward_kernel,
        grid_spec=pltpu.PrefetchScalarGridSpec(
            num_scalar_prefetch=1,
            grid=(SLOTS // ROWS,),
            in_specs=[by_rows(WIDE), by_group(), by_group(), row_part(), whole((1, SLOTS)), row_part()],
            out_specs=[by_rows(WIDE), pl.BlockSpec((WIDE, ROWS), lambda i, info: (0, i)), by_rows(HEADS)],
        ),
        out_shape=[shape_of((SLOTS, WIDE), BF), shape_of((WIDE, SLOTS), BF), shape_of((SLOTS, HEADS), F32)],
        compiler_params=LIMIT,
        cost_estimate=pl.CostEstimate(flops=4 * 10**9, bytes_accessed=2 * 10**6, transcendentals=1200000),
    )(info, q, k, v, pos_col, pos_row, logit_col)


def backward(info, q, k, v, pos_col, pos_row, logit_col, lse, att, grad_o):
    return pl.pallas_call(
        backward_kernel,
        grid_spec=pltpu.PrefetchScalarGridSpec(
            num_scalar_prefetch=1,
            grid=(SLOTS // ROWS,),
            in_specs=[
                by_rows(WIDE), by_group(), by_group(), row_part(), whole((1, SLOTS)), row_part(),
                by_rows(HEADS), by_rows(WIDE), by_rows(WIDE),
            ],
            out_specs=[by_rows(WIDE), whole((HALF, WIDE)), whole((HALF + EXTRA, WIDE)), row_part()],
            scratch_shapes=[pltpu.VMEM((SLOTS, WIDE), F32), pltpu.VMEM((EXTRA, WIDE), F32)],
        ),
        out_shape=[
            shape_of((SLOTS, WIDE), BF), shape_of((HALF, WIDE), BF),
            shape_of((HALF + EXTRA, WIDE), BF), shape_of((1, SLOTS), F32),
        ],
        compiler_params=LIMIT,
        cost_estimate=pl.CostEstimate(flops=7 * 10**9, bytes_accessed=4 * 10**6, transcendentals=1200000),
    )(info, q, k, v, pos_col, pos_row, logit_col, lse, att, grad_o)


def products_kernel(info_ref, near_ref, far_ref, wn_ref, wf_ref, scaled_ref, *refs):
    go_ref, wg_ref = refs[-2:]
    core = info_ref[0]
    near, far = near_ref[0], far_ref[0]
    part = jnp.dot(near, wn_ref[0], preferred_element_type=F32)
    part = part + jnp.dot(far, wf_ref[0], preferred_element_type=F32)
    first = pl.program_id(0) == 0

    @pl.when(first)
    def _():
        go_ref[...] = part + refs[0][...] if len(refs) == 3 else part

    @pl.when(jnp.logical_not(first))
    def _():
        go_ref[...] += part

    for shard, y in ((near, 2 * core), (far, 2 - 2 * core)):
        grad = jnp.dot(scaled_ref[...], shard, preferred_element_type=F32).astype(BF)
        wg_ref[0, y, 0] = grad[:, :128]
        wg_ref[0, y + 1, 0] = grad[:, 128:]


def products(core, half, near, far, w_out, scaled_t, begin=None):
    info = jnp.stack([core, half]).astype(jnp.int32)
    more = [] if begin is None else [begin]
    shard = pl.BlockSpec((1, SLOTS, WIDE), lambda i, info: (i, 0, 0))
    w_near = pl.BlockSpec((1, WIDE, WIDE), lambda i, info: (info[1] * 8 + i * 2 + info[0], 0, 0))
    w_far = pl.BlockSpec((1, WIDE, WIDE), lambda i, info: (info[1] * 8 + i * 2 + 1 - info[0], 0, 0))
    w_parts = w_out.reshape(ZH * X * CORE, WIDE, WIDE)
    return pl.pallas_call(
        products_kernel,
        grid_spec=pltpu.PrefetchScalarGridSpec(
            num_scalar_prefetch=1,
            grid=(X,),
            in_specs=[shard, shard, w_near, w_far, whole((WIDE, SLOTS))]
            + [whole((SLOTS, WIDE)) for _ in more],
            out_specs=[
                whole((SLOTS, WIDE)),
                pl.BlockSpec((1, Y, 1, WIDE, 128), lambda i, info: (i % 2, 0, i // 2, 0, 0)),
            ],
        ),
        out_shape=[shape_of((SLOTS, WIDE), F32), shape_of((ZP, Y, 2, WIDE, 128), BF)],
        compiler_params=LIMIT,
        cost_estimate=pl.CostEstimate(flops=4 * 10**9, bytes_accessed=8 * 10**6, transcendentals=0),
    )(info, near, far, w_parts, w_parts, scaled_t, *more)


def fold_kernel(info_ref, moved_ref, *refs):
    refs[-1][0] = jnp.sum(moved_ref[...].astype(F32), axis=0)[0].astype(BF)


def fold(half, moved, begin=None):
    more = [] if begin is None else [begin]
    return pl.pallas_call(
        fold_kernel,
        grid_spec=pltpu.PrefetchScalarGridSpec(
            num_scalar_prefetch=1,
            grid=(2,),
            in_specs=[pl.BlockSpec((ZP * Y, 1, WIDE, 128), lambda i, info: (0, i, 0, 0))]
            + [pl.BlockSpec(memory_space=pl.ANY) for _ in more],
            out_specs=pl.BlockSpec((1, WIDE, 128), lambda i, info: (info[0] * 2 + i, 0, 0)),
        ),
        out_shape=shape_of((ZQ, WIDE, 128), BF),
        input_output_aliases={2: 0} if more else {},
        compiler_params=LIMIT,
        cost_estimate=pl.CostEstimate(flops=1 * 10**6, bytes_accessed=2 * 10**6, transcendentals=0),
    )(half.astype(jnp.int32).reshape(1), moved, *more)


def over_zp_y(blocks):
    blocks = blocks.reshape(ZP * Y, 2, WIDE, 128)
    return lax.all_to_all(blocks, ("zp", "y"), 0, 0, tiled=True)


def packed(router):
    lead = lax.reduce_precision(router, 8, 7)
    terms = jnp.concatenate([lead, router - lead]).astype(BF).reshape(-1, WIDE)
    return jnp.pad(terms, ((0, EXTRA - terms.shape[0]), (0, 0)))


def unpacked(rows):
    terms = rows[: 2 * SLOTS // WIDE].astype(F32).reshape(2, SLOTS)
    return terms[0] + terms[1]


def per_device(cotangent, routed, counts, logits, query_rows, key_rows, routed_value_rows, w_out):
    zh, x, core = lax.axis_index("zh"), lax.axis_index("x"), lax.axis_index("core")
    dp_index = (lax.axis_index("zq") * ZP + lax.axis_index("zp")) * Y + lax.axis_index("y")
    own = jnp.arange(counts.shape[0], dtype=jnp.int32) == dp_index
    own_count = jnp.sum(jnp.where(own, counts, 0))
    positions = routed[0]
    picked = cotangent[0].at[positions].get(mode="promise_in_bounds")
    live = jnp.arange(SLOTS, dtype=jnp.int32) < own_count
    picked = jnp.where(live[:, None], picked, jnp.zeros((), BF))

    info = jnp.stack([x // 2, own_count, core]).astype(jnp.int32)
    attention = (
        info, query_rows[0], key_rows[0], routed_value_rows[0],
        routed, routed, logits,
    )
    sizes = range(STEP, SLOTS + 1, STEP)
    branch = jnp.maximum(own_count - 1, 0) // STEP
    other_copies, own_near, (attended, scaled_t, lse) = lax.switch(
        branch, [functools.partial(exchange, rows) for rows in sizes], picked, attention
    )
    other_near = spread_x(other_copies)
    own_far = swap(own_near, "core")
    begun, w_grad_own = products(core, zh, own_near, own_far, w_out, scaled_t)

    other_near, begun, w_grad_own = lax.optimization_barrier((other_near, begun, w_grad_own))
    other_far = swap(other_near, "core")
    moved_own = over_zp_y(w_grad_own)
    grad_o, w_grad_other = products(core, 1 - zh, other_near, other_far, w_out, scaled_t, begun)

    moved_own, grad_o, w_grad_other = lax.optimization_barrier((moved_own, grad_o, w_grad_other))
    moved_other = over_zp_y(w_grad_other)
    blocks = fold(zh, moved_own)
    grad_q, kept, sent, router = backward(*attention, lse, attended, grad_o)
    came = swap(sent, "core")
    chip = (kept.astype(F32) + came[:HALF].astype(F32)).astype(BF)
    chip = jnp.concatenate([chip, packed(router[0] + unpacked(came[HALF:]))], 0)

    moved_other, blocks, chip = lax.optimization_barrier((moved_other, blocks, chip))
    blocks = fold(1 - zh, moved_other, blocks)
    final = lax.all_to_all(blocks, "zq", 0, 0, tiled=True)
    w_grad = jnp.sum(final.astype(F32), axis=0).T.astype(BF)

    pieces = [chip] + [lax.ppermute(chip, "x", ring(X, k)) for k in (1, 2, 3)]
    wide = [piece[:HALF].astype(F32) for piece in pieces]
    first = sum(jnp.where((x - k) % X < 2, wide[k], 0.0) for k in range(X))
    second = sum(jnp.where((x - k) % X < 2, 0.0, wide[k]) for k in range(X))
    joined = jnp.concatenate(
        [first[:, :HEAD_SIZE], second[:, :HEAD_SIZE], first[:, HEAD_SIZE:], second[:, HEAD_SIZE:]], 1
    ).astype(BF)
    theirs = swap(joined, "core")
    router = sum(unpacked(piece[HALF:]) for piece in pieces)
    router = router + swap(router, "zh")
    rows = jnp.where(
        core == 0, jnp.concatenate([joined, theirs], 0), jnp.concatenate([theirs, joined], 0)
    )
    key_total, value_total = rows[:, : 2 * HEAD_SIZE], rows[:, 2 * HEAD_SIZE :]
    router_weight = jax.nn.sigmoid(logits[0])
    grad_logits = router * router_weight * (1.0 - router_weight)
    return (grad_q[None], key_total[None], value_total[None], w_grad, grad_logits[None])


def solution(mesh):
    fine = Mesh(mesh.devices.reshape(ZQ, ZP, Y, ZH, X, CORE), ("zq", "zp", "y", "zh", "x", "core"))
    dp, col = ("zq", "zp", "y"), ("x", "core")
    row_col = ("zh",) + col
    placed = (
        P(dp, None, row_col),
        P(dp, None),
        P(),
        P(dp, None),
        P(dp, None, row_col),
        P(dp, None, "zh"),
        P(dp, None, "zh"),
        P(None, row_col),
    )
    return jax.shard_map(
        per_device,
        mesh=fine,
        in_specs=placed,
        out_specs=(
            P(dp, None, row_col),
            P(dp, None, "zh"),
            P(dp, None, "zh"),
            P(dp, row_col),
            P(dp, None),
        ),
        check_vma=False,
    )
```

time: 225 us -> 168 us (0.75)
  the two profiles are of different devices: /device:TPU:64 before, /device:TPU:6 now
where the time goes in v4:
time: 168 us; the launch traced here: 166 us
  starting transfers between devices  82.5 us (49%)
  Pallas kernels  30.8 us (18%)
  waiting for transfers between devices  23.4 us (14%)
  local copies, waits for them, and re-layouts  20.4 us (12%)
  other arithmetic  7.01 us (4%)
  between operations  1.74 us (1%)
    ppermute x6, starting transfers between devices, swap(): return lax.ppermute(value, axis, ring(2, 1))  27.6 us
    all_to_all x2, starting transfers between devices, over_zp_y(): return lax.all_to_all(blocks, ('zp', 'y'), 0, 0, tiled=True)  17.3 us
    all_to_all x2, starting transfers between devices, spread_x(): return lax.all_to_all(copies, 'x', 0, 0, tiled=True)  15.1 us
    unnamed x37, local copies, waits for them, and re-layouts  14.8 us
    ppermute x6, waiting for transfers between devices, swap(): return lax.ppermute(value, axis, ring(2, 1))  14.3 us
    pallas_call x2, Pallas kernels, products(): pl.pallas_call(products_kernel, grid_spec=pltpu.PrefetchScalarGridSpec(nu...  13.5 us
    all_to_all x1, starting transfers between devices, per_device(): final = lax.all_to_all(blocks, 'zq', 0, 0, tiled=True)  12.1 us
    ppermute x3, starting transfers between devices, per_device(): pieces = [chip] + [lax.ppermute(chip, 'x', ring(X, k)) for k in (1, 2, 3)]  10.4 us
  transfers between devices with their start and end apart: 14, of which 5 were waited for; matrix products, arithmetic and copies ran while one was open for 3% of the time, Pallas kernels for 19%

profile of v4, /device:TPU:6, one launch (start us, length us, event | category | flops | bytes accessed | tf_op | source)
XLA Modules:
  0.0 166.2 jit_solution(8870633460556860437)
XLA Ops:
  4.2 2.7 %gather_fusion = bf16[768,256]{1,0:T(8,128)(2,1)S(1)} fusion(bf16[3072,256]{1,0:T(8,128)(2,1)S(1)} %bitcast.20, s32[1024]{0:T(1024)S(1)} %pad_clamp_fusion), kind=kCustom, calls=%fused_computation | custom fusion | bytes 789504 | tf_op jit(solution)/shard_map/gather | solution.py:278
  7.8 34.5 %conditional.1 = (bf16[4,768,256]{2,1,0:T(8,128)(2,1)S(1)}, bf16[4,768,256]{2,1,0:T(8,128)(2,1)}, bf16[768,256]{1,0:T(8,128)(2,1)}, bf16[256,768]{1,0:T(8,128)(2,1)}, f32[768,2]{1,0:T(8,128)}) conditional(s32[]{:T(128)} %clamp.3, (bf16[768,256]{1,0:T(8,128)(2,1)S(1)}, s32[3]{0:T(128)S(1)}, ...), branch_computations={%region_1.2_spmd, %region_2.3_spmd, %region_3.4_spmd, %region_4.5_... | conditional | flops 4000000000 | bytes 15140110 | solution.py:289
  9.3 10.3 %all-to-all-start.9 = ((bf16[4,768,256]{2,1,0:T(8,128)(2,1)}), bf16[4,768,256]{2,1,0:T(8,128)(2,1)}, u32[]{:S(2)}, u32[]{:S(2)}) async-start(bf16[4,768,256]{2,1,0:T(8,128)(2,1)} %broadcast_in_dim.125), calls=%async_computation.9 | async-start | bytes 3145728 | tf_op jit(solution)/shard_map/cond/branch_9_fun/all_to_all | solution.py:31
  19.6 10.3 %collective-permute-start.9 = (bf16[640,256]{1,0:T(8,128)(2,1)S(1)}, bf16[640,256]{1,0:T(8,128)(2,1)S(1)}, u32[]{:S(2)}, u32[]{:S(2)}) collective-permute-start(bf16[640,256]{1,0:T(8,128)(2,1)S(1)} %slice.107), channel_id=1, source_target_pairs={{0,8},{8,0},{1,9},{9,1},{2,10},{10,2},{3,11},{11,3},{4,12},{12,4},... | collective-permute-start | bytes 983048 | tf_op jit(solution)/shard_map/cond/branch_9_fun/ppermute | solution.py:27
  29.9 6.1 %branch_9_fun.1 = (bf16[768,256]{1,0:T(8,128)(2,1)}, bf16[256,768]{1,0:T(8,128)(2,1)}, f32[768,2]{1,0:T(8,128)}) custom-call(s32[3]{0:T(128)S(1)} %get-tuple-element.259.info_ref, bf16[768,256]{1,0:T(8,128)(2,1)S(1)} %get-tuple-element.260.q_ref, bf16[768,256]{1,0:T(8,128)(2,1)S(1)} %get-tuple-element.261.k_ref, bf16[768,256]{1,0:T(8,128)(2,1)S(1)} %copy-done.27, ...), custom_call_target="tpu_custom_call" | custom-call | flops 4000000000 | bytes 2000000 | tf_op jit(solution)/shard_map/cond/branch_9_fun/pallas_call | solution.py:151
  36.0 6.1 %collective-permute-done.9 = bf16[640,256]{1,0:T(8,128)(2,1)S(1)} collective-permute-done((bf16[640,256]{1,0:T(8,128)(2,1)S(1)}, bf16[640,256]{1,0:T(8,128)(2,1)S(1)}, u32[]{:S(2)}, u32[]{:S(2)}) %collective-permute-start.9) | collective-permute-done | bytes 327712 | tf_op jit(solution)/shard_map/cond/branch_9_fun/ppermute | solution.py:27
  42.3 1.9 %collective-permute-start.12 = (bf16[4,768,256]{2,1,0:T(8,128)(2,1)}, bf16[4,768,256]{2,1,0:T(8,128)(2,1)}, u32[]{:S(2)}, u32[]{:S(2)}) collective-permute-start(bf16[4,768,256]{2,1,0:T(8,128)(2,1)} %get-tuple-element.318.near_ref), channel_id=1, source_target_pairs={{0,1},{1,0},{2,3},{3,2},{4,5},{5,4},{6,7},{7,6},{8,9},{9,8},{10,11... | collective-permute-start | bytes 4718600 | tf_op jit(solution)/shard_map/ppermute | solution.py:27
  44.2 4.8 %all-to-all-start.12 = ((bf16[4,768,256]{2,1,0:T(8,128)(2,1)}), bf16[4,768,256]{2,1,0:T(8,128)(2,1)S(1)}, u32[]{:S(2)}, u32[]{:S(2)}) async-start(bf16[4,768,256]{2,1,0:T(8,128)(2,1)} %copy-done.13), calls=%async_computation.12 | async-start | bytes 3145728 | tf_op jit(solution)/shard_map/all_to_all | solution.py:31
  50.7 6.8 %shard_map.119 = (f32[768,256]{1,0:T(8,128)S(1)}, bf16[2,4,2,256,128]{4,3,2,1,0:T(8,128)(2,1)S(1)}) custom-call(s32[2]{0:T(128)S(1)} %pad_add_fusion.1.info_ref, bf16[4,768,256]{2,1,0:T(8,128)(2,1)} %get-tuple-element.318.near_ref, bf16[4,768,256]{2,1,0:T(8,128)(2,1)} %collective-permute-done.12.far_ref, bf16[16,256,256]{2,1,0:T(8,128)(2,1)S(1)} %bitcast.23, ...), custom_call_target="tpu_custom_call" | custom-call | flops 4000000000 | bytes 8000000 | tf_op jit(solution)/shard_map/pallas_call | solution.py:216
  59.4 8.9 %all-to-all-done.12.near_ref = bf16[4,768,256]{2,1,0:T(8,128)(2,1)S(1)} async-done(((bf16[4,768,256]{2,1,0:T(8,128)(2,1)}), bf16[4,768,256]{2,1,0:T(8,128)(2,1)S(1)}, u32[]{:S(2)}, u32[]{:S(2)}) %all-to-all-start.12) | async-done | bytes 1572896 | tf_op jit(solution)/shard_map/all_to_all | solution.py:31
  69.5 11.6 %all-to-all-start.13 = ((bf16[8,2,256,128]{3,2,1,0:T(8,128)(2,1)}), bf16[8,2,256,128]{3,2,1,0:T(8,128)(2,1)S(1)}, u32[]{:S(2)}, u32[]{:S(2)}) async-start(bf16[8,2,256,128]{3,2,1,0:T(8,128)(2,1)} %bitcast.22), calls=%async_computation.13 | async-start | bytes 2097152 | tf_op jit(solution)/shard_map/all_to_all | solution.py:258
  81.0 1.9 %collective-permute-start.13 = (bf16[4,768,256]{2,1,0:T(8,128)(2,1)}, bf16[4,768,256]{2,1,0:T(8,128)(2,1)}, u32[]{:S(2)}, u32[]{:S(2)}) collective-permute-start(bf16[4,768,256]{2,1,0:T(8,128)(2,1)} %copy-done.3), channel_id=1, source_target_pairs={{0,1},{1,0},{2,3},{3,2},{4,5},{5,4},{6,7},{7,6},{8,9},{9,8},{10,11... | collective-permute-start | bytes 4718600 | tf_op jit(solution)/shard_map/ppermute | solution.py:27
  83.0 3.6 %collective-permute-done.13.far_ref = bf16[4,768,256]{2,1,0:T(8,128)(2,1)} collective-permute-done((bf16[4,768,256]{2,1,0:T(8,128)(2,1)}, bf16[4,768,256]{2,1,0:T(8,128)(2,1)}, u32[]{:S(2)}, u32[]{:S(2)}) %collective-permute-start.13) | collective-permute-done | bytes 1572896 | tf_op jit(solution)/shard_map/ppermute | solution.py:27
  90.8 6.7 %shard_map.120 = (f32[768,256]{1,0:T(8,128)S(1)}, bf16[2,4,2,256,128]{4,3,2,1,0:T(8,128)(2,1)S(1)}) custom-call(s32[2]{0:T(128)S(1)} %pad_add_fusion.2.info_ref, bf16[4,768,256]{2,1,0:T(8,128)(2,1)S(1)} %copy-done.4, bf16[4,768,256]{2,1,0:T(8,128)(2,1)} %collective-permute-done.13.far_ref, bf16[16,256,256]{2,1,0:T(8,128)(2,1)S(1)} %bitcast.25, ...), custom_call_target="tpu_custom_call" | custom-call | flops 4000000000 | bytes 8000000 | tf_op jit(solution)/shard_map/pallas_call | solution.py:216
  100.3 5.7 %all-to-all-start.14 = ((bf16[8,2,256,128]{3,2,1,0:T(8,128)(2,1)}), bf16[8,2,256,128]{3,2,1,0:T(8,128)(2,1)S(1)}, u32[]{:S(2)}, u32[]{:S(2)}) async-start(bf16[8,2,256,128]{3,2,1,0:T(8,128)(2,1)} %bitcast.21), calls=%async_computation.14 | async-start | bytes 2097152 | tf_op jit(solution)/shard_map/all_to_all | solution.py:258
  107.2 9.5 %shard_map.121 = (bf16[768,256]{1,0:T(8,128)(2,1)}, bf16[384,256]{1,0:T(8,128)(2,1)S(1)}, bf16[400,256]{1,0:T(8,128)(2,1)S(1)}, f32[1,768]{1,0:T(1,128)S(1)}) custom-call(s32[3]{0:T(128)S(1)} %pad_add_fusion.info_ref, bf16[768,256]{1,0:T(8,128)(2,1)} %bitcast.28, bf16[768,256]{1,0:T(8,128)(2,1)} %bitcast.41, bf16[768,256]{1,0:T(8,128)(2,1)} %bitcast.66, ...), custom_call_target="tpu_custom_call" | custom-call | flops 7000000000 | bytes 4000000 | tf_op jit(solution)/shard_map/pallas_call | solution.py:166
  116.7 1.9 %collective-permute-start.14 = (bf16[400,256]{1,0:T(8,128)(2,1)S(1)}, bf16[400,256]{1,0:T(8,128)(2,1)S(1)}, u32[]{:S(2)}, u32[]{:S(2)}) collective-permute-start(bf16[400,256]{1,0:T(8,128)(2,1)S(1)} %get-tuple-element.332), channel_id=1, source_target_pairs={{0,1},{1,0},{2,3},{3,2},{4,5},{5,4},{6,7},{7,6},{8,9},{9,8},{10,11... | collective-permute-start | bytes 614408 | tf_op jit(solution)/shard_map/ppermute | solution.py:27
  121.1 1.9 %collective-permute-start.17 = (bf16[400,256]{1,0:T(8,128)(2,1)S(1)}, bf16[400,256]{1,0:T(8,128)(2,1)S(1)}, u32[]{:S(2)}, u32[]{:S(2)}) collective-permute-start(bf16[400,256]{1,0:T(8,128)(2,1)S(1)} %pad_maximum_fusion.1), channel_id=1, source_target_pairs={{0,6},{2,0},{4,2},{6,4},{1,7},{3,1},{5,3},{7,5},{8,14},{10,8},{12,... | collective-permute-start | bytes 614408 | tf_op jit(solution)/shard_map/ppermute | solution.py:314
  123.1 5.4 %collective-permute-start.16 = (bf16[400,256]{1,0:T(8,128)(2,1)S(1)}, bf16[400,256]{1,0:T(8,128)(2,1)}, u32[]{:S(2)}, u32[]{:S(2)}) collective-permute-start(bf16[400,256]{1,0:T(8,128)(2,1)S(1)} %pad_maximum_fusion.1), channel_id=1, source_target_pairs={{0,4},{2,6},{4,0},{6,2},{1,5},{3,7},{5,1},{7,3},{8,12},{10,14},{12... | collective-permute-start | bytes 614408 | tf_op jit(solution)/shard_map/ppermute | solution.py:314
  128.5 3.1 %collective-permute-start.15 = (bf16[400,256]{1,0:T(8,128)(2,1)S(1)}, bf16[400,256]{1,0:T(8,128)(2,1)}, u32[]{:S(2)}, u32[]{:S(2)}) collective-permute-start(bf16[400,256]{1,0:T(8,128)(2,1)S(1)} %pad_maximum_fusion.1), channel_id=1, source_target_pairs={{0,2},{2,4},{4,6},{6,0},{1,3},{3,5},{5,7},{7,1},{8,10},{10,12},{12... | collective-permute-start | bytes 614408 | tf_op jit(solution)/shard_map/ppermute | solution.py:314
  132.5 12.1 %all-to-all-start.15 = ((bf16[4,256,128]{2,1,0:T(8,128)(2,1)}), bf16[4,256,128]{2,1,0:T(8,128)(2,1)S(1)}, u32[]{:S(2)}, u32[]{:S(2)}) async-start(bf16[4,256,128]{2,1,0:T(8,128)(2,1)} %shard_map.123), calls=%async_computation.15 | async-start | bytes 524288 | tf_op jit(solution)/shard_map/all_to_all | solution.py:311
  146.0 1.9 %collective-permute-start.18 = (bf16[384,512]{1,0:T(8,128)(2,1)S(1)}, bf16[384,512]{1,0:T(8,128)(2,1)S(1)}, u32[]{:S(2)}, u32[]{:S(2)}) collective-permute-start(bf16[384,512]{1,0:T(8,128)(2,1)S(1)} %pad_maximum_fusion), channel_id=1, source_target_pairs={{0,1},{1,0},{2,3},{3,2},{4,5},{5,4},{6,7},{7,6},{8,9},{9,8},{10,11... | collective-permute-start | bytes 1179656 | tf_op jit(solution)/shard_map/ppermute | solution.py:27
  149.3 9.6 %collective-permute-start.19 = (f32[768]{0:T(1024)S(1)}, f32[768]{0:T(1024)S(1)}, u32[]{:S(2)}, u32[]{:S(2)}) collective-permute-start(f32[768]{0:T(1024)S(1)} %add.158), channel_id=1, source_target_pairs={{0,8},{8,0},{1,9},{9,1},{2,10},{10,2},{3,11},{11,3},{4,12},{12,4},... | collective-permute-start | bytes 9224 | tf_op jit(solution)/shard_map/ppermute | solution.py:27
  159.0 4.6 %collective-permute-done.19 = f32[768]{0:T(1024)S(1)} collective-permute-done((f32[768]{0:T(1024)S(1)}, f32[768]{0:T(1024)S(1)}, u32[]{:S(2)}, u32[]{:S(2)}) %collective-permute-start.19) | collective-permute-done | bytes 3104 | tf_op jit(solution)/shard_map/ppermute | solution.py:27
  (85 shorter events, 26.8 us)
Async XLA Ops:
  0.6 3.5 %copy-start = (bf16[1,3072,256]{2,1,0:T(8,128)(2,1)S(1)}, bf16[1,3072,256]{2,1,0:T(8,128)(2,1)}, u32[]{:S(2)}) copy-start(bf16[1,3072,256]{2,1,0:T(8,128)(2,1)} %param.20) | copy-start | bytes 4718596
  4.1 3.6 %copy-start.14 = (s32[1,768]{1,0:T(1,128)S(1)}, s32[1,768]{1,0:T(1,128)}, u32[]{:S(2)}) copy-start(s32[1,768]{1,0:T(1,128)} %row_ref.1) | copy-start | bytes 9220
  4.1 3.6 %copy-start.15 = (f32[1,768]{1,0:T(1,128)S(1)}, f32[1,768]{1,0:T(1,128)}, u32[]{:S(2)}) copy-start(f32[1,768]{1,0:T(1,128)} %logit_ref.1) | copy-start | bytes 9220
  4.2 3.6 %copy-start.16 = (bf16[1,768,256]{2,1,0:T(8,128)(2,1)S(1)}, bf16[1,768,256]{2,1,0:T(8,128)(2,1)}, u32[]{:S(2)}) copy-start(bf16[1,768,256]{2,1,0:T(8,128)(2,1)} %param.24) | copy-start | bytes 1179652
  4.2 3.6 %copy-start.17 = (bf16[1,768,256]{2,1,0:T(8,128)(2,1)S(1)}, bf16[1,768,256]{2,1,0:T(8,128)(2,1)}, u32[]{:S(2)}) copy-start(bf16[1,768,256]{2,1,0:T(8,128)(2,1)} %param.25) | copy-start | bytes 1179652
  9.3 20.7 %copy-start.27 = (bf16[768,256]{1,0:T(8,128)(2,1)S(1)}, bf16[768,256]{1,0:T(8,128)(2,1)}, u32[]{:S(2)}) copy-start(bf16[768,256]{1,0:T(8,128)(2,1)} %get-tuple-element.262.v_ref) | copy-start | bytes 1179652 | tf_op jit(solution)/shard_map/cond
  9.3 32.9 %all-to-all-start.9 = ((bf16[4,768,256]{2,1,0:T(8,128)(2,1)}), bf16[4,768,256]{2,1,0:T(8,128)(2,1)}, u32[]{:S(2)}, u32[]{:S(2)}) async-start(bf16[4,768,256]{2,1,0:T(8,128)(2,1)} %broadcast_in_dim.125), calls=%async_computation.9 | async-start | bytes 3145728 | tf_op jit(solution)/shard_map/cond/branch_9_fun/all_to_all | solution.py:31
  19.6 22.5 %collective-permute-start.9 = (bf16[640,256]{1,0:T(8,128)(2,1)S(1)}, bf16[640,256]{1,0:T(8,128)(2,1)S(1)}, u32[]{:S(2)}, u32[]{:S(2)}) collective-permute-start(bf16[640,256]{1,0:T(8,128)(2,1)S(1)} %slice.107), channel_id=1, source_target_pairs={{0,8},{8,0},{1,9},{9,1},{2,10},{10,2},{3,11},{11,3},{4,12},{12,4},... | collective-permute-start | bytes 983048 | tf_op jit(solution)/shard_map/cond/branch_9_fun/ppermute | solution.py:27
  42.3 1.9 %copy-start.13 = (bf16[4,768,256]{2,1,0:T(8,128)(2,1)}, bf16[4,768,256]{2,1,0:T(8,128)(2,1)S(1)}, u32[]{:S(2)}) copy-start(bf16[4,768,256]{2,1,0:T(8,128)(2,1)S(1)} %get-tuple-element.317) | copy-start | bytes 4718596
  42.3 6.8 %collective-permute-start.12 = (bf16[4,768,256]{2,1,0:T(8,128)(2,1)}, bf16[4,768,256]{2,1,0:T(8,128)(2,1)}, u32[]{:S(2)}, u32[]{:S(2)}) collective-permute-start(bf16[4,768,256]{2,1,0:T(8,128)(2,1)} %get-tuple-element.318.near_ref), channel_id=1, source_target_pairs={{0,1},{1,0},{2,3},{3,2},{4,5},{5,4},{6,7},{7,6},{8,9},{9,8},{10,11... | collective-permute-start | bytes 4718600 | tf_op jit(solution)/shard_map/ppermute | solution.py:27
  44.2 24.1 %all-to-all-start.12 = ((bf16[4,768,256]{2,1,0:T(8,128)(2,1)}), bf16[4,768,256]{2,1,0:T(8,128)(2,1)S(1)}, u32[]{:S(2)}, u32[]{:S(2)}) async-start(bf16[4,768,256]{2,1,0:T(8,128)(2,1)} %copy-done.13), calls=%async_computation.12 | async-start | bytes 3145728 | tf_op jit(solution)/shard_map/all_to_all | solution.py:31
  49.1 1.6 copy-start.7
  69.5 29.9 %all-to-all-start.13 = ((bf16[8,2,256,128]{3,2,1,0:T(8,128)(2,1)}), bf16[8,2,256,128]{3,2,1,0:T(8,128)(2,1)S(1)}, u32[]{:S(2)}, u32[]{:S(2)}) async-start(bf16[8,2,256,128]{3,2,1,0:T(8,128)(2,1)} %bitcast.22), calls=%async_computation.13 | async-start | bytes 2097152 | tf_op jit(solution)/shard_map/all_to_all | solution.py:258
  81.0 5.6 %collective-permute-start.13 = (bf16[4,768,256]{2,1,0:T(8,128)(2,1)}, bf16[4,768,256]{2,1,0:T(8,128)(2,1)}, u32[]{:S(2)}, u32[]{:S(2)}) collective-permute-start(bf16[4,768,256]{2,1,0:T(8,128)(2,1)} %copy-done.3), channel_id=1, source_target_pairs={{0,1},{1,0},{2,3},{3,2},{4,5},{5,4},{6,7},{7,6},{8,9},{9,8},{10,11... | collective-permute-start | bytes 4718600 | tf_op jit(solution)/shard_map/ppermute | solution.py:27
  86.7 1.4 copy-start.4
  88.1 1.6 copy-start.8
  100.3 20.8 %all-to-all-start.14 = ((bf16[8,2,256,128]{3,2,1,0:T(8,128)(2,1)}), bf16[8,2,256,128]{3,2,1,0:T(8,128)(2,1)S(1)}, u32[]{:S(2)}, u32[]{:S(2)}) async-start(bf16[8,2,256,128]{3,2,1,0:T(8,128)(2,1)} %bitcast.21), calls=%async_computation.14 | async-start | bytes 2097152 | tf_op jit(solution)/shard_map/all_to_all | solution.py:258
  116.7 4.1 %collective-permute-start.14 = (bf16[400,256]{1,0:T(8,128)(2,1)S(1)}, bf16[400,256]{1,0:T(8,128)(2,1)S(1)}, u32[]{:S(2)}, u32[]{:S(2)}) collective-permute-start(bf16[400,256]{1,0:T(8,128)(2,1)S(1)} %get-tuple-element.332), channel_id=1, source_target_pairs={{0,1},{1,0},{2,3},{3,2},{4,5},{5,4},{6,7},{7,6},{8,9},{9,8},{10,11... | collective-permute-start | bytes 614408 | tf_op jit(solution)/shard_map/ppermute | solution.py:27
  121.1 23.4 %collective-permute-start.17 = (bf16[400,256]{1,0:T(8,128)(2,1)S(1)}, bf16[400,256]{1,0:T(8,128)(2,1)S(1)}, u32[]{:S(2)}, u32[]{:S(2)}) collective-permute-start(bf16[400,256]{1,0:T(8,128)(2,1)S(1)} %pad_maximum_fusion.1), channel_id=1, source_target_pairs={{0,6},{2,0},{4,2},{6,4},{1,7},{3,1},{5,3},{7,5},{8,14},{10,8},{12,... | collective-permute-start | bytes 614408 | tf_op jit(solution)/shard_map/ppermute | solution.py:314
  123.1 21.5 %collective-permute-start.16 = (bf16[400,256]{1,0:T(8,128)(2,1)S(1)}, bf16[400,256]{1,0:T(8,128)(2,1)}, u32[]{:S(2)}, u32[]{:S(2)}) collective-permute-start(bf16[400,256]{1,0:T(8,128)(2,1)S(1)} %pad_maximum_fusion.1), channel_id=1, source_target_pairs={{0,4},{2,6},{4,0},{6,2},{1,5},{3,7},{5,1},{7,3},{8,12},{10,14},{12... | collective-permute-start | bytes 614408 | tf_op jit(solution)/shard_map/ppermute | solution.py:314
  128.5 16.1 %collective-permute-start.15 = (bf16[400,256]{1,0:T(8,128)(2,1)S(1)}, bf16[400,256]{1,0:T(8,128)(2,1)}, u32[]{:S(2)}, u32[]{:S(2)}) collective-permute-start(bf16[400,256]{1,0:T(8,128)(2,1)S(1)} %pad_maximum_fusion.1), channel_id=1, source_target_pairs={{0,2},{2,4},{4,6},{6,0},{1,3},{3,5},{5,7},{7,1},{8,10},{10,12},{12... | collective-permute-start | bytes 614408 | tf_op jit(solution)/shard_map/ppermute | solution.py:314
  132.5 32.9 %all-to-all-start.15 = ((bf16[4,256,128]{2,1,0:T(8,128)(2,1)}), bf16[4,256,128]{2,1,0:T(8,128)(2,1)S(1)}, u32[]{:S(2)}, u32[]{:S(2)}) async-start(bf16[4,256,128]{2,1,0:T(8,128)(2,1)} %shard_map.123), calls=%async_computation.15 | async-start | bytes 524288 | tf_op jit(solution)/shard_map/all_to_all | solution.py:311
  146.0 18.1 %collective-permute-start.18 = (bf16[384,512]{1,0:T(8,128)(2,1)S(1)}, bf16[384,512]{1,0:T(8,128)(2,1)S(1)}, u32[]{:S(2)}, u32[]{:S(2)}) collective-permute-start(bf16[384,512]{1,0:T(8,128)(2,1)S(1)} %pad_maximum_fusion), channel_id=1, source_target_pairs={{0,1},{1,0},{2,3},{3,2},{4,5},{5,4},{6,7},{7,6},{8,9},{9,8},{10,11... | collective-permute-start | bytes 1179656 | tf_op jit(solution)/shard_map/ppermute | solution.py:27
  149.3 14.2 %collective-permute-start.19 = (f32[768]{0:T(1024)S(1)}, f32[768]{0:T(1024)S(1)}, u32[]{:S(2)}, u32[]{:S(2)}) collective-permute-start(f32[768]{0:T(1024)S(1)} %add.158), channel_id=1, source_target_pairs={{0,8},{8,0},{1,9},{9,1},{2,10},{10,2},{3,11},{11,3},{4,12},{12,4},... | collective-permute-start | bytes 9224 | tf_op jit(solution)/shard_map/ppermute | solution.py:27
  (9 other events, 9.4 us)

commit v5 on v4

v5 whole, which is shorter than its diff:
```python
import functools

import jax
import jax.numpy as jnp
from jax import lax
from jax.experimental import pallas as pl
from jax.experimental.pallas import tpu as pltpu
from jax.sharding import Mesh
from jax.sharding import PartitionSpec as P

HEAD_SIZE = 128
ZQ, ZP, Y, ZH, X, CORE = 4, 2, 4, 2, 4, 2
SLOTS, WIDE, HEADS = 768, 256, 2
SCALE = HEAD_SIZE ** (-0.5)
BF, F32 = jnp.bfloat16, jnp.float32
ROWS = 256
STEP = 64
PAD_COST = 10**6
CHUNK = 128
CHUNKS = range(0, SLOTS, CHUNK)
HALF, EXTRA = SLOTS // 2, 16
LIMIT = pltpu.CompilerParams(vmem_limit_bytes=60 * 1024 * 1024)
SMALL = pltpu.CompilerParams(vmem_limit_bytes=16 * 1024 * 1024)


def ring(n, k):
    return [(i, (i + k) % n) for i in range(n)]


def swap(value, axis):
    return lax.ppermute(value, axis, ring(2, 1))


def spread_x(copies):
    return lax.all_to_all(copies, "x", 0, 0, tiled=True)


def repeated(block):
    return jnp.broadcast_to(block[None], (X,) + block.shape)


def pad_kernel(rows_ref, out_ref):
    rows = rows_ref.shape[0]
    out_ref[:rows] = rows_ref[...]
    if rows < SLOTS:
        out_ref[rows:] = jnp.zeros((SLOTS - rows, WIDE), BF)


def padded(rows):
    return pl.pallas_call(
        pad_kernel,
        out_shape=shape_of((SLOTS, WIDE), BF),
        compiler_params=SMALL,
        cost_estimate=pl.CostEstimate(flops=PAD_COST, bytes_accessed=10**6, transcendentals=0),
    )(rows)


def exchange(rows, picked, attention):
    other = padded(swap(picked[:rows], "zh"))
    near = spread_x(repeated(picked))
    return other, near, forward(*attention)


def rows_dot(a, b):
    return lax.dot_general(a, b, (((1,), (1,)), ((), ())), preferred_element_type=F32)


def column(row):
    parts = [
        jnp.broadcast_to(row[:, a : a + 128], (128, 128)).T for a in range(0, row.shape[1], 128)
    ]
    return jnp.concatenate(parts, axis=0)[:, :1]


def key_positions(info_ref, pos_row):
    j = lax.broadcasted_iota(jnp.int32, (1, SLOTS), 1)
    return jnp.broadcast_to(column(jnp.where(j < info_ref[1], pos_row, 1 << 20)), (SLOTS, ROWS))


def allowed_block(key_ref, pos_ref, first):
    shape = (CHUNK, ROWS)
    ahead = lax.broadcasted_iota(jnp.int32, shape, 0) - lax.broadcasted_iota(jnp.int32, shape, 1)
    same = ahead == pl.program_id(0) * ROWS - first
    return (key_ref[first : first + CHUNK, :] <= pos_ref[...]) | same


def forward_kernel(
    info_ref, q_ref, k_ref, v_ref, pos_ref, row_ref, logit_ref,
    att_ref, scaled_ref, lse_ref, key_ref, vt_ref,
):
    @pl.when(pl.program_id(0) == 0)
    def _():
        key_ref[...] = key_positions(info_ref, row_ref[...])
        vt_ref[...] = v_ref[...].astype(F32).T.astype(BF)

    weight = 1.0 / (1.0 + jnp.exp(-logit_ref[...]))
    allowed = [allowed_block(key_ref, pos_ref, c) for c in CHUNKS]
    for h in range(HEADS):
        lanes = slice(h * HEAD_SIZE, (h + 1) * HEAD_SIZE)
        q = q_ref[:, lanes]
        s = [
            jnp.where(seen, rows_dot(k_ref[c : c + CHUNK, :], q) * SCALE, -1e30)
            for c, seen in zip(CHUNKS, allowed)
        ]
        top = functools.reduce(jnp.maximum, [jnp.max(t, axis=0, keepdims=True) for t in s])
        e = [jnp.exp(t - top) for t in s]
        total = sum(jnp.sum(t, axis=0, keepdims=True) for t in e)
        scale = 1.0 / total
        p = jnp.concatenate([(t * scale).astype(BF) for t in e], 0)
        att = jnp.dot(vt_ref[...], p, preferred_element_type=F32).astype(BF).astype(F32)
        att_ref[:, lanes] = att.T.astype(BF)
        scaled_ref[lanes, :] = (weight * att).astype(BF)
        lse_ref[h : h + 1, :] = top + jnp.log(total)


def backward_kernel(
    info_ref, q_ref, k_ref, v_ref, pos_ref, row_ref, logit_ref, lse_ref, att_ref, go_ref,
    gq_ref, kept_ref, sent_ref, sum_ref, terms_ref, key_ref, kt_ref,
):
    step = pl.program_id(0)

    @pl.when(step == 0)
    def _():
        sum_ref[...] = jnp.zeros_like(sum_ref)
        terms_ref[...] = jnp.zeros_like(terms_ref)
        key_ref[...] = key_positions(info_ref, row_ref[...])
        kt_ref[...] = k_ref[...].astype(F32).T.astype(BF)

    allowed = [allowed_block(key_ref, pos_ref, c) for c in CHUNKS]
    weight = 1.0 / (1.0 + jnp.exp(-column(logit_ref[...])))
    grad_o = go_ref[...]
    grad_attn = (weight * grad_o).astype(BF)
    router = jnp.sum(grad_o * att_ref[...].astype(F32), axis=1, keepdims=True)
    router = jnp.broadcast_to(router, (ROWS, 128)).T[:1]
    lead = router.astype(BF).astype(F32)
    terms_ref[pl.ds(step, 1), :] = lead
    terms_ref[pl.ds(step + SLOTS // ROWS, 1), :] = router - lead
    for h in range(HEADS):
        lanes = slice(h * HEAD_SIZE, (h + 1) * HEAD_SIZE)
        q = q_ref[:, lanes]
        ga = grad_attn[:, lanes]
        lse = lse_ref[h : h + 1, :]
        p, gp, delta = [], [], jnp.zeros((1, ROWS), F32)
        for c, seen in zip(CHUNKS, allowed):
            s = rows_dot(k_ref[c : c + CHUNK, :], q) * SCALE
            p.append(jnp.exp(jnp.where(seen, s - lse, -1e30)))
            gp.append(rows_dot(v_ref[c : c + CHUNK, :], ga))
            delta = delta + jnp.sum(p[-1] * gp[-1], axis=0, keepdims=True)
        gs = [(a * (b - delta)).astype(BF) for a, b in zip(p, gp)]
        for c, a, b in zip(CHUNKS, gs, p):
            rows = slice(c, c + CHUNK)
            sum_ref[rows, :HEAD_SIZE] += jnp.dot(a, q, preferred_element_type=F32)
            sum_ref[rows, HEAD_SIZE:] += jnp.dot(b.astype(BF), ga, preferred_element_type=F32)
        gs = jnp.concatenate(gs, 0)
        gq = jnp.dot(kt_ref[...], gs, preferred_element_type=F32) * SCALE
        gq_ref[:, lanes] = gq.T.astype(BF)

    @pl.when(step == pl.num_programs(0) - 1)
    def _():
        core = info_ref[2]
        for ref, side in ((kept_ref, core), (sent_ref, 1 - core)):
            rows = pl.ds(pl.multiple_of(side * HALF, HALF), HALF)
            ref[:HALF, :HEAD_SIZE] = (sum_ref[rows, :HEAD_SIZE] * SCALE).astype(BF)
            ref[:HALF, HEAD_SIZE:] = sum_ref[rows, HEAD_SIZE:].astype(BF)
            ref[HALF:, :] = terms_ref[...].astype(BF)


def by_rows(width):
    return pl.BlockSpec((ROWS, width), lambda i, info: (i, 0))


def row_part():
    return pl.BlockSpec((1, ROWS), lambda i, info: (0, i))


def by_heads():
    return pl.BlockSpec((HEADS, ROWS), lambda i, info: (0, i))


def by_group():
    return pl.BlockSpec((SLOTS, HEAD_SIZE), lambda i, info: (0, info[0]))


def whole(shape):
    return pl.BlockSpec(shape, lambda i, info: (0,) * len(shape))


def shape_of(shape, dtype):
    return jax.ShapeDtypeStruct(shape, dtype)


def forward(info, q, k, v, pos_col, pos_row, logit_col):
    return pl.pallas_call(
        forward_kernel,
        grid_spec=pltpu.PrefetchScalarGridSpec(
            num_scalar_prefetch=1,
            grid=(SLOTS // ROWS,),
            in_specs=[by_rows(WIDE), by_group(), by_group(), row_part(), whole((1, SLOTS)), row_part()],
            out_specs=[by_rows(WIDE), pl.BlockSpec((WIDE, ROWS), lambda i, info: (0, i)), by_heads()],
            scratch_shapes=[pltpu.VMEM((SLOTS, ROWS), jnp.int32), pltpu.VMEM((HEAD_SIZE, SLOTS), BF)],
        ),
        out_shape=[shape_of((SLOTS, WIDE), BF), shape_of((WIDE, SLOTS), BF), shape_of((HEADS, SLOTS), F32)],
        compiler_params=SMALL,
        cost_estimate=pl.CostEstimate(flops=4 * 10**9, bytes_accessed=2 * 10**6, transcendentals=1200000),
    )(info, q, k, v, pos_col, pos_row, logit_col)


def backward(info, q, k, v, pos_col, pos_row, logit_col, lse, att, grad_o):
    return pl.pallas_call(
        backward_kernel,
        grid_spec=pltpu.PrefetchScalarGridSpec(
            num_scalar_prefetch=1,
            grid=(SLOTS // ROWS,),
            in_specs=[
                by_rows(WIDE), by_group(), by_group(), row_part(), whole((1, SLOTS)), row_part(),
                by_heads(), by_rows(WIDE), by_rows(WIDE),
            ],
            out_specs=[by_rows(WIDE), whole((HALF + EXTRA, WIDE)), whole((HALF + EXTRA, WIDE))],
            scratch_shapes=[
                pltpu.VMEM((SLOTS, WIDE), F32), pltpu.VMEM((EXTRA, WIDE), F32),
                pltpu.VMEM((SLOTS, ROWS), jnp.int32), pltpu.VMEM((HEAD_SIZE, SLOTS), BF),
            ],
        ),
        out_shape=[
            shape_of((SLOTS, WIDE), BF), shape_of((HALF + EXTRA, WIDE), BF),
            shape_of((HALF + EXTRA, WIDE), BF),
        ],
        compiler_params=LIMIT,
        cost_estimate=pl.CostEstimate(flops=7 * 10**9, bytes_accessed=4 * 10**6, transcendentals=1200000),
    )(info, q, k, v, pos_col, pos_row, logit_col, lse, att, grad_o)


def products_kernel(info_ref, near_ref, far_ref, wn_ref, wf_ref, scaled_ref, *refs):
    go_ref, wg_ref = refs[-2:]
    core = info_ref[0]
    near, far = near_ref[0], far_ref[0]
    first = pl.program_id(0) == 0

    @pl.when(first)
    def _():
        go_ref[...] = refs[0][...] if len(refs) == 3 else jnp.zeros_like(go_ref)

    w = jnp.concatenate([wn_ref[0], wf_ref[0]], 0)
    for r in range(0, SLOTS, 128):
        rows = slice(r, r + 128)
        both = jnp.concatenate([near_ref[0, rows], far_ref[0, rows]], 1)
        go_ref[rows] += jnp.dot(both, w, preferred_element_type=F32)

    for shard, y in ((near, 2 * core), (far, 2 - 2 * core)):
        grad = jnp.dot(scaled_ref[...], shard, preferred_element_type=F32).astype(BF)
        wg_ref[0, y, 0] = grad[:, :128]
        wg_ref[0, y + 1, 0] = grad[:, 128:]


def products(core, half, base, turn, near, far, w_out, scaled_t, begin=None):
    info = jnp.stack([core, half, base, turn]).astype(jnp.int32)
    more = [] if begin is None else [begin]
    shard = pl.BlockSpec((1, SLOTS, WIDE), lambda i, info: (i, 0, 0))
    at = lambda i, info: (info[2] + info[3] * i) % X
    w_near = pl.BlockSpec((1, WIDE, WIDE), lambda i, info: (info[1] * 8 + at(i, info) * 2 + info[0], 0, 0))
    w_far = pl.BlockSpec((1, WIDE, WIDE), lambda i, info: (info[1] * 8 + at(i, info) * 2 + 1 - info[0], 0, 0))
    w_parts = w_out.reshape(ZH * X * CORE, WIDE, WIDE)
    return pl.pallas_call(
        products_kernel,
        grid_spec=pltpu.PrefetchScalarGridSpec(
            num_scalar_prefetch=1,
            grid=(X,),
            in_specs=[shard, shard, w_near, w_far, whole((WIDE, SLOTS))]
            + [whole((SLOTS, WIDE)) for _ in more],
            out_specs=[
                whole((SLOTS, WIDE)),
                pl.BlockSpec((1, Y, 1, WIDE, 128), lambda i, info: (at(i, info) % 2, 0, at(i, info) // 2, 0, 0)),
            ],
        ),
        out_shape=[shape_of((SLOTS, WIDE), F32), shape_of((ZP, Y, 2, WIDE, 128), BF)],
        compiler_params=LIMIT,
        cost_estimate=pl.CostEstimate(flops=2 * 10**10, bytes_accessed=8 * 10**6, transcendentals=0),
    )(info, near, far, w_parts, w_parts, scaled_t, *more)


def fold_kernel(info_ref, moved_ref, *refs):
    refs[-1][0] = jnp.sum(moved_ref[...].astype(F32), axis=0)[0].astype(BF)


def fold(half, moved, begin=None):
    more = [] if begin is None else [begin]
    return pl.pallas_call(
        fold_kernel,
        grid_spec=pltpu.PrefetchScalarGridSpec(
            num_scalar_prefetch=1,
            grid=(2,),
            in_specs=[pl.BlockSpec((ZP * Y, 1, WIDE, 128), lambda i, info: (0, i, 0, 0))]
            + [pl.BlockSpec(memory_space=pl.ANY) for _ in more],
            out_specs=pl.BlockSpec((1, WIDE, 128), lambda i, info: (info[0] * 2 + i, 0, 0)),
        ),
        out_shape=shape_of((ZQ, WIDE, 128), BF),
        input_output_aliases={2: 0} if more else {},
        compiler_params=SMALL,
        cost_estimate=pl.CostEstimate(flops=1 * 10**6, bytes_accessed=2 * 10**6, transcendentals=0),
    )(half.astype(jnp.int32).reshape(1), moved, *more)


def over_zp_y(blocks):
    blocks = blocks.reshape(ZP * Y, 2, WIDE, 128)
    return lax.all_to_all(blocks, ("zp", "y"), 0, 0, tiled=True)


def per_device(cotangent, routed, counts, logits, query_rows, key_rows, routed_value_rows, w_out):
    zh, x, core = lax.axis_index("zh"), lax.axis_index("x"), lax.axis_index("core")
    dp_index = (lax.axis_index("zq") * ZP + lax.axis_index("zp")) * Y + lax.axis_index("y")
    own = jnp.arange(counts.shape[0], dtype=jnp.int32) == dp_index
    own_count = jnp.sum(jnp.where(own, counts, 0))
    positions = routed[0]
    picked = cotangent[0].at[positions].get(mode="promise_in_bounds", wrap_negative_indices=False)
    live = jnp.arange(SLOTS, dtype=jnp.int32) < own_count
    picked = lax.optimization_barrier(jnp.where(live[:, None], picked, jnp.zeros((), BF)))

    info = jnp.stack([x // 2, own_count, core]).astype(jnp.int32)
    attention = (
        info, query_rows[0], key_rows[0], routed_value_rows[0],
        routed, routed, logits,
    )
    sizes = range(STEP, SLOTS + 1, STEP)
    branch = jnp.maximum(own_count - 1, 0) // STEP
    other, own_near, (attended, scaled_t, lse) = lax.switch(
        branch, [functools.partial(exchange, rows) for rows in sizes], picked, attention
    )
    other_near = jnp.stack([other] + [lax.ppermute(other, "x", ring(X, k)) for k in range(1, X)])
    own_far = swap(own_near, "core")
    begun, w_grad_own = products(core, zh, 0, 1, own_near, own_far, w_out, scaled_t)

    other_near, begun = lax.optimization_barrier((other_near, begun))
    other_far = swap(other_near, "core")
    moved_own = over_zp_y(w_grad_own)
    grad_o, w_grad_other = products(core, 1 - zh, x, 3, other_near, other_far, w_out, scaled_t, begun)

    moved_own, grad_o, w_grad_other = lax.optimization_barrier((moved_own, grad_o, w_grad_other))
    moved_other = over_zp_y(w_grad_other)
    blocks = fold(zh, moved_own)
    grad_q, kept, sent = backward(*attention, lse, attended, grad_o)
    came = swap(sent, "core")
    chip = (kept.astype(F32) + came.astype(F32)).astype(BF)

    moved_other, blocks, chip = lax.optimization_barrier((moved_other, blocks, chip))
    pair = lax.ppermute(chip, "x", [(0, 1), (1, 0), (2, 3), (3, 2)])
    blocks = fold(1 - zh, moved_other, blocks)
    pair, blocks = lax.optimization_barrier((pair, blocks))
    final = lax.all_to_all(blocks, "zq", 0, 0, tiled=True)
    w_grad = jnp.sum(final.astype(F32), axis=0).T.astype(BF)

    group = (chip.astype(F32) + pair.astype(F32)).astype(BF)
    apart = lax.ppermute(group, "x", [(0, 3), (3, 0), (1, 2), (2, 1)])
    router = group[HALF:].astype(F32) + apart[HALF:].astype(F32)
    router = (router[: SLOTS // WIDE] + router[SLOTS // WIDE : 2 * SLOTS // WIDE]).reshape(SLOTS)
    first = jnp.where(x < 2, group, apart)[:HALF]
    second = jnp.where(x < 2, apart, group)[:HALF]
    joined = jnp.concatenate(
        [first[:, :HEAD_SIZE], second[:, :HEAD_SIZE], first[:, HEAD_SIZE:], second[:, HEAD_SIZE:]], 1
    )
    theirs = swap(joined, "core")
    router = router + swap(router, "zh")
    rows = jnp.where(
        core == 0, jnp.concatenate([joined, theirs], 0), jnp.concatenate([theirs, joined], 0)
    )
    key_total, value_total = rows[:, : 2 * HEAD_SIZE], rows[:, 2 * HEAD_SIZE :]
    router_weight = jax.nn.sigmoid(logits[0])
    grad_logits = router * router_weight * (1.0 - router_weight)
    return (grad_q[None], key_total[None], value_total[None], w_grad, grad_logits[None])


def solution(mesh):
    fine = Mesh(mesh.devices.reshape(ZQ, ZP, Y, ZH, X, CORE), ("zq", "zp", "y", "zh", "x", "core"))
    dp, col = ("zq", "zp", "y"), ("x", "core")
    row_col = ("zh",) + col
    placed = (
        P(dp, None, row_col),
        P(dp, None),
        P(),
        P(dp, None),
        P(dp, None, row_col),
        P(dp, None, "zh"),
        P(dp, None, "zh"),
        P(None, row_col),
    )
    return jax.shard_map(
        per_device,
        mesh=fine,
        in_specs=placed,
        out_specs=(
            P(dp, None, row_col),
            P(dp, None, "zh"),
            P(dp, None, "zh"),
            P(dp, row_col),
            P(dp, None),
        ),
        check_vma=False,
    )
```

time: 168 us -> 157 us (0.935)
  local copies, waits for them, and re-layouts: 20.4 us -> 7.28 us
  starting transfers between devices: 82.5 us -> 85.8 us
  waiting for transfers between devices: 23.4 us -> 21 us
  other arithmetic: 7.01 us -> 8.8 us
    unnamed x37 -> x15, local copies, waits for them, and re-layouts: 14.8 us -> 0.79 us
    all_to_all x2 -> x1, waiting for transfers between devices: 8.92 us -> 0.01 us  [spread_x(): return lax.all_to_all(copies, 'x', 0, 0, tiled=True)]
    ppermute x3 -> x5, starting transfers between devices: 10.4 us -> 17.2 us  [the longest x3 10 us: per_device(): lax.ppermute(other, 'x', ring(X, k))]
    all_to_all x2 -> x1, starting transfers between devices: 15.1 us -> 10.3 us  [spread_x(): return lax.all_to_all(copies, 'x', 0, 0, tiled=True)]
    ppermute x3 -> x5, waiting for transfers between devices: 0.01 us -> 3.96 us  [the longest x1 3.95 us: per_device(): pair = lax.ppermute(chip, 'x', [(0, 1), (1, 0), (2, 3), (3, 2)])]
    all_to_all x2, starting transfers between devices: 17.3 us -> 21.1 us  [over_zp_y(): return lax.all_to_all(blocks, ('zp', 'y'), 0, 0, tiled=True)]
    another operation x4 -> x3, other arithmetic: 1.43 us -> 3.64 us  [the longest x1 2.45 us: per_device(): jnp.stack([other] + [lax.ppermute(other, 'x', ring(X, k)) for k in range(...]
  transfers between devices with their start and end apart: 14 -> 15, of which waited for: 5 -> 6; matrix products, arithmetic and copies ran while one was open for 3% -> 5% of each run, Pallas kernels for 19% -> 20%
where the time goes in v5:
time: 157 us; the launch traced here: 156 us
  starting transfers between devices  85.8 us (55%)
  Pallas kernels  31.1 us (20%)
  waiting for transfers between devices  21 us (13%)
  other arithmetic  8.8 us (6%)
  local copies, waits for them, and re-layouts  7.28 us (5%)
  between operations  1.64 us (1%)
    ppermute x6, starting transfers between devices, swap(): return lax.ppermute(value, axis, ring(2, 1))  26.2 us
    all_to_all x2, starting transfers between devices, over_zp_y(): return lax.all_to_all(blocks, ('zp', 'y'), 0, 0, tiled=True)  21.1 us
    ppermute x6, waiting for transfers between devices, swap(): return lax.ppermute(value, axis, ring(2, 1))  15.1 us
    pallas_call x2, Pallas kernels, products(): pl.pallas_call(products_kernel, grid_spec=pltpu.PrefetchScalarGridSpec(nu...  13 us
    all_to_all x1, starting transfers between devices, per_device(): final = lax.all_to_all(blocks, 'zq', 0, 0, tiled=True)  10.9 us
    all_to_all x1, starting transfers between devices, spread_x(): return lax.all_to_all(copies, 'x', 0, 0, tiled=True)  10.3 us
    ppermute x3, starting transfers between devices, per_device(): lax.ppermute(other, 'x', ring(X, k))  10 us
    pallas_call x1, Pallas kernels, backward(): pl.pallas_call(backward_kernel, grid_spec=pltpu.PrefetchScalarGridSpec(nu...  8.79 us
  transfers between devices with their start and end apart: 15, of which 6 were waited for; matrix products, arithmetic and copies ran while one was open for 5% of the time, Pallas kernels for 20%

profile of v5, /device:TPU:6, one launch (start us, length us, event | category | flops | bytes accessed | tf_op | source)
XLA Modules:
  0.0 155.8 jit_solution(11709148906913069430)
XLA Ops:
  4.2 2.7 %gather_fusion = bf16[768,256]{1,0:T(8,128)(2,1)S(1)} fusion(bf16[3072,256]{1,0:T(8,128)(2,1)S(1)} %bitcast.34, s32[1024]{0:T(1024)S(1)} %pad_clamp_fusion), kind=kCustom, calls=%fused_computation | custom fusion | bytes 789504 | tf_op jit(solution)/shard_map/gather | solution.py:314
  7.8 34.9 %conditional.1 = (bf16[768,256]{1,0:T(8,128)(2,1)}, bf16[4,768,256]{2,1,0:T(8,128)(2,1)}, bf16[768,256]{1,0:T(8,128)(2,1)}, bf16[256,768]{1,0:T(8,128)(2,1)}, f3...) conditional(s32[]{:T(128)} %clamp.3, (bf16[768,256]{1,0:T(8,128)(2,1)S(1)}, ...), branch_computations={%region_1.2_spmd, %region_2.3_spmd, %region_3.4_spmd, %region_4.5_... | conditional | flops 4000999936 | bytes 14206804 | solution.py:325
  9.2 10.3 %all-to-all-start.7 = ((bf16[4,768,256]{2,1,0:T(8,128)(2,1)}), bf16[4,768,256]{2,1,0:T(8,128)(2,1)}, u32[]{:S(2)}, u32[]{:S(2)}) async-start(bf16[4,768,256]{2,1,0:T(8,128)(2,1)} %broadcast_in_dim.60), calls=%async_computation.7 | async-start | bytes 3145728 | tf_op jit(solution)/shard_map/cond/branch_7_fun/all_to_all | solution.py:35
  19.6 10.3 %collective-permute-start.7 = (bf16[512,256]{1,0:T(8,128)(2,1)S(1)}, bf16[512,256]{1,0:T(8,128)(2,1)S(1)}, u32[]{:S(2)}, u32[]{:S(2)}) collective-permute-start(bf16[512,256]{1,0:T(8,128)(2,1)S(1)} %slice.55), channel_id=1, source_target_pairs={{0,8},{8,0},{1,9},{9,1},{2,10},{10,2},{3,11},{11,3},{4,12},{12,4},... | collective-permute-start | bytes 786440 | tf_op jit(solution)/shard_map/cond/branch_7_fun/ppermute | solution.py:31
  29.9 5.7 %branch_7_fun.3 = (bf16[768,256]{1,0:T(8,128)(2,1)}, bf16[256,768]{1,0:T(8,128)(2,1)}, f32[2,768]{1,0:T(2,128)S(1)}) custom-call(s32[3]{0:T(128)S(1)} %get-tuple-element.240.info_ref, bf16[768,256]{1,0:T(8,128)(2,1)S(1)} %get-tuple-element.241.q_ref, bf16[768,256]{1,0:T(8,128)(2,1)S(1)} %get-tuple-element.242.k_ref, bf16[768,256]{1,0:T(8,128)(2,1)S(1)} %copy-done.14, ...), custom_call_target="tpu_custom_call" | custom-call | flops 4000000000 | bytes 2000000 | tf_op jit(solution)/shard_map/cond/branch_7_fun/pallas_call | solution.py:193
  35.6 5.3 %collective-permute-done.7.rows_ref = bf16[512,256]{1,0:T(8,128)(2,1)S(1)} collective-permute-done((bf16[512,256]{1,0:T(8,128)(2,1)S(1)}, bf16[512,256]{1,0:T(8,128)(2,1)S(1)}, u32[]{:S(2)}, u32[]{:S(2)}) %collective-permute-start.7) | collective-permute-done | bytes 262176 | tf_op jit(solution)/shard_map/cond/branch_7_fun/ppermute | solution.py:31
  44.6 2.8 %collective-permute-start.15 = (bf16[768,256]{1,0:T(8,128)(2,1)}, bf16[768,256]{1,0:T(8,128)(2,1)S(1)}, u32[]{:S(2)}, u32[]{:S(2)}) collective-permute-start(bf16[768,256]{1,0:T(8,128)(2,1)} %get-tuple-element.323), channel_id=1, source_target_pairs={{0,6},{2,0},{4,2},{6,4},{1,7},{3,1},{5,3},{7,5},{8,14},{10,8},{12,... | collective-permute-start | bytes 1179656 | tf_op jit(solution)/shard_map/ppermute | solution.py:328
  47.4 2.5 %collective-permute-start.14 = (bf16[768,256]{1,0:T(8,128)(2,1)}, bf16[768,256]{1,0:T(8,128)(2,1)}, u32[]{:S(2)}, u32[]{:S(2)}) collective-permute-start(bf16[768,256]{1,0:T(8,128)(2,1)} %get-tuple-element.323), channel_id=1, source_target_pairs={{0,4},{2,6},{4,0},{6,2},{1,5},{3,7},{5,1},{7,3},{8,12},{10,14},{12... | collective-permute-start | bytes 1179656 | tf_op jit(solution)/shard_map/ppermute | solution.py:328
  49.9 4.7 %collective-permute-start.13 = (bf16[768,256]{1,0:T(8,128)(2,1)}, bf16[768,256]{1,0:T(8,128)(2,1)}, u32[]{:S(2)}, u32[]{:S(2)}) collective-permute-start(bf16[768,256]{1,0:T(8,128)(2,1)} %get-tuple-element.323), channel_id=1, source_target_pairs={{0,2},{2,4},{4,6},{6,0},{1,3},{3,5},{5,7},{7,1},{8,10},{10,12},{12... | collective-permute-start | bytes 1179656 | tf_op jit(solution)/shard_map/ppermute | solution.py:328
  55.3 6.4 %shard_map.119 = (f32[768,256]{1,0:T(8,128)}, bf16[2,4,2,256,128]{4,3,2,1,0:T(8,128)(2,1)}) custom-call(s32[4]{0:T(128)} %pad_add_fusion.1.info_ref, bf16[4,768,256]{2,1,0:T(8,128)(2,1)} %get-tuple-element.319.near_ref, bf16[4,768,256]{2,1,0:T(8,128)(2,1)} %collective-permute-done.12.far_ref, bf16[16,256,256]{2,1,0:T(8,128)(2,1)} %bitcast.39, ...), custom_call_target="tpu_custom_call" | custom-call | flops 20000000000 | bytes 8000000 | tf_op jit(solution)/shard_map/pallas_call | solution.py:263
  61.7 12.2 %all-to-all-start.12 = ((bf16[8,2,256,128]{3,2,1,0:T(8,128)(2,1)}), bf16[8,2,256,128]{3,2,1,0:T(8,128)(2,1)S(1)}, u32[]{:S(2)}, u32[]{:S(2)}) async-start(bf16[8,2,256,128]{3,2,1,0:T(8,128)(2,1)} %bitcast.35), calls=%async_computation.12 | async-start | bytes 2097152 | tf_op jit(solution)/shard_map/all_to_all | solution.py:305
  73.8 2.4 %pad_maximum_fusion.near_ref = bf16[4,768,256]{2,1,0:T(8,128)(2,1)} fusion(bf16[1,768,256]{2,1,0:T(8,128)(2,1)S(1)} %bitcast.37, bf16[1,768,256]{2,1,0:T(8,128)(2,1)} %bitcast.25, bf16[1,768,256]{2,1,0:T(8,128)(2,1)} %bitcast.24, bf16[1,768,256]{2,1,0:T(8,128)(2,1)S(1)} %get-tuple-element.322), kind=kLoop, calls=%fused_computation.1 | loop fusion | flops 2359296 | bytes 3145728 | tf_op jit(solution)/shard_map/stack | solution.py:328
  78.8 3.1 %collective-permute-done.16.far_ref = bf16[4,768,256]{2,1,0:T(8,128)(2,1)} collective-permute-done((bf16[4,768,256]{2,1,0:T(8,128)(2,1)}, bf16[4,768,256]{2,1,0:T(8,128)(2,1)}, u32[]{:S(2)}, u32[]{:S(2)}) %collective-permute-start.16) | collective-permute-done | bytes 1572896 | tf_op jit(solution)/shard_map/ppermute | solution.py:31
  81.9 6.7 %shard_map.120 = (f32[768,256]{1,0:T(8,128)}, bf16[2,4,2,256,128]{4,3,2,1,0:T(8,128)(2,1)}) custom-call(s32[4]{0:T(128)} %pad_add_fusion.2.info_ref, bf16[4,768,256]{2,1,0:T(8,128)(2,1)} %pad_maximum_fusion.near_ref, bf16[4,768,256]{2,1,0:T(8,128)(2,1)} %collective-permute-done.16.far_ref, bf16[16,256,256]{2,1,0:T(8,128)(2,1)} %bitcast.41, ...), custom_call_target="tpu_custom_call" | custom-call | flops 20000000000 | bytes 8000000 | tf_op jit(solution)/shard_map/pallas_call | solution.py:263
  88.6 8.9 %all-to-all-start.13 = ((bf16[8,2,256,128]{3,2,1,0:T(8,128)(2,1)}), bf16[8,2,256,128]{3,2,1,0:T(8,128)(2,1)}, u32[]{:S(2)}, u32[]{:S(2)}) async-start(bf16[8,2,256,128]{3,2,1,0:T(8,128)(2,1)} %bitcast.36), calls=%async_computation.13 | async-start | bytes 2097152 | tf_op jit(solution)/shard_map/all_to_all | solution.py:305
  97.5 8.8 %shard_map.121 = (bf16[768,256]{1,0:T(8,128)(2,1)}, bf16[400,256]{1,0:T(8,128)(2,1)}, bf16[400,256]{1,0:T(8,128)(2,1)}) custom-call(s32[3]{0:T(128)S(1)} %pad_add_fusion.info_ref, bf16[768,256]{1,0:T(8,128)(2,1)S(1)} %bitcast.55, bf16[768,256]{1,0:T(8,128)(2,1)S(1)} %bitcast.68, bf16[768,256]{1,0:T(8,128)(2,1)} %bitcast.81, s32[1,768]{1,0:T(1,128)S(1)} %copy-done.2, ...), custom_call_target="tpu_custom_call" | custom-call | flops 7000000000 | bytes 4000000 | tf_op jit(solution)/shard_map/pallas_call | solution.py:209
  112.7 2.7 %collective-permute-start.18 = (bf16[400,256]{1,0:T(8,128)(2,1)S(1)}, bf16[400,256]{1,0:T(8,128)(2,1)S(1)}, u32[]{:S(2)}, u32[]{:S(2)}) collective-permute-start(bf16[400,256]{1,0:T(8,128)(2,1)S(1)} %add_convert_fusion.1), channel_id=1, source_target_pairs={{0,2},{2,0},{4,6},{6,4},{1,3},{3,1},{5,7},{7,5},{8,10},{10,8},{12,... | collective-permute-start | bytes 614408 | tf_op jit(solution)/shard_map/ppermute | solution.py:345
  115.4 1.9 %shard_map.123 = bf16[4,256,128]{2,1,0:T(8,128)(2,1)} custom-call(s32[1]{0:T(128)} %bitcast.22.info_ref, bf16[8,2,256,128]{3,2,1,0:T(8,128)(2,1)} %all-to-all-done.13.moved_ref, bf16[4,256,128]{2,1,0:T(8,128)(2,1)} %shard_map.122.refs_0_), custom_call_target="tpu_custom_call", output_to_operand_aliasing={{}: (2, {})} | custom-call | flops 1000000 | bytes 2000000 | tf_op jit(solution)/shard_map/pallas_call | solution.py:287
  117.4 3.9 %collective-permute-done.18 = bf16[400,256]{1,0:T(8,128)(2,1)S(1)} collective-permute-done((bf16[400,256]{1,0:T(8,128)(2,1)S(1)}, bf16[400,256]{1,0:T(8,128)(2,1)S(1)}, u32[]{:S(2)}, u32[]{:S(2)}) %collective-permute-start.18) | collective-permute-done | bytes 204832 | tf_op jit(solution)/shard_map/ppermute | solution.py:345
  121.4 4.5 %collective-permute-start.19 = (bf16[400,256]{1,0:T(8,128)(2,1)S(1)}, bf16[400,256]{1,0:T(8,128)(2,1)S(1)}, u32[]{:S(2)}, u32[]{:S(2)}) collective-permute-start(bf16[400,256]{1,0:T(8,128)(2,1)S(1)} %add_convert_fusion), channel_id=1, source_target_pairs={{0,6},{6,0},{2,4},{4,2},{1,7},{7,1},{3,5},{5,3},{8,14},{14,8},{10,... | collective-permute-start | bytes 614408 | tf_op jit(solution)/shard_map/ppermute | solution.py:352
  125.9 10.9 %all-to-all-start.14 = ((bf16[4,256,128]{2,1,0:T(8,128)(2,1)}), bf16[4,256,128]{2,1,0:T(8,128)(2,1)S(1)}, u32[]{:S(2)}, u32[]{:S(2)}) async-start(bf16[4,256,128]{2,1,0:T(8,128)(2,1)} %shard_map.123), calls=%async_computation.14 | async-start | bytes 524288 | tf_op jit(solution)/shard_map/all_to_all | solution.py:348
  137.0 1.9 %collective-permute-start.20 = (bf16[384,512]{1,0:T(8,128)(2,1)S(1)}, bf16[384,512]{1,0:T(8,128)(2,1)S(1)}, u32[]{:S(2)}, u32[]{:S(2)}) collective-permute-start(bf16[384,512]{1,0:T(8,128)(2,1)S(1)} %pad_maximum_fusion.1), channel_id=1, source_target_pairs={{0,1},{1,0},{2,3},{3,2},{4,5},{5,4},{6,7},{7,6},{8,9},{9,8},{10,11... | collective-permute-start | bytes 1179656 | tf_op jit(solution)/shard_map/ppermute | solution.py:31
  138.9 8.2 %collective-permute-start.21 = (f32[768]{0:T(1024)S(1)}, f32[768]{0:T(1024)S(1)}, u32[]{:S(2)}, u32[]{:S(2)}) collective-permute-start(f32[768]{0:T(1024)S(1)} %reshape.50), channel_id=1, source_target_pairs={{0,8},{8,0},{1,9},{9,1},{2,10},{10,2},{3,11},{11,3},{4,12},{12,4},... | collective-permute-start | bytes 9224 | tf_op jit(solution)/shard_map/ppermute | solution.py:31
  147.2 5.9 %collective-permute-done.21 = f32[768]{0:T(1024)S(1)} collective-permute-done((f32[768]{0:T(1024)S(1)}, f32[768]{0:T(1024)S(1)}, u32[]{:S(2)}, u32[]{:S(2)}) %collective-permute-start.21) | collective-permute-done | bytes 3104 | tf_op jit(solution)/shard_map/ppermute | solution.py:31
  (58 shorter events, 21.0 us)
Async XLA Ops:
  0.6 3.5 %copy-start = (bf16[1,3072,256]{2,1,0:T(8,128)(2,1)S(1)}, bf16[1,3072,256]{2,1,0:T(8,128)(2,1)}, u32[]{:S(2)}) copy-start(bf16[1,3072,256]{2,1,0:T(8,128)(2,1)} %param.20) | copy-start | bytes 4718596
  4.1 3.6 %copy-start.1 = (f32[1,768]{1,0:T(1,128)S(1)}, f32[1,768]{1,0:T(1,128)}, u32[]{:S(2)}) copy-start(f32[1,768]{1,0:T(1,128)} %logit_ref.1) | copy-start | bytes 9220
  4.1 3.6 %copy-start.2 = (s32[1,768]{1,0:T(1,128)S(1)}, s32[1,768]{1,0:T(1,128)}, u32[]{:S(2)}) copy-start(s32[1,768]{1,0:T(1,128)} %row_ref.1) | copy-start | bytes 9220
  4.1 3.6 %copy-start.3 = (bf16[1,768,256]{2,1,0:T(8,128)(2,1)S(1)}, bf16[1,768,256]{2,1,0:T(8,128)(2,1)}, u32[]{:S(2)}) copy-start(bf16[1,768,256]{2,1,0:T(8,128)(2,1)} %param.24) | copy-start | bytes 1179652
  4.2 3.6 %copy-start.5 = (bf16[1,768,256]{2,1,0:T(8,128)(2,1)S(1)}, bf16[1,768,256]{2,1,0:T(8,128)(2,1)}, u32[]{:S(2)}) copy-start(bf16[1,768,256]{2,1,0:T(8,128)(2,1)} %param.25) | copy-start | bytes 1179652
  9.2 20.7 %copy-start.14 = (bf16[768,256]{1,0:T(8,128)(2,1)S(1)}, bf16[768,256]{1,0:T(8,128)(2,1)}, u32[]{:S(2)}) copy-start(bf16[768,256]{1,0:T(8,128)(2,1)} %get-tuple-element.243.v_ref) | copy-start | bytes 1179652 | tf_op jit(solution)/shard_map/cond
  9.2 33.4 %all-to-all-start.7 = ((bf16[4,768,256]{2,1,0:T(8,128)(2,1)}), bf16[4,768,256]{2,1,0:T(8,128)(2,1)}, u32[]{:S(2)}, u32[]{:S(2)}) async-start(bf16[4,768,256]{2,1,0:T(8,128)(2,1)} %broadcast_in_dim.60), calls=%async_computation.7 | async-start | bytes 3145728 | tf_op jit(solution)/shard_map/cond/branch_7_fun/all_to_all | solution.py:35
  19.6 21.3 %collective-permute-start.7 = (bf16[512,256]{1,0:T(8,128)(2,1)S(1)}, bf16[512,256]{1,0:T(8,128)(2,1)S(1)}, u32[]{:S(2)}, u32[]{:S(2)}) collective-permute-start(bf16[512,256]{1,0:T(8,128)(2,1)S(1)} %slice.55), channel_id=1, source_target_pairs={{0,8},{8,0},{1,9},{9,1},{2,10},{10,2},{3,11},{11,3},{4,12},{12,4},... | collective-permute-start | bytes 786440 | tf_op jit(solution)/shard_map/cond/branch_7_fun/ppermute | solution.py:31
  42.7 12.6 %collective-permute-start.12 = (bf16[4,768,256]{2,1,0:T(8,128)(2,1)}, bf16[4,768,256]{2,1,0:T(8,128)(2,1)}, u32[]{:S(2)}, u32[]{:S(2)}) collective-permute-start(bf16[4,768,256]{2,1,0:T(8,128)(2,1)} %get-tuple-element.319.near_ref), channel_id=1, source_target_pairs={{0,1},{1,0},{2,3},{3,2},{4,5},{5,4},{6,7},{7,6},{8,9},{9,8},{10,11... | collective-permute-start | bytes 4718600 | tf_op jit(solution)/shard_map/ppermute | solution.py:31
  44.6 29.2 %collective-permute-start.15 = (bf16[768,256]{1,0:T(8,128)(2,1)}, bf16[768,256]{1,0:T(8,128)(2,1)S(1)}, u32[]{:S(2)}, u32[]{:S(2)}) collective-permute-start(bf16[768,256]{1,0:T(8,128)(2,1)} %get-tuple-element.323), channel_id=1, source_target_pairs={{0,6},{2,0},{4,2},{6,4},{1,7},{3,1},{5,3},{7,5},{8,14},{10,8},{12,... | collective-permute-start | bytes 1179656 | tf_op jit(solution)/shard_map/ppermute | solution.py:328
  47.4 26.5 %collective-permute-start.14 = (bf16[768,256]{1,0:T(8,128)(2,1)}, bf16[768,256]{1,0:T(8,128)(2,1)}, u32[]{:S(2)}, u32[]{:S(2)}) collective-permute-start(bf16[768,256]{1,0:T(8,128)(2,1)} %get-tuple-element.323), channel_id=1, source_target_pairs={{0,4},{2,6},{4,0},{6,2},{1,5},{3,7},{5,1},{7,3},{8,12},{10,14},{12... | collective-permute-start | bytes 1179656 | tf_op jit(solution)/shard_map/ppermute | solution.py:328
  49.9 23.9 %collective-permute-start.13 = (bf16[768,256]{1,0:T(8,128)(2,1)}, bf16[768,256]{1,0:T(8,128)(2,1)}, u32[]{:S(2)}, u32[]{:S(2)}) collective-permute-start(bf16[768,256]{1,0:T(8,128)(2,1)} %get-tuple-element.323), channel_id=1, source_target_pairs={{0,2},{2,4},{4,6},{6,0},{1,3},{3,5},{5,7},{7,1},{8,10},{10,12},{12... | collective-permute-start | bytes 1179656 | tf_op jit(solution)/shard_map/ppermute | solution.py:328
  61.7 26.9 %all-to-all-start.12 = ((bf16[8,2,256,128]{3,2,1,0:T(8,128)(2,1)}), bf16[8,2,256,128]{3,2,1,0:T(8,128)(2,1)S(1)}, u32[]{:S(2)}, u32[]{:S(2)}) async-start(bf16[8,2,256,128]{3,2,1,0:T(8,128)(2,1)} %bitcast.35), calls=%async_computation.12 | async-start | bytes 2097152 | tf_op jit(solution)/shard_map/all_to_all | solution.py:305
  76.3 5.6 %collective-permute-start.16 = (bf16[4,768,256]{2,1,0:T(8,128)(2,1)}, bf16[4,768,256]{2,1,0:T(8,128)(2,1)}, u32[]{:S(2)}, u32[]{:S(2)}) collective-permute-start(bf16[4,768,256]{2,1,0:T(8,128)(2,1)} %pad_maximum_fusion.near_ref), channel_id=1, source_target_pairs={{0,1},{1,0},{2,3},{3,2},{4,5},{5,4},{6,7},{7,6},{8,9},{9,8},{10,11... | collective-permute-start | bytes 4718600 | tf_op jit(solution)/shard_map/ppermute | solution.py:31
  88.6 9.0 %copy-start.4 = (bf16[1,768,256]{2,1,0:T(8,128)(2,1)S(1)}, bf16[1,768,256]{2,1,0:T(8,128)(2,1)}, u32[]{:S(2)}) copy-start(bf16[1,768,256]{2,1,0:T(8,128)(2,1)} %param.24) | copy-start | bytes 1179652
  88.6 9.0 %copy-start.6 = (bf16[1,768,256]{2,1,0:T(8,128)(2,1)S(1)}, bf16[1,768,256]{2,1,0:T(8,128)(2,1)}, u32[]{:S(2)}) copy-start(bf16[1,768,256]{2,1,0:T(8,128)(2,1)} %param.25) | copy-start | bytes 1179652
  88.6 24.2 %all-to-all-start.13 = ((bf16[8,2,256,128]{3,2,1,0:T(8,128)(2,1)}), bf16[8,2,256,128]{3,2,1,0:T(8,128)(2,1)}, u32[]{:S(2)}, u32[]{:S(2)}) async-start(bf16[8,2,256,128]{3,2,1,0:T(8,128)(2,1)} %bitcast.36), calls=%async_computation.13 | async-start | bytes 2097152 | tf_op jit(solution)/shard_map/all_to_all | solution.py:305
  106.3 3.5 %collective-permute-start.17 = (bf16[400,256]{1,0:T(8,128)(2,1)}, bf16[400,256]{1,0:T(8,128)(2,1)S(1)}, u32[]{:S(2)}, u32[]{:S(2)}) collective-permute-start(bf16[400,256]{1,0:T(8,128)(2,1)} %get-tuple-element.334), channel_id=1, source_target_pairs={{0,1},{1,0},{2,3},{3,2},{4,5},{5,4},{6,7},{7,6},{8,9},{9,8},{10,11... | collective-permute-start | bytes 614408 | tf_op jit(solution)/shard_map/ppermute | solution.py:31
  112.7 8.6 %collective-permute-start.18 = (bf16[400,256]{1,0:T(8,128)(2,1)S(1)}, bf16[400,256]{1,0:T(8,128)(2,1)S(1)}, u32[]{:S(2)}, u32[]{:S(2)}) collective-permute-start(bf16[400,256]{1,0:T(8,128)(2,1)S(1)} %add_convert_fusion.1), channel_id=1, source_target_pairs={{0,2},{2,0},{4,6},{6,4},{1,3},{3,1},{5,7},{7,5},{8,10},{10,8},{12,... | collective-permute-start | bytes 614408 | tf_op jit(solution)/shard_map/ppermute | solution.py:345
  121.4 15.4 %collective-permute-start.19 = (bf16[400,256]{1,0:T(8,128)(2,1)S(1)}, bf16[400,256]{1,0:T(8,128)(2,1)S(1)}, u32[]{:S(2)}, u32[]{:S(2)}) collective-permute-start(bf16[400,256]{1,0:T(8,128)(2,1)S(1)} %add_convert_fusion), channel_id=1, source_target_pairs={{0,6},{6,0},{2,4},{4,2},{1,7},{7,1},{3,5},{5,3},{8,14},{14,8},{10,... | collective-permute-start | bytes 614408 | tf_op jit(solution)/shard_map/ppermute | solution.py:352
  125.9 29.1 %all-to-all-start.14 = ((bf16[4,256,128]{2,1,0:T(8,128)(2,1)}), bf16[4,256,128]{2,1,0:T(8,128)(2,1)S(1)}, u32[]{:S(2)}, u32[]{:S(2)}) async-start(bf16[4,256,128]{2,1,0:T(8,128)(2,1)} %shard_map.123), calls=%async_computation.14 | async-start | bytes 524288 | tf_op jit(solution)/shard_map/all_to_all | solution.py:348
  137.0 16.8 %collective-permute-start.20 = (bf16[384,512]{1,0:T(8,128)(2,1)S(1)}, bf16[384,512]{1,0:T(8,128)(2,1)S(1)}, u32[]{:S(2)}, u32[]{:S(2)}) collective-permute-start(bf16[384,512]{1,0:T(8,128)(2,1)S(1)} %pad_maximum_fusion.1), channel_id=1, source_target_pairs={{0,1},{1,0},{2,3},{3,2},{4,5},{5,4},{6,7},{7,6},{8,9},{9,8},{10,11... | collective-permute-start | bytes 1179656 | tf_op jit(solution)/shard_map/ppermute | solution.py:31
  138.9 14.2 %collective-permute-start.21 = (f32[768]{0:T(1024)S(1)}, f32[768]{0:T(1024)S(1)}, u32[]{:S(2)}, u32[]{:S(2)}) collective-permute-start(f32[768]{0:T(1024)S(1)} %reshape.50), channel_id=1, source_target_pairs={{0,8},{8,0},{1,9},{9,1},{2,10},{10,2},{3,11},{11,3},{4,12},{12,4},... | collective-permute-start | bytes 9224 | tf_op jit(solution)/shard_map/ppermute | solution.py:31

commit v6 on v5

--- a/solution.py
+++ b/solution.py
@@ -55,10 +55,11 @@
     )(rows)
 
 
-def exchange(rows, picked, attention):
+def exchange(rows, picked, scalars, attention):
     other = padded(swap(picked[:rows], "zh"))
     near = spread_x(repeated(picked))
-    return other, near, forward(*attention)
+    info = jnp.stack(scalars).astype(jnp.int32)
+    return other, near, info, forward(info, *attention)
 
 
 def rows_dot(a, b):
@@ -230,52 +231,46 @@
     )(info, q, k, v, pos_col, pos_row, logit_col, lse, att, grad_o)
 
 
-def products_kernel(info_ref, near_ref, far_ref, wn_ref, wf_ref, scaled_ref, *refs):
+def products_kernel(info_ref, near_ref, far_ref, w_ref, scaled_ref, *refs):
     go_ref, wg_ref = refs[-2:]
     core = info_ref[0]
-    near, far = near_ref[0], far_ref[0]
-    first = pl.program_id(0) == 0
-
-    @pl.when(first)
-    def _():
-        go_ref[...] = refs[0][...] if len(refs) == 3 else jnp.zeros_like(go_ref)
-
-    w = jnp.concatenate([wn_ref[0], wf_ref[0]], 0)
-    for r in range(0, SLOTS, 128):
-        rows = slice(r, r + 128)
-        both = jnp.concatenate([near_ref[0, rows], far_ref[0, rows]], 1)
-        go_ref[rows] += jnp.dot(both, w, preferred_element_type=F32)
-
-    for shard, y in ((near, 2 * core), (far, 2 - 2 * core)):
-        grad = jnp.dot(scaled_ref[...], shard, preferred_element_type=F32).astype(BF)
-        wg_ref[0, y, 0] = grad[:, :128]
-        wg_ref[0, y + 1, 0] = grad[:, 128:]
+    entry = [(info_ref[2] + info_ref[3] * s) % X for s in range(X)]
+    w = [jnp.concatenate([w_ref[2 * s + core], w_ref[2 * s + 1 - core]], 0) for s in range(X)]
+    for r in range(0, SLOTS, ROWS):
+        rows = slice(r, r + ROWS)
+        total = refs[0][rows] if len(refs) == 3 else jnp.zeros((ROWS, WIDE), F32)
+        for s in range(X):
+            both = jnp.concatenate([near_ref[entry[s], rows], far_ref[entry[s], rows]], 1)
+            total = total + jnp.dot(both, w[s], preferred_element_type=F32)
+        go_ref[rows] = total
+    for s in range(X):
+        for ref, y in ((near_ref, 2 * core), (far_ref, 2 - 2 * core)):
+            grad = jnp.dot(scaled_ref[...], ref[entry[s]], preferred_element_type=F32).astype(BF)
+            wg_ref[s % 2, y, s // 2] = grad[:, :128]
+            wg_ref[s % 2, y + 1, s // 2] = grad[:, 128:]
 
 
 def products(core, half, base, turn, near, far, w_out, scaled_t, begin=None):
     info = jnp.stack([core, half, base, turn]).astype(jnp.int32)
     more = [] if begin is None else [begin]
-    shard = pl.BlockSpec((1, SLOTS, WIDE), lambda i, info: (i, 0, 0))
-    at = lambda i, info: (info[2] + info[3] * i) % X
-    w_near = pl.BlockSpec((1, WIDE, WIDE), lambda i, info: (info[1] * 8 + at(i, info) * 2 + info[0], 0, 0))
-    w_far = pl.BlockSpec((1, WIDE, WIDE), lambda i, info: (info[1] * 8 + at(i, info) * 2 + 1 - info[0], 0, 0))
-    w_parts = w_out.reshape(ZH * X * CORE, WIDE, WIDE)
+    shards = whole((X, SLOTS, WIDE))
     return pl.pallas_call(
         products_kernel,
         grid_spec=pltpu.PrefetchScalarGridSpec(
             num_scalar_prefetch=1,
-            grid=(X,),
-            in_specs=[shard, shard, w_near, w_far, whole((WIDE, SLOTS))]
+            grid=(1,),
+            in_specs=[
+                shards, shards,
+                pl.BlockSpec((X * CORE, WIDE, WIDE), lambda i, info: (info[1], 0, 0)),
+                whole((WIDE, SLOTS)),
+            ]
             + [whole((SLOTS, WIDE)) for _ in more],
-            out_specs=[
-                whole((SLOTS, WIDE)),
-                pl.BlockSpec((1, Y, 1, WIDE, 128), lambda i, info: (at(i, info) % 2, 0, at(i, info) // 2, 0, 0)),
-            ],
+            out_specs=[whole((SLOTS, WIDE)), whole((ZP, Y, 2, WIDE, 128))],
         ),
         out_shape=[shape_of((SLOTS, WIDE), F32), shape_of((ZP, Y, 2, WIDE, 128), BF)],
         compiler_params=LIMIT,
         cost_estimate=pl.CostEstimate(flops=2 * 10**10, bytes_accessed=8 * 10**6, transcendentals=0),
-    )(info, near, far, w_parts, w_parts, scaled_t, *more)
+    )(info, near, far, w_out.reshape(ZH * X * CORE, WIDE, WIDE), scaled_t, *more)
 
 
 def fold_kernel(info_ref, moved_ref, *refs):
@@ -300,6 +295,20 @@
     )(half.astype(jnp.int32).reshape(1), moved, *more)
 
 
+def logits_kernel(router_ref, other_ref, logit_ref, out_ref):
+    weight = 1.0 / (1.0 + jnp.exp(-logit_ref[...]))
+    out_ref[...] = (router_ref[...] + other_ref[...]) * weight * (1.0 - weight)
+
+
+def logits_gradient(router, other, logits):
+    return pl.pallas_call(
+        logits_kernel,
+        out_shape=shape_of((1, SLOTS), F32),
+        compiler_params=SMALL,
+        cost_estimate=pl.CostEstimate(flops=2 * 10**10, bytes_accessed=10**4, transcendentals=0),
+    )(router, other, logits)
+
+
 def over_zp_y(blocks):
     blocks = blocks.reshape(ZP * Y, 2, WIDE, 128)
     return lax.all_to_all(blocks, ("zp", "y"), 0, 0, tiled=True)
@@ -315,15 +324,14 @@
     live = jnp.arange(SLOTS, dtype=jnp.int32) < own_count
     picked = lax.optimization_barrier(jnp.where(live[:, None], picked, jnp.zeros((), BF)))
 
-    info = jnp.stack([x // 2, own_count, core]).astype(jnp.int32)
     attention = (
-        info, query_rows[0], key_rows[0], routed_value_rows[0],
+        query_rows[0], key_rows[0], routed_value_rows[0],
         routed, routed, logits,
     )
     sizes = range(STEP, SLOTS + 1, STEP)
     branch = jnp.maximum(own_count - 1, 0) // STEP
-    other, own_near, (attended, scaled_t, lse) = lax.switch(
-        branch, [functools.partial(exchange, rows) for rows in sizes], picked, attention
+    other, own_near, info, (attended, scaled_t, lse) = lax.switch(
+        branch, [functools.partial(exchange, rows) for rows in sizes], picked, (x // 2, own_count, core), attention
     )
     other_near = jnp.stack([other] + [lax.ppermute(other, "x", ring(X, k)) for k in range(1, X)])
     own_far = swap(own_near, "core")
@@ -337,7 +345,7 @@
     moved_own, grad_o, w_grad_other = lax.optimization_barrier((moved_own, grad_o, w_grad_other))
     moved_other = over_zp_y(w_grad_other)
     blocks = fold(zh, moved_own)
-    grad_q, kept, sent = backward(*attention, lse, attended, grad_o)
+    grad_q, kept, sent = backward(info, *attention, lse, attended, grad_o)
     came = swap(sent, "core")
     chip = (kept.astype(F32) + came.astype(F32)).astype(BF)
 
@@ -351,21 +359,19 @@
     group = (chip.astype(F32) + pair.astype(F32)).astype(BF)
     apart = lax.ppermute(group, "x", [(0, 3), (3, 0), (1, 2), (2, 1)])
     router = group[HALF:].astype(F32) + apart[HALF:].astype(F32)
-    router = (router[: SLOTS // WIDE] + router[SLOTS // WIDE : 2 * SLOTS // WIDE]).reshape(SLOTS)
+    router = (router[: SLOTS // WIDE] + router[SLOTS // WIDE : 2 * SLOTS // WIDE]).reshape(1, SLOTS)
     first = jnp.where(x < 2, group, apart)[:HALF]
     second = jnp.where(x < 2, apart, group)[:HALF]
     joined = jnp.concatenate(
         [first[:, :HEAD_SIZE], second[:, :HEAD_SIZE], first[:, HEAD_SIZE:], second[:, HEAD_SIZE:]], 1
     )
     theirs = swap(joined, "core")
-    router = router + swap(router, "zh")
+    grad_logits = logits_gradient(router, swap(router, "zh"), logits)
     rows = jnp.where(
         core == 0, jnp.concatenate([joined, theirs], 0), jnp.concatenate([theirs, joined], 0)
     )
     key_total, value_total = rows[:, : 2 * HEAD_SIZE], rows[:, 2 * HEAD_SIZE :]
-    router_weight = jax.nn.sigmoid(logits[0])
-    grad_logits = router * router_weight * (1.0 - router_weight)
-    return (grad_q[None], key_total[None], value_total[None], w_grad, grad_logits[None])
+    return (grad_q[None], key_total[None], value_total[None], w_grad, grad_logits)
 
 
 def solution(mesh):

time: 157 us -> 161 us (1.025)
  the two profiles are of different devices: /device:TPU:6 before, /device:TPU:64 now
where the time goes in v6:
time: 161 us; the launch traced here: 158 us
  starting transfers between devices  90.2 us (56%)
  Pallas kernels  31.5 us (20%)
  waiting for transfers between devices  18.6 us (12%)
  other arithmetic  9.34 us (6%)
  local copies, waits for them, and re-layouts  6.71 us (4%)
  between operations  1.61 us (1%)
    ppermute x6, starting transfers between devices, swap(): return lax.ppermute(value, axis, ring(2, 1))  31.1 us
    all_to_all x1, starting transfers between devices, per_device(): final = lax.all_to_all(blocks, 'zq', 0, 0, tiled=True)  20.2 us
    all_to_all x2, starting transfers between devices, over_zp_y(): return lax.all_to_all(blocks, ('zp', 'y'), 0, 0, tiled=True)  16.8 us
    ppermute x3, starting transfers between devices, per_device(): lax.ppermute(other, 'x', ring(X, k))  13.3 us
    pallas_call x2, Pallas kernels, products(): pl.pallas_call(products_kernel, grid_spec=pltpu.PrefetchScalarGridSpec(nu...  11.7 us
    ppermute x6, waiting for transfers between devices, swap(): return lax.ppermute(value, axis, ring(2, 1))  8.92 us
    pallas_call x1, Pallas kernels, backward(): pl.pallas_call(backward_kernel, grid_spec=pltpu.PrefetchScalarGridSpec(nu...  8.9 us
    pallas_call x1, Pallas kernels, forward(): pl.pallas_call(forward_kernel, grid_spec=pltpu.PrefetchScalarGridSpec(num...  6.69 us
  transfers between devices with their start and end apart: 15, of which 7 were waited for; matrix products, arithmetic and copies ran while one was open for 5% of the time, Pallas kernels for 20%

profile of v6, /device:TPU:64, one launch (start us, length us, event | category | flops | bytes accessed | tf_op | source)
XLA Modules:
  0.0 158.0 jit_solution(7913404735421366898)
XLA Ops:
  4.2 2.7 %gather_fusion = bf16[768,256]{1,0:T(8,128)(2,1)S(1)} fusion(bf16[3072,256]{1,0:T(8,128)(2,1)S(1)} %bitcast.72, s32[1024]{0:T(1024)S(1)} %pad_clamp_fusion), kind=kCustom, calls=%fused_computation | custom fusion | bytes 789504 | tf_op jit(solution)/shard_map/gather | solution.py:323
  7.1 29.5 %conditional.1 = (bf16[768,256]{1,0:T(8,128)(2,1)}, bf16[4,768,256]{2,1,0:T(8,128)(2,1)}, s32[3]{0:T(128)}, bf16[768,256]{1,0:T(8,128)(2,1)}, bf16[256,768]{1,0:...) conditional(s32[]{:T(128)} %clamp.3, ...), branch_computations={%region_1.2_spmd, %region_2.3_spmd, %region_3.4_spmd, %region_4.5_... | conditional | flops 4000999936 | bytes 12634019 | solution.py:333
  8.3 4.4 %all-to-all-start.3 = ((bf16[4,768,256]{2,1,0:T(8,128)(2,1)}), bf16[4,768,256]{2,1,0:T(8,128)(2,1)}, u32[]{:S(2)}, u32[]{:S(2)}) async-start(bf16[4,768,256]{2,1,0:T(8,128)(2,1)} %broadcast_in_dim.51), calls=%async_computation.3 | async-start | bytes 3145728 | tf_op jit(solution)/shard_map/cond/branch_3_fun/all_to_all | solution.py:35
  12.7 13.9 %collective-permute-start.3 = (bf16[256,256]{1,0:T(8,128)(2,1)S(1)}, bf16[256,256]{1,0:T(8,128)(2,1)S(1)}, u32[]{:S(2)}, u32[]{:S(2)}) collective-permute-start(bf16[256,256]{1,0:T(8,128)(2,1)S(1)} %slice.51), channel_id=1, source_target_pairs={{0,8},{8,0},{1,9},{9,1},{2,10},{10,2},{3,11},{11,3},{4,12},{12,4},... | collective-permute-start | bytes 393224 | tf_op jit(solution)/shard_map/cond/branch_3_fun/ppermute | solution.py:31
  27.9 6.7 %branch_3_fun.3 = (bf16[768,256]{1,0:T(8,128)(2,1)}, bf16[256,768]{1,0:T(8,128)(2,1)}, f32[2,768]{1,0:T(2,128)S(1)}) custom-call(s32[3]{0:T(128)} %pad_add_fusion.3.info_ref, bf16[768,256]{1,0:T(8,128)(2,1)S(1)} %get-tuple-element.497.q_ref, bf16[768,256]{1,0:T(8,128)(2,1)S(1)} %get-tuple-element.498.k_ref, bf16[768,256]{1,0:T(8,128)(2,1)} %get-tuple-element.499.v_ref, ...), custom_call_target="tpu_custom_call" | custom-call | flops 4000000000 | bytes 2000000 | tf_op jit(solution)/shard_map/cond/branch_3_fun/pallas_call | solution.py:194
  38.4 7.8 %collective-permute-start.15 = (bf16[768,256]{1,0:T(8,128)(2,1)}, bf16[768,256]{1,0:T(8,128)(2,1)S(1)}, u32[]{:S(2)}, u32[]{:S(2)}) collective-permute-start(bf16[768,256]{1,0:T(8,128)(2,1)} %get-tuple-element.661), channel_id=1, source_target_pairs={{0,6},{2,0},{4,2},{6,4},{1,7},{3,1},{5,3},{7,5},{8,14},{10,8},{12,... | collective-permute-start | bytes 1179656 | tf_op jit(solution)/shard_map/ppermute | solution.py:336
  46.2 2.8 %collective-permute-start.14 = (bf16[768,256]{1,0:T(8,128)(2,1)}, bf16[768,256]{1,0:T(8,128)(2,1)}, u32[]{:S(2)}, u32[]{:S(2)}) collective-permute-start(bf16[768,256]{1,0:T(8,128)(2,1)} %get-tuple-element.661), channel_id=1, source_target_pairs={{0,4},{2,6},{4,0},{6,2},{1,5},{3,7},{5,1},{7,3},{8,12},{10,14},{12... | collective-permute-start | bytes 1179656 | tf_op jit(solution)/shard_map/ppermute | solution.py:336
  49.0 2.8 %collective-permute-start.13 = (bf16[768,256]{1,0:T(8,128)(2,1)}, bf16[768,256]{1,0:T(8,128)(2,1)}, u32[]{:S(2)}, u32[]{:S(2)}) collective-permute-start(bf16[768,256]{1,0:T(8,128)(2,1)} %get-tuple-element.661), channel_id=1, source_target_pairs={{0,2},{2,4},{4,6},{6,0},{1,3},{3,5},{5,7},{7,1},{8,10},{10,12},{12... | collective-permute-start | bytes 1179656 | tf_op jit(solution)/shard_map/ppermute | solution.py:336
  52.4 5.7 %shard_map.119 = (f32[768,256]{1,0:T(8,128)}, bf16[2,4,2,256,128]{4,3,2,1,0:T(8,128)(2,1)}) custom-call(s32[4]{0:T(128)} %pad_add_fusion.12.info_ref, bf16[4,768,256]{2,1,0:T(8,128)(2,1)} %get-tuple-element.657.near_ref, bf16[4,768,256]{2,1,0:T(8,128)(2,1)} %collective-permute-done.12.far_ref, bf16[16,256,256]{2,1,0:T(8,128)(2,1)} %bitcast.79, ...), custom_call_target="tpu_custom_call" | custom-call | flops 20000000000 | bytes 8000000 | tf_op jit(solution)/shard_map/pallas_call | solution.py:257
  58.1 8.3 %all-to-all-start.12 = ((bf16[8,2,256,128]{3,2,1,0:T(8,128)(2,1)}), bf16[8,2,256,128]{3,2,1,0:T(8,128)(2,1)S(1)}, u32[]{:S(2)}, u32[]{:S(2)}) async-start(bf16[8,2,256,128]{3,2,1,0:T(8,128)(2,1)} %bitcast.75), calls=%async_computation.12 | async-start | bytes 2097152 | tf_op jit(solution)/shard_map/all_to_all | solution.py:314
  66.5 3.1 %collective-permute-done.13 = bf16[768,256]{1,0:T(8,128)(2,1)} collective-permute-done((bf16[768,256]{1,0:T(8,128)(2,1)}, bf16[768,256]{1,0:T(8,128)(2,1)}, u32[]{:S(2)}, u32[]{:S(2)}) %collective-permute-start.13) | collective-permute-done | bytes 393248 | tf_op jit(solution)/shard_map/ppermute | solution.py:336
  69.6 2.5 %pad_maximum_fusion.near_ref = bf16[4,768,256]{2,1,0:T(8,128)(2,1)} fusion(bf16[1,768,256]{2,1,0:T(8,128)(2,1)S(1)} %bitcast.77, bf16[1,768,256]{2,1,0:T(8,128)(2,1)} %bitcast.59, bf16[1,768,256]{2,1,0:T(8,128)(2,1)} %bitcast.58, bf16[1,768,256]{2,1,0:T(8,128)(2,1)S(1)} %get-tuple-element.660), kind=kLoop, calls=%fused_computation.13 | loop fusion | flops 2359296 | bytes 3145728 | tf_op jit(solution)/shard_map/stack | solution.py:336
  72.1 1.9 %collective-permute-start.16 = (bf16[4,768,256]{2,1,0:T(8,128)(2,1)}, bf16[4,768,256]{2,1,0:T(8,128)(2,1)}, u32[]{:S(2)}, u32[]{:S(2)}) collective-permute-start(bf16[4,768,256]{2,1,0:T(8,128)(2,1)} %pad_maximum_fusion.near_ref), channel_id=1, source_target_pairs={{0,1},{1,0},{2,3},{3,2},{4,5},{5,4},{6,7},{7,6},{8,9},{9,8},{10,11... | collective-permute-start | bytes 4718600 | tf_op jit(solution)/shard_map/ppermute | solution.py:31
  74.6 3.1 %collective-permute-done.16.far_ref = bf16[4,768,256]{2,1,0:T(8,128)(2,1)} collective-permute-done((bf16[4,768,256]{2,1,0:T(8,128)(2,1)}, bf16[4,768,256]{2,1,0:T(8,128)(2,1)}, u32[]{:S(2)}, u32[]{:S(2)}) %collective-permute-start.16) | collective-permute-done | bytes 1572896 | tf_op jit(solution)/shard_map/ppermute | solution.py:31
  77.7 6.0 %shard_map.120 = (f32[768,256]{1,0:T(8,128)}, bf16[2,4,2,256,128]{4,3,2,1,0:T(8,128)(2,1)}) custom-call(s32[4]{0:T(128)} %pad_add_fusion.13.info_ref, bf16[4,768,256]{2,1,0:T(8,128)(2,1)} %pad_maximum_fusion.near_ref, bf16[4,768,256]{2,1,0:T(8,128)(2,1)} %collective-permute-done.16.far_ref, bf16[16,256,256]{2,1,0:T(8,128)(2,1)} %bitcast.80, ...), custom_call_target="tpu_custom_call" | custom-call | flops 20000000000 | bytes 8000000 | tf_op jit(solution)/shard_map/pallas_call | solution.py:257
  83.7 8.5 %all-to-all-start.13 = ((bf16[8,2,256,128]{3,2,1,0:T(8,128)(2,1)}), bf16[8,2,256,128]{3,2,1,0:T(8,128)(2,1)}, u32[]{:S(2)}, u32[]{:S(2)}) async-start(bf16[8,2,256,128]{3,2,1,0:T(8,128)(2,1)} %bitcast.76), calls=%async_computation.13 | async-start | bytes 2097152 | tf_op jit(solution)/shard_map/all_to_all | solution.py:314
  92.2 8.9 %shard_map.121 = (bf16[768,256]{1,0:T(8,128)(2,1)}, bf16[400,256]{1,0:T(8,128)(2,1)}, bf16[400,256]{1,0:T(8,128)(2,1)}) custom-call(s32[3]{0:T(128)} %get-tuple-element.654.info_ref, bf16[768,256]{1,0:T(8,128)(2,1)S(1)} %bitcast.93, bf16[768,256]{1,0:T(8,128)(2,1)S(1)} %bitcast.106, bf16[768,256]{1,0:T(8,128)(2,1)} %bitcast.119, s32[1,768]{1,0:T(1,128)S(1)} %copy-done.1, ...), custom_call_target="tpu_custom_call" | custom-call | flops 7000000000 | bytes 4000000 | tf_op jit(solution)/shard_map/pallas_call | solution.py:210
  109.3 1.9 %shard_map.123 = bf16[4,256,128]{2,1,0:T(8,128)(2,1)} custom-call(s32[1]{0:T(128)} %bitcast.56.info_ref, bf16[8,2,256,128]{3,2,1,0:T(8,128)(2,1)} %all-to-all-done.13.moved_ref, bf16[4,256,128]{2,1,0:T(8,128)(2,1)} %shard_map.122.refs_0_), custom_call_target="tpu_custom_call", output_to_operand_aliasing={{}: (2, {})} | custom-call | flops 1000000 | bytes 2000000 | tf_op jit(solution)/shard_map/pallas_call | solution.py:282
  111.2 4.7 %collective-permute-done.18 = bf16[400,256]{1,0:T(8,128)(2,1)S(1)} collective-permute-done((bf16[400,256]{1,0:T(8,128)(2,1)S(1)}, bf16[400,256]{1,0:T(8,128)(2,1)S(1)}, u32[]{:S(2)}, u32[]{:S(2)}) %collective-permute-start.18) | collective-permute-done | bytes 204832 | tf_op jit(solution)/shard_map/ppermute | solution.py:353
  116.0 2.5 %collective-permute-start.19 = (bf16[400,256]{1,0:T(8,128)(2,1)S(1)}, bf16[400,256]{1,0:T(8,128)(2,1)S(1)}, u32[]{:S(2)}, u32[]{:S(2)}) collective-permute-start(bf16[400,256]{1,0:T(8,128)(2,1)S(1)} %add_convert_fusion), channel_id=1, source_target_pairs={{0,6},{6,0},{2,4},{4,2},{1,7},{7,1},{3,5},{5,3},{8,14},{14,8},{10,... | collective-permute-start | bytes 614408 | tf_op jit(solution)/shard_map/ppermute | solution.py:360
  118.6 20.2 %all-to-all-start.14 = ((bf16[4,256,128]{2,1,0:T(8,128)(2,1)}), bf16[4,256,128]{2,1,0:T(8,128)(2,1)S(1)}, u32[]{:S(2)}, u32[]{:S(2)}) async-start(bf16[4,256,128]{2,1,0:T(8,128)(2,1)} %shard_map.123), calls=%async_computation.14 | async-start | bytes 524288 | tf_op jit(solution)/shard_map/all_to_all | solution.py:356
  138.8 9.6 %collective-permute-start.21 = (f32[1,768]{1,0:T(1,128)S(1)}, f32[1,768]{1,0:T(1,128)S(1)}, u32[]{:S(2)}, u32[]{:S(2)}) collective-permute-start(f32[1,768]{1,0:T(1,128)S(1)} %bitcast.73), channel_id=1, source_target_pairs={{0,8},{8,0},{1,9},{9,1},{2,10},{10,2},{3,11},{11,3},{4,12},{12,4},... | collective-permute-start | bytes 9224 | tf_op jit(solution)/shard_map/ppermute | solution.py:31
  148.5 1.9 %collective-permute-start.20 = (bf16[384,512]{1,0:T(8,128)(2,1)S(1)}, bf16[384,512]{1,0:T(8,128)(2,1)S(1)}, u32[]{:S(2)}, u32[]{:S(2)}) collective-permute-start(bf16[384,512]{1,0:T(8,128)(2,1)S(1)} %pad_maximum_fusion.1), channel_id=1, source_target_pairs={{0,1},{1,0},{2,3},{3,2},{4,5},{5,4},{6,7},{7,6},{8,9},{9,8},{10,11... | collective-permute-start | bytes 1179656 | tf_op jit(solution)/shard_map/ppermute | solution.py:31
  150.5 4.9 %collective-permute-done.21.other_ref = f32[1,768]{1,0:T(1,128)S(1)} collective-permute-done((f32[1,768]{1,0:T(1,128)S(1)}, f32[1,768]{1,0:T(1,128)S(1)}, u32[]{:S(2)}, u32[]{:S(2)}) %collective-permute-start.21) | collective-permute-done | bytes 3104 | tf_op jit(solution)/shard_map/ppermute | solution.py:31
  (54 shorter events, 21.6 us)
Async XLA Ops:
  0.6 3.5 %copy-start = (bf16[1,3072,256]{2,1,0:T(8,128)(2,1)S(1)}, bf16[1,3072,256]{2,1,0:T(8,128)(2,1)}, u32[]{:S(2)}) copy-start(bf16[1,3072,256]{2,1,0:T(8,128)(2,1)} %param.20) | copy-start | bytes 4718596
  4.1 2.9 %copy-start.1 = (s32[1,768]{1,0:T(1,128)S(1)}, s32[1,768]{1,0:T(1,128)}, u32[]{:S(2)}) copy-start(s32[1,768]{1,0:T(1,128)} %row_ref.1) | copy-start | bytes 9220
  4.1 2.9 %copy-start.2 = (bf16[1,768,256]{2,1,0:T(8,128)(2,1)S(1)}, bf16[1,768,256]{2,1,0:T(8,128)(2,1)}, u32[]{:S(2)}) copy-start(bf16[1,768,256]{2,1,0:T(8,128)(2,1)} %param.24) | copy-start | bytes 1179652
  4.1 2.9 %copy-start.4 = (bf16[1,768,256]{2,1,0:T(8,128)(2,1)S(1)}, bf16[1,768,256]{2,1,0:T(8,128)(2,1)}, u32[]{:S(2)}) copy-start(bf16[1,768,256]{2,1,0:T(8,128)(2,1)} %param.25) | copy-start | bytes 1179652
  4.1 2.9 %copy-start.6 = (f32[1,768]{1,0:T(1,128)S(1)}, f32[1,768]{1,0:T(1,128)}, u32[]{:S(2)}) copy-start(f32[1,768]{1,0:T(1,128)} %logit_ref.3) | copy-start | bytes 9220
  8.3 28.2 %all-to-all-start.3 = ((bf16[4,768,256]{2,1,0:T(8,128)(2,1)}), bf16[4,768,256]{2,1,0:T(8,128)(2,1)}, u32[]{:S(2)}, u32[]{:S(2)}) async-start(bf16[4,768,256]{2,1,0:T(8,128)(2,1)} %broadcast_in_dim.51), calls=%async_computation.3 | async-start | bytes 3145728 | tf_op jit(solution)/shard_map/cond/branch_3_fun/all_to_all | solution.py:35
  12.7 22.0 %collective-permute-start.3 = (bf16[256,256]{1,0:T(8,128)(2,1)S(1)}, bf16[256,256]{1,0:T(8,128)(2,1)S(1)}, u32[]{:S(2)}, u32[]{:S(2)}) collective-permute-start(bf16[256,256]{1,0:T(8,128)(2,1)S(1)} %slice.51), channel_id=1, source_target_pairs={{0,8},{8,0},{1,9},{9,1},{2,10},{10,2},{3,11},{11,3},{4,12},{12,4},... | collective-permute-start | bytes 393224 | tf_op jit(solution)/shard_map/cond/branch_3_fun/ppermute | solution.py:31
  36.5 15.9 %collective-permute-start.12 = (bf16[4,768,256]{2,1,0:T(8,128)(2,1)}, bf16[4,768,256]{2,1,0:T(8,128)(2,1)}, u32[]{:S(2)}, u32[]{:S(2)}) collective-permute-start(bf16[4,768,256]{2,1,0:T(8,128)(2,1)} %get-tuple-element.657.near_ref), channel_id=1, source_target_pairs={{0,1},{1,0},{2,3},{3,2},{4,5},{5,4},{6,7},{7,6},{8,9},{9,8},{10,11... | collective-permute-start | bytes 4718600 | tf_op jit(solution)/shard_map/ppermute | solution.py:31
  38.4 28.0 %collective-permute-start.15 = (bf16[768,256]{1,0:T(8,128)(2,1)}, bf16[768,256]{1,0:T(8,128)(2,1)S(1)}, u32[]{:S(2)}, u32[]{:S(2)}) collective-permute-start(bf16[768,256]{1,0:T(8,128)(2,1)} %get-tuple-element.661), channel_id=1, source_target_pairs={{0,6},{2,0},{4,2},{6,4},{1,7},{3,1},{5,3},{7,5},{8,14},{10,8},{12,... | collective-permute-start | bytes 1179656 | tf_op jit(solution)/shard_map/ppermute | solution.py:336
  46.2 20.2 %collective-permute-start.14 = (bf16[768,256]{1,0:T(8,128)(2,1)}, bf16[768,256]{1,0:T(8,128)(2,1)}, u32[]{:S(2)}, u32[]{:S(2)}) collective-permute-start(bf16[768,256]{1,0:T(8,128)(2,1)} %get-tuple-element.661), channel_id=1, source_target_pairs={{0,4},{2,6},{4,0},{6,2},{1,5},{3,7},{5,1},{7,3},{8,12},{10,14},{12... | collective-permute-start | bytes 1179656 | tf_op jit(solution)/shard_map/ppermute | solution.py:336
  49.0 20.6 %collective-permute-start.13 = (bf16[768,256]{1,0:T(8,128)(2,1)}, bf16[768,256]{1,0:T(8,128)(2,1)}, u32[]{:S(2)}, u32[]{:S(2)}) collective-permute-start(bf16[768,256]{1,0:T(8,128)(2,1)} %get-tuple-element.661), channel_id=1, source_target_pairs={{0,2},{2,4},{4,6},{6,0},{1,3},{3,5},{5,7},{7,1},{8,10},{10,12},{12... | collective-permute-start | bytes 1179656 | tf_op jit(solution)/shard_map/ppermute | solution.py:336
  58.1 25.6 %all-to-all-start.12 = ((bf16[8,2,256,128]{3,2,1,0:T(8,128)(2,1)}), bf16[8,2,256,128]{3,2,1,0:T(8,128)(2,1)S(1)}, u32[]{:S(2)}, u32[]{:S(2)}) async-start(bf16[8,2,256,128]{3,2,1,0:T(8,128)(2,1)} %bitcast.75), calls=%async_computation.12 | async-start | bytes 2097152 | tf_op jit(solution)/shard_map/all_to_all | solution.py:314
  72.1 5.6 %collective-permute-start.16 = (bf16[4,768,256]{2,1,0:T(8,128)(2,1)}, bf16[4,768,256]{2,1,0:T(8,128)(2,1)}, u32[]{:S(2)}, u32[]{:S(2)}) collective-permute-start(bf16[4,768,256]{2,1,0:T(8,128)(2,1)} %pad_maximum_fusion.near_ref), channel_id=1, source_target_pairs={{0,1},{1,0},{2,3},{3,2},{4,5},{5,4},{6,7},{7,6},{8,9},{9,8},{10,11... | collective-permute-start | bytes 4718600 | tf_op jit(solution)/shard_map/ppermute | solution.py:31
  83.7 8.5 %copy-start.3 = (bf16[1,768,256]{2,1,0:T(8,128)(2,1)S(1)}, bf16[1,768,256]{2,1,0:T(8,128)(2,1)}, u32[]{:S(2)}) copy-start(bf16[1,768,256]{2,1,0:T(8,128)(2,1)} %param.24) | copy-start | bytes 1179652
  83.7 8.5 %copy-start.5 = (bf16[1,768,256]{2,1,0:T(8,128)(2,1)S(1)}, bf16[1,768,256]{2,1,0:T(8,128)(2,1)}, u32[]{:S(2)}) copy-start(bf16[1,768,256]{2,1,0:T(8,128)(2,1)} %param.25) | copy-start | bytes 1179652
  83.7 23.7 %all-to-all-start.13 = ((bf16[8,2,256,128]{3,2,1,0:T(8,128)(2,1)}), bf16[8,2,256,128]{3,2,1,0:T(8,128)(2,1)}, u32[]{:S(2)}, u32[]{:S(2)}) async-start(bf16[8,2,256,128]{3,2,1,0:T(8,128)(2,1)} %bitcast.76), calls=%async_computation.13 | async-start | bytes 2097152 | tf_op jit(solution)/shard_map/all_to_all | solution.py:314
  101.1 3.5 %collective-permute-start.17 = (bf16[400,256]{1,0:T(8,128)(2,1)}, bf16[400,256]{1,0:T(8,128)(2,1)S(1)}, u32[]{:S(2)}, u32[]{:S(2)}) collective-permute-start(bf16[400,256]{1,0:T(8,128)(2,1)} %get-tuple-element.672), channel_id=1, source_target_pairs={{0,1},{1,0},{2,3},{3,2},{4,5},{5,4},{6,7},{7,6},{8,9},{9,8},{10,11... | collective-permute-start | bytes 614408 | tf_op jit(solution)/shard_map/ppermute | solution.py:31
  107.4 8.6 %collective-permute-start.18 = (bf16[400,256]{1,0:T(8,128)(2,1)S(1)}, bf16[400,256]{1,0:T(8,128)(2,1)S(1)}, u32[]{:S(2)}, u32[]{:S(2)}) collective-permute-start(bf16[400,256]{1,0:T(8,128)(2,1)S(1)} %add_convert_fusion.1), channel_id=1, source_target_pairs={{0,2},{2,0},{4,6},{6,4},{1,3},{3,1},{5,7},{7,5},{8,10},{10,8},{12,... | collective-permute-start | bytes 614408 | tf_op jit(solution)/shard_map/ppermute | solution.py:353
  116.0 22.7 %collective-permute-start.19 = (bf16[400,256]{1,0:T(8,128)(2,1)S(1)}, bf16[400,256]{1,0:T(8,128)(2,1)S(1)}, u32[]{:S(2)}, u32[]{:S(2)}) collective-permute-start(bf16[400,256]{1,0:T(8,128)(2,1)S(1)} %add_convert_fusion), channel_id=1, source_target_pairs={{0,6},{6,0},{2,4},{4,2},{1,7},{7,1},{3,5},{5,3},{8,14},{14,8},{10,... | collective-permute-start | bytes 614408 | tf_op jit(solution)/shard_map/ppermute | solution.py:360
  118.6 38.7 %all-to-all-start.14 = ((bf16[4,256,128]{2,1,0:T(8,128)(2,1)}), bf16[4,256,128]{2,1,0:T(8,128)(2,1)S(1)}, u32[]{:S(2)}, u32[]{:S(2)}) async-start(bf16[4,256,128]{2,1,0:T(8,128)(2,1)} %shard_map.123), calls=%async_computation.14 | async-start | bytes 524288 | tf_op jit(solution)/shard_map/all_to_all | solution.py:356
  138.8 16.6 %collective-permute-start.21 = (f32[1,768]{1,0:T(1,128)S(1)}, f32[1,768]{1,0:T(1,128)S(1)}, u32[]{:S(2)}, u32[]{:S(2)}) collective-permute-start(f32[1,768]{1,0:T(1,128)S(1)} %bitcast.73), channel_id=1, source_target_pairs={{0,8},{8,0},{1,9},{9,1},{2,10},{10,2},{3,11},{11,3},{4,12},{12,4},... | collective-permute-start | bytes 9224 | tf_op jit(solution)/shard_map/ppermute | solution.py:31
  148.5 7.4 %collective-permute-start.20 = (bf16[384,512]{1,0:T(8,128)(2,1)S(1)}, bf16[384,512]{1,0:T(8,128)(2,1)S(1)}, u32[]{:S(2)}, u32[]{:S(2)}) collective-permute-start(bf16[384,512]{1,0:T(8,128)(2,1)S(1)} %pad_maximum_fusion.1), channel_id=1, source_target_pairs={{0,1},{1,0},{2,3},{3,2},{4,5},{5,4},{6,7},{7,6},{8,9},{9,8},{10,11... | collective-permute-start | bytes 1179656 | tf_op jit(solution)/shard_map/ppermute | solution.py:31

commit v7 on v6

--- a/solution.py
+++ b/solution.py
@@ -95,6 +95,8 @@
         vt_ref[...] = v_ref[...].astype(F32).T.astype(BF)
 
     weight = 1.0 / (1.0 + jnp.exp(-logit_ref[...]))
+    slot = lax.broadcasted_iota(jnp.int32, (1, ROWS), 1) + pl.program_id(0) * ROWS
+    weight = jnp.where(slot < info_ref[1], weight, 0.0)
     allowed = [allowed_block(key_ref, pos_ref, c) for c in CHUNKS]
     for h in range(HEADS):
         lanes = slice(h * HEAD_SIZE, (h + 1) * HEAD_SIZE)
@@ -129,7 +131,8 @@
 
     allowed = [allowed_block(key_ref, pos_ref, c) for c in CHUNKS]
     weight = 1.0 / (1.0 + jnp.exp(-column(logit_ref[...])))
-    grad_o = go_ref[...]
+    slot = lax.broadcasted_iota(jnp.int32, (ROWS, 1), 0) + step * ROWS
+    grad_o = jnp.where(slot < info_ref[1], go_ref[...], 0.0)
     grad_attn = (weight * grad_o).astype(BF)
     router = jnp.sum(grad_o * att_ref[...].astype(F32), axis=1, keepdims=True)
     router = jnp.broadcast_to(router, (ROWS, 128)).T[:1]
@@ -321,8 +324,7 @@
     own_count = jnp.sum(jnp.where(own, counts, 0))
     positions = routed[0]
     picked = cotangent[0].at[positions].get(mode="promise_in_bounds", wrap_negative_indices=False)
-    live = jnp.arange(SLOTS, dtype=jnp.int32) < own_count
-    picked = lax.optimization_barrier(jnp.where(live[:, None], picked, jnp.zeros((), BF)))
+    picked = lax.optimization_barrier(picked)
 
     attention = (
         query_rows[0], key_rows[0], routed_value_rows[0],

time: 161 us -> 155 us (0.963)
  the two profiles are of different devices: /device:TPU:64 before, /device:TPU:6 now
where the time goes in v7:
time: 155 us; the launch traced here: 153 us
  starting transfers between devices  90.4 us (58%)
  Pallas kernels  31.5 us (20%)
  waiting for transfers between devices  14.4 us (9%)
  other arithmetic  8.53 us (6%)
  local copies, waits for them, and re-layouts  6.71 us (4%)
  between operations  1.61 us (1%)
    ppermute x6, starting transfers between devices, swap(): return lax.ppermute(value, axis, ring(2, 1))  26.9 us
    all_to_all x2, starting transfers between devices, over_zp_y(): return lax.all_to_all(blocks, ('zp', 'y'), 0, 0, tiled=True)  25.7 us
    pallas_call x2, Pallas kernels, products(): pl.pallas_call(products_kernel, grid_spec=pltpu.PrefetchScalarGridSpec(nu...  11.7 us
    all_to_all x1, starting transfers between devices, per_device(): final = lax.all_to_all(blocks, 'zq', 0, 0, tiled=True)  11.2 us
    all_to_all x1, starting transfers between devices, spread_x(): return lax.all_to_all(copies, 'x', 0, 0, tiled=True)  10.2 us
    ppermute x3, starting transfers between devices, per_device(): lax.ppermute(other, 'x', ring(X, k))  9.81 us
    pallas_call x1, Pallas kernels, backward(): pl.pallas_call(backward_kernel, grid_spec=pltpu.PrefetchScalarGridSpec(nu...  8.91 us
    ppermute x6, waiting for transfers between devices, swap(): return lax.ppermute(value, axis, ring(2, 1))  7.24 us
  transfers between devices with their start and end apart: 15, of which 7 were waited for; matrix products, arithmetic and copies ran while one was open for 5% of the time, Pallas kernels for 21%

profile of v7, /device:TPU:6, one launch (start us, length us, event | category | flops | bytes accessed | tf_op | source)
XLA Modules:
  0.0 153.2 jit_solution(15102940796931358007)
XLA Ops:
  3.5 2.7 %gather_fusion = bf16[768,256]{1,0:T(8,128)(2,1)S(1)} fusion(bf16[3072,256]{1,0:T(8,128)(2,1)S(1)} %bitcast.72, s32[1024]{0:T(1024)S(1)} %pad_clamp_fusion), kind=kCustom, calls=%fused_computation | custom fusion | bytes 789504 | tf_op jit(solution)/shard_map/gather | solution.py:326
  6.2 31.6 %conditional.1 = (bf16[768,256]{1,0:T(8,128)(2,1)}, bf16[4,768,256]{2,1,0:T(8,128)(2,1)}, s32[3]{0:T(128)}, bf16[768,256]{1,0:T(8,128)(2,1)}, bf16[256,768]{1,0:...) conditional(s32[]{:T(128)} %clamp.3, ...), branch_computations={%region_1.2_spmd, %region_2.3_spmd, %region_3.4_spmd, %region_4.5_... | conditional | flops 4000999936 | bytes 12634019 | solution.py:335
  7.5 10.2 %all-to-all-start.5 = ((bf16[4,768,256]{2,1,0:T(8,128)(2,1)}), bf16[4,768,256]{2,1,0:T(8,128)(2,1)}, u32[]{:S(2)}, u32[]{:S(2)}) async-start(bf16[4,768,256]{2,1,0:T(8,128)(2,1)} %broadcast_in_dim.43), calls=%async_computation.5 | async-start | bytes 3145728 | tf_op jit(solution)/shard_map/cond/branch_5_fun/all_to_all | solution.py:35
  17.7 10.3 %collective-permute-start.5 = (bf16[384,256]{1,0:T(8,128)(2,1)S(1)}, bf16[384,256]{1,0:T(8,128)(2,1)S(1)}, u32[]{:S(2)}, u32[]{:S(2)}) collective-permute-start(bf16[384,256]{1,0:T(8,128)(2,1)S(1)} %slice.53), channel_id=1, source_target_pairs={{0,8},{8,0},{1,9},{9,1},{2,10},{10,2},{3,11},{11,3},{4,12},{12,4},... | collective-permute-start | bytes 589832 | tf_op jit(solution)/shard_map/cond/branch_5_fun/ppermute | solution.py:31
  29.3 6.7 %branch_5_fun.3 = (bf16[768,256]{1,0:T(8,128)(2,1)}, bf16[256,768]{1,0:T(8,128)(2,1)}, f32[2,768]{1,0:T(2,128)S(1)}) custom-call(s32[3]{0:T(128)} %pad_add_fusion.5.info_ref, bf16[768,256]{1,0:T(8,128)(2,1)S(1)} %get-tuple-element.527.q_ref, bf16[768,256]{1,0:T(8,128)(2,1)S(1)} %get-tuple-element.528.k_ref, bf16[768,256]{1,0:T(8,128)(2,1)} %get-tuple-element.529.v_ref, ...), custom_call_target="tpu_custom_call" | custom-call | flops 4000000000 | bytes 2000000 | tf_op jit(solution)/shard_map/cond/branch_5_fun/pallas_call | solution.py:197
  37.8 1.9 %collective-permute-start.12 = (bf16[4,768,256]{2,1,0:T(8,128)(2,1)}, bf16[4,768,256]{2,1,0:T(8,128)(2,1)}, u32[]{:S(2)}, u32[]{:S(2)}) collective-permute-start(bf16[4,768,256]{2,1,0:T(8,128)(2,1)} %get-tuple-element.657.near_ref), channel_id=1, source_target_pairs={{0,1},{1,0},{2,3},{3,2},{4,5},{5,4},{6,7},{7,6},{8,9},{9,8},{10,11... | collective-permute-start | bytes 4718600 | tf_op jit(solution)/shard_map/ppermute | solution.py:31
  39.7 2.8 %collective-permute-start.15 = (bf16[768,256]{1,0:T(8,128)(2,1)}, bf16[768,256]{1,0:T(8,128)(2,1)S(1)}, u32[]{:S(2)}, u32[]{:S(2)}) collective-permute-start(bf16[768,256]{1,0:T(8,128)(2,1)} %get-tuple-element.661), channel_id=1, source_target_pairs={{0,6},{2,0},{4,2},{6,4},{1,7},{3,1},{5,3},{7,5},{8,14},{10,8},{12,... | collective-permute-start | bytes 1179656 | tf_op jit(solution)/shard_map/ppermute | solution.py:338
  42.5 2.6 %collective-permute-start.14 = (bf16[768,256]{1,0:T(8,128)(2,1)}, bf16[768,256]{1,0:T(8,128)(2,1)}, u32[]{:S(2)}, u32[]{:S(2)}) collective-permute-start(bf16[768,256]{1,0:T(8,128)(2,1)} %get-tuple-element.661), channel_id=1, source_target_pairs={{0,4},{2,6},{4,0},{6,2},{1,5},{3,7},{5,1},{7,3},{8,12},{10,14},{12... | collective-permute-start | bytes 1179656 | tf_op jit(solution)/shard_map/ppermute | solution.py:338
  45.0 4.5 %collective-permute-start.13 = (bf16[768,256]{1,0:T(8,128)(2,1)}, bf16[768,256]{1,0:T(8,128)(2,1)}, u32[]{:S(2)}, u32[]{:S(2)}) collective-permute-start(bf16[768,256]{1,0:T(8,128)(2,1)} %get-tuple-element.661), channel_id=1, source_target_pairs={{0,2},{2,4},{4,6},{6,0},{1,3},{3,5},{5,7},{7,1},{8,10},{10,12},{12... | collective-permute-start | bytes 1179656 | tf_op jit(solution)/shard_map/ppermute | solution.py:338
  50.1 5.7 %shard_map.119 = (f32[768,256]{1,0:T(8,128)}, bf16[2,4,2,256,128]{4,3,2,1,0:T(8,128)(2,1)}) custom-call(s32[4]{0:T(128)} %pad_add_fusion.12.info_ref, bf16[4,768,256]{2,1,0:T(8,128)(2,1)} %get-tuple-element.657.near_ref, bf16[4,768,256]{2,1,0:T(8,128)(2,1)} %collective-permute-done.12.far_ref, bf16[16,256,256]{2,1,0:T(8,128)(2,1)} %bitcast.79, ...), custom_call_target="tpu_custom_call" | custom-call | flops 20000000000 | bytes 8000000 | tf_op jit(solution)/shard_map/pallas_call | solution.py:260
  55.9 16.9 %all-to-all-start.12 = ((bf16[8,2,256,128]{3,2,1,0:T(8,128)(2,1)}), bf16[8,2,256,128]{3,2,1,0:T(8,128)(2,1)S(1)}, u32[]{:S(2)}, u32[]{:S(2)}) async-start(bf16[8,2,256,128]{3,2,1,0:T(8,128)(2,1)} %bitcast.75), calls=%async_computation.12 | async-start | bytes 2097152 | tf_op jit(solution)/shard_map/all_to_all | solution.py:317
  72.8 2.5 %pad_maximum_fusion.near_ref = bf16[4,768,256]{2,1,0:T(8,128)(2,1)} fusion(bf16[1,768,256]{2,1,0:T(8,128)(2,1)S(1)} %bitcast.77, bf16[1,768,256]{2,1,0:T(8,128)(2,1)} %bitcast.59, bf16[1,768,256]{2,1,0:T(8,128)(2,1)} %bitcast.58, bf16[1,768,256]{2,1,0:T(8,128)(2,1)S(1)} %get-tuple-element.660), kind=kLoop, calls=%fused_computation.13 | loop fusion | flops 2359296 | bytes 3145728 | tf_op jit(solution)/shard_map/stack | solution.py:338
  77.8 3.1 %collective-permute-done.16.far_ref = bf16[4,768,256]{2,1,0:T(8,128)(2,1)} collective-permute-done((bf16[4,768,256]{2,1,0:T(8,128)(2,1)}, bf16[4,768,256]{2,1,0:T(8,128)(2,1)}, u32[]{:S(2)}, u32[]{:S(2)}) %collective-permute-start.16) | collective-permute-done | bytes 1572896 | tf_op jit(solution)/shard_map/ppermute | solution.py:31
  80.9 6.0 %shard_map.120 = (f32[768,256]{1,0:T(8,128)}, bf16[2,4,2,256,128]{4,3,2,1,0:T(8,128)(2,1)}) custom-call(s32[4]{0:T(128)} %pad_add_fusion.13.info_ref, bf16[4,768,256]{2,1,0:T(8,128)(2,1)} %pad_maximum_fusion.near_ref, bf16[4,768,256]{2,1,0:T(8,128)(2,1)} %collective-permute-done.16.far_ref, bf16[16,256,256]{2,1,0:T(8,128)(2,1)} %bitcast.80, ...), custom_call_target="tpu_custom_call" | custom-call | flops 20000000000 | bytes 8000000 | tf_op jit(solution)/shard_map/pallas_call | solution.py:260
  87.7 8.7 %all-to-all-start.13 = ((bf16[8,2,256,128]{3,2,1,0:T(8,128)(2,1)}), bf16[8,2,256,128]{3,2,1,0:T(8,128)(2,1)}, u32[]{:S(2)}, u32[]{:S(2)}) async-start(bf16[8,2,256,128]{3,2,1,0:T(8,128)(2,1)} %bitcast.76), calls=%async_computation.13 | async-start | bytes 2097152 | tf_op jit(solution)/shard_map/all_to_all | solution.py:317
  96.4 8.9 %shard_map.121 = (bf16[768,256]{1,0:T(8,128)(2,1)}, bf16[400,256]{1,0:T(8,128)(2,1)}, bf16[400,256]{1,0:T(8,128)(2,1)}) custom-call(s32[3]{0:T(128)} %get-tuple-element.654.info_ref, bf16[768,256]{1,0:T(8,128)(2,1)S(1)} %bitcast.93, bf16[768,256]{1,0:T(8,128)(2,1)S(1)} %bitcast.106, bf16[768,256]{1,0:T(8,128)(2,1)} %bitcast.119, s32[1,768]{1,0:T(1,128)S(1)} %copy-done.1, ...), custom_call_target="tpu_custom_call" | custom-call | flops 7000000000 | bytes 4000000 | tf_op jit(solution)/shard_map/pallas_call | solution.py:213
  111.6 2.1 %collective-permute-start.18 = (bf16[400,256]{1,0:T(8,128)(2,1)S(1)}, bf16[400,256]{1,0:T(8,128)(2,1)S(1)}, u32[]{:S(2)}, u32[]{:S(2)}) collective-permute-start(bf16[400,256]{1,0:T(8,128)(2,1)S(1)} %add_convert_fusion.1), channel_id=1, source_target_pairs={{0,2},{2,0},{4,6},{6,4},{1,3},{3,1},{5,7},{7,5},{8,10},{10,8},{12,... | collective-permute-start | bytes 614408 | tf_op jit(solution)/shard_map/ppermute | solution.py:355
  113.8 1.9 %shard_map.123 = bf16[4,256,128]{2,1,0:T(8,128)(2,1)} custom-call(s32[1]{0:T(128)} %bitcast.56.info_ref, bf16[8,2,256,128]{3,2,1,0:T(8,128)(2,1)} %all-to-all-done.13.moved_ref, bf16[4,256,128]{2,1,0:T(8,128)(2,1)} %shard_map.122.refs_0_), custom_call_target="tpu_custom_call", output_to_operand_aliasing={{}: (2, {})} | custom-call | flops 1000000 | bytes 2000000 | tf_op jit(solution)/shard_map/pallas_call | solution.py:285
  115.7 4.5 %collective-permute-done.18 = bf16[400,256]{1,0:T(8,128)(2,1)S(1)} collective-permute-done((bf16[400,256]{1,0:T(8,128)(2,1)S(1)}, bf16[400,256]{1,0:T(8,128)(2,1)S(1)}, u32[]{:S(2)}, u32[]{:S(2)}) %collective-permute-start.18) | collective-permute-done | bytes 204832 | tf_op jit(solution)/shard_map/ppermute | solution.py:355
  120.3 4.5 %collective-permute-start.19 = (bf16[400,256]{1,0:T(8,128)(2,1)S(1)}, bf16[400,256]{1,0:T(8,128)(2,1)S(1)}, u32[]{:S(2)}, u32[]{:S(2)}) collective-permute-start(bf16[400,256]{1,0:T(8,128)(2,1)S(1)} %add_convert_fusion), channel_id=1, source_target_pairs={{0,6},{6,0},{2,4},{4,2},{1,7},{7,1},{3,5},{5,3},{8,14},{14,8},{10,... | collective-permute-start | bytes 614408 | tf_op jit(solution)/shard_map/ppermute | solution.py:362
  124.8 11.2 %all-to-all-start.14 = ((bf16[4,256,128]{2,1,0:T(8,128)(2,1)}), bf16[4,256,128]{2,1,0:T(8,128)(2,1)S(1)}, u32[]{:S(2)}, u32[]{:S(2)}) async-start(bf16[4,256,128]{2,1,0:T(8,128)(2,1)} %shard_map.123), calls=%async_computation.14 | async-start | bytes 524288 | tf_op jit(solution)/shard_map/all_to_all | solution.py:358
  136.0 8.9 %collective-permute-start.21 = (f32[1,768]{1,0:T(1,128)S(1)}, f32[1,768]{1,0:T(1,128)S(1)}, u32[]{:S(2)}, u32[]{:S(2)}) collective-permute-start(f32[1,768]{1,0:T(1,128)S(1)} %bitcast.73), channel_id=1, source_target_pairs={{0,8},{8,0},{1,9},{9,1},{2,10},{10,2},{3,11},{11,3},{4,12},{12,4},... | collective-permute-start | bytes 9224 | tf_op jit(solution)/shard_map/ppermute | solution.py:31
  145.1 1.9 %collective-permute-start.20 = (bf16[384,512]{1,0:T(8,128)(2,1)S(1)}, bf16[384,512]{1,0:T(8,128)(2,1)S(1)}, u32[]{:S(2)}, u32[]{:S(2)}) collective-permute-start(bf16[384,512]{1,0:T(8,128)(2,1)S(1)} %pad_maximum_fusion.1), channel_id=1, source_target_pairs={{0,1},{1,0},{2,3},{3,2},{4,5},{5,4},{6,7},{7,6},{8,9},{9,8},{10,11... | collective-permute-start | bytes 1179656 | tf_op jit(solution)/shard_map/ppermute | solution.py:31
  147.1 3.4 %collective-permute-done.21.other_ref = f32[1,768]{1,0:T(1,128)S(1)} collective-permute-done((f32[1,768]{1,0:T(1,128)S(1)}, f32[1,768]{1,0:T(1,128)S(1)}, u32[]{:S(2)}, u32[]{:S(2)}) %collective-permute-start.21) | collective-permute-done | bytes 3104 | tf_op jit(solution)/shard_map/ppermute | solution.py:31
  (52 shorter events, 19.6 us)
Async XLA Ops:
  0.6 2.8 %copy-start = (bf16[1,3072,256]{2,1,0:T(8,128)(2,1)S(1)}, bf16[1,3072,256]{2,1,0:T(8,128)(2,1)}, u32[]{:S(2)}) copy-start(bf16[1,3072,256]{2,1,0:T(8,128)(2,1)} %param.20) | copy-start | bytes 4718596
  3.5 2.7 %copy-start.1 = (s32[1,768]{1,0:T(1,128)S(1)}, s32[1,768]{1,0:T(1,128)}, u32[]{:S(2)}) copy-start(s32[1,768]{1,0:T(1,128)} %row_ref.1) | copy-start | bytes 9220
  3.5 2.7 %copy-start.2 = (bf16[1,768,256]{2,1,0:T(8,128)(2,1)S(1)}, bf16[1,768,256]{2,1,0:T(8,128)(2,1)}, u32[]{:S(2)}) copy-start(bf16[1,768,256]{2,1,0:T(8,128)(2,1)} %param.24) | copy-start | bytes 1179652
  3.5 2.7 %copy-start.4 = (bf16[1,768,256]{2,1,0:T(8,128)(2,1)S(1)}, bf16[1,768,256]{2,1,0:T(8,128)(2,1)}, u32[]{:S(2)}) copy-start(bf16[1,768,256]{2,1,0:T(8,128)(2,1)} %param.25) | copy-start | bytes 1179652
  3.5 2.7 %copy-start.6 = (f32[1,768]{1,0:T(1,128)S(1)}, f32[1,768]{1,0:T(1,128)}, u32[]{:S(2)}) copy-start(f32[1,768]{1,0:T(1,128)} %logit_ref.3) | copy-start | bytes 9220
  7.5 30.3 %all-to-all-start.5 = ((bf16[4,768,256]{2,1,0:T(8,128)(2,1)}), bf16[4,768,256]{2,1,0:T(8,128)(2,1)}, u32[]{:S(2)}, u32[]{:S(2)}) async-start(bf16[4,768,256]{2,1,0:T(8,128)(2,1)} %broadcast_in_dim.43), calls=%async_computation.5 | async-start | bytes 3145728 | tf_op jit(solution)/shard_map/cond/branch_5_fun/all_to_all | solution.py:35
  17.7 18.3 %collective-permute-start.5 = (bf16[384,256]{1,0:T(8,128)(2,1)S(1)}, bf16[384,256]{1,0:T(8,128)(2,1)S(1)}, u32[]{:S(2)}, u32[]{:S(2)}) collective-permute-start(bf16[384,256]{1,0:T(8,128)(2,1)S(1)} %slice.53), channel_id=1, source_target_pairs={{0,8},{8,0},{1,9},{9,1},{2,10},{10,2},{3,11},{11,3},{4,12},{12,4},... | collective-permute-start | bytes 589832 | tf_op jit(solution)/shard_map/cond/branch_5_fun/ppermute | solution.py:31
  37.8 12.3 %collective-permute-start.12 = (bf16[4,768,256]{2,1,0:T(8,128)(2,1)}, bf16[4,768,256]{2,1,0:T(8,128)(2,1)}, u32[]{:S(2)}, u32[]{:S(2)}) collective-permute-start(bf16[4,768,256]{2,1,0:T(8,128)(2,1)} %get-tuple-element.657.near_ref), channel_id=1, source_target_pairs={{0,1},{1,0},{2,3},{3,2},{4,5},{5,4},{6,7},{7,6},{8,9},{9,8},{10,11... | collective-permute-start | bytes 4718600 | tf_op jit(solution)/shard_map/ppermute | solution.py:31
  39.7 33.1 %collective-permute-start.15 = (bf16[768,256]{1,0:T(8,128)(2,1)}, bf16[768,256]{1,0:T(8,128)(2,1)S(1)}, u32[]{:S(2)}, u32[]{:S(2)}) collective-permute-start(bf16[768,256]{1,0:T(8,128)(2,1)} %get-tuple-element.661), channel_id=1, source_target_pairs={{0,6},{2,0},{4,2},{6,4},{1,7},{3,1},{5,3},{7,5},{8,14},{10,8},{12,... | collective-permute-start | bytes 1179656 | tf_op jit(solution)/shard_map/ppermute | solution.py:338
  42.5 30.3 %collective-permute-start.14 = (bf16[768,256]{1,0:T(8,128)(2,1)}, bf16[768,256]{1,0:T(8,128)(2,1)}, u32[]{:S(2)}, u32[]{:S(2)}) collective-permute-start(bf16[768,256]{1,0:T(8,128)(2,1)} %get-tuple-element.661), channel_id=1, source_target_pairs={{0,4},{2,6},{4,0},{6,2},{1,5},{3,7},{5,1},{7,3},{8,12},{10,14},{12... | collective-permute-start | bytes 1179656 | tf_op jit(solution)/shard_map/ppermute | solution.py:338
  45.0 27.8 %collective-permute-start.13 = (bf16[768,256]{1,0:T(8,128)(2,1)}, bf16[768,256]{1,0:T(8,128)(2,1)}, u32[]{:S(2)}, u32[]{:S(2)}) collective-permute-start(bf16[768,256]{1,0:T(8,128)(2,1)} %get-tuple-element.661), channel_id=1, source_target_pairs={{0,2},{2,4},{4,6},{6,0},{1,3},{3,5},{5,7},{7,1},{8,10},{10,12},{12... | collective-permute-start | bytes 1179656 | tf_op jit(solution)/shard_map/ppermute | solution.py:338
  55.9 31.8 %all-to-all-start.12 = ((bf16[8,2,256,128]{3,2,1,0:T(8,128)(2,1)}), bf16[8,2,256,128]{3,2,1,0:T(8,128)(2,1)S(1)}, u32[]{:S(2)}, u32[]{:S(2)}) async-start(bf16[8,2,256,128]{3,2,1,0:T(8,128)(2,1)} %bitcast.75), calls=%async_computation.12 | async-start | bytes 2097152 | tf_op jit(solution)/shard_map/all_to_all | solution.py:317
  75.3 5.6 %collective-permute-start.16 = (bf16[4,768,256]{2,1,0:T(8,128)(2,1)}, bf16[4,768,256]{2,1,0:T(8,128)(2,1)}, u32[]{:S(2)}, u32[]{:S(2)}) collective-permute-start(bf16[4,768,256]{2,1,0:T(8,128)(2,1)} %pad_maximum_fusion.near_ref), channel_id=1, source_target_pairs={{0,1},{1,0},{2,3},{3,2},{4,5},{5,4},{6,7},{7,6},{8,9},{9,8},{10,11... | collective-permute-start | bytes 4718600 | tf_op jit(solution)/shard_map/ppermute | solution.py:31
  86.9 9.5 %copy-start.3 = (bf16[1,768,256]{2,1,0:T(8,128)(2,1)S(1)}, bf16[1,768,256]{2,1,0:T(8,128)(2,1)}, u32[]{:S(2)}) copy-start(bf16[1,768,256]{2,1,0:T(8,128)(2,1)} %param.24) | copy-start | bytes 1179652
  86.9 9.5 %copy-start.5 = (bf16[1,768,256]{2,1,0:T(8,128)(2,1)S(1)}, bf16[1,768,256]{2,1,0:T(8,128)(2,1)}, u32[]{:S(2)}) copy-start(bf16[1,768,256]{2,1,0:T(8,128)(2,1)} %param.25) | copy-start | bytes 1179652
  87.7 23.9 %all-to-all-start.13 = ((bf16[8,2,256,128]{3,2,1,0:T(8,128)(2,1)}), bf16[8,2,256,128]{3,2,1,0:T(8,128)(2,1)}, u32[]{:S(2)}, u32[]{:S(2)}) async-start(bf16[8,2,256,128]{3,2,1,0:T(8,128)(2,1)} %bitcast.76), calls=%async_computation.13 | async-start | bytes 2097152 | tf_op jit(solution)/shard_map/all_to_all | solution.py:317
  105.3 3.5 %collective-permute-start.17 = (bf16[400,256]{1,0:T(8,128)(2,1)}, bf16[400,256]{1,0:T(8,128)(2,1)S(1)}, u32[]{:S(2)}, u32[]{:S(2)}) collective-permute-start(bf16[400,256]{1,0:T(8,128)(2,1)} %get-tuple-element.672), channel_id=1, source_target_pairs={{0,1},{1,0},{2,3},{3,2},{4,5},{5,4},{6,7},{7,6},{8,9},{9,8},{10,11... | collective-permute-start | bytes 614408 | tf_op jit(solution)/shard_map/ppermute | solution.py:31
  111.6 8.6 %collective-permute-start.18 = (bf16[400,256]{1,0:T(8,128)(2,1)S(1)}, bf16[400,256]{1,0:T(8,128)(2,1)S(1)}, u32[]{:S(2)}, u32[]{:S(2)}) collective-permute-start(bf16[400,256]{1,0:T(8,128)(2,1)S(1)} %add_convert_fusion.1), channel_id=1, source_target_pairs={{0,2},{2,0},{4,6},{6,4},{1,3},{3,1},{5,7},{7,5},{8,10},{10,8},{12,... | collective-permute-start | bytes 614408 | tf_op jit(solution)/shard_map/ppermute | solution.py:355
  120.3 15.7 %collective-permute-start.19 = (bf16[400,256]{1,0:T(8,128)(2,1)S(1)}, bf16[400,256]{1,0:T(8,128)(2,1)S(1)}, u32[]{:S(2)}, u32[]{:S(2)}) collective-permute-start(bf16[400,256]{1,0:T(8,128)(2,1)S(1)} %add_convert_fusion), channel_id=1, source_target_pairs={{0,6},{6,0},{2,4},{4,2},{1,7},{7,1},{3,5},{5,3},{8,14},{14,8},{10,... | collective-permute-start | bytes 614408 | tf_op jit(solution)/shard_map/ppermute | solution.py:362
  124.8 27.6 %all-to-all-start.14 = ((bf16[4,256,128]{2,1,0:T(8,128)(2,1)}), bf16[4,256,128]{2,1,0:T(8,128)(2,1)S(1)}, u32[]{:S(2)}, u32[]{:S(2)}) async-start(bf16[4,256,128]{2,1,0:T(8,128)(2,1)} %shard_map.123), calls=%async_computation.14 | async-start | bytes 524288 | tf_op jit(solution)/shard_map/all_to_all | solution.py:358
  136.0 14.4 %collective-permute-start.21 = (f32[1,768]{1,0:T(1,128)S(1)}, f32[1,768]{1,0:T(1,128)S(1)}, u32[]{:S(2)}, u32[]{:S(2)}) collective-permute-start(f32[1,768]{1,0:T(1,128)S(1)} %bitcast.73), channel_id=1, source_target_pairs={{0,8},{8,0},{1,9},{9,1},{2,10},{10,2},{3,11},{11,3},{4,12},{12,4},... | collective-permute-start | bytes 9224 | tf_op jit(solution)/shard_map/ppermute | solution.py:31
  145.1 5.9 %collective-permute-start.20 = (bf16[384,512]{1,0:T(8,128)(2,1)S(1)}, bf16[384,512]{1,0:T(8,128)(2,1)S(1)}, u32[]{:S(2)}, u32[]{:S(2)}) collective-permute-start(bf16[384,512]{1,0:T(8,128)(2,1)S(1)} %pad_maximum_fusion.1), channel_id=1, source_target_pairs={{0,1},{1,0},{2,3},{3,2},{4,5},{5,4},{6,7},{7,6},{8,9},{9,8},{10,11... | collective-permute-start | bytes 1179656 | tf_op jit(solution)/shard_map/ppermute | solution.py:31
